TPU v7x, 32 devices: a whole 2x2x4 slice. The times are simulated.
32 devices in a mesh: dp: 8 (over z, y), tensor: 4 (over x, core).
Axes of the slice: x: 2, y: 2, z: 4, core: 2. Of those that a mesh axis runs over, the one named last changes fastest.
Arguments:
- tokens: bfloat16 [8192, 2048], P('dp'), may hold values from -6 to 6
- seg_ids: int32 [8192], P('dp'), may hold values from -1 to 1023, as said below
- cotangent: bfloat16 [8192, 2048], P('dp'), may hold values from -6 to 6
- attn_gain: float32 [2048], replicated, may hold values from 0.5 to 1.5
- w_query: bfloat16 [2048, 2048], P(None, 'tensor'), may hold values from -0.125 to 0.125
- w_key: bfloat16 [2048, 1024], P(None, 'tensor'), may hold values from -0.125 to 0.125
- w_value: bfloat16 [2048, 1024], P(None, 'tensor'), may hold values from -0.125 to 0.125
- w_out: bfloat16 [2048, 2048], P('tensor'), may hold values from -0.5 to 0.5
- mlp_gain: float32 [2048], replicated, may hold values from 0.5 to 1.5
- w_gate: bfloat16 [2048, 6144], P(None, 'tensor'), may hold values from -0.125 to 0.125
- w_up: bfloat16 [2048, 6144], P(None, 'tensor'), may hold values from -0.125 to 0.125
- w_down: bfloat16 [6144, 2048], P('tensor'), may hold values from -0.078125 to 0.078125
- query_gain: float32 [128], replicated, may hold values from 0.5 to 1.5
- key_gain: float32 [128], replicated, may hold values from 0.5 to 1.5
Outputs:
- mixed: bfloat16 [8192, 2048], P('dp')
- grad_tokens: bfloat16 [8192, 2048], P('dp')
- grad_attn_gain: float32 [2048], P('dp')
- grad_query: float32 [2048, 2048], P('dp', 'tensor')
- grad_key: float32 [2048, 1024], P('dp', 'tensor')
- grad_value: float32 [2048, 1024], P('dp', 'tensor')
- grad_out: float32 [2048, 2048], P('tensor', 'dp')
- grad_mlp_gain: float32 [2048], P('dp')
- grad_gate: float32 [2048, 6144], P('dp', 'tensor')
- grad_up: float32 [2048, 6144], P('dp', 'tensor')
- grad_down: float32 [6144, 2048], P('tensor', 'dp')
- grad_qgain: float32 [128], P('dp')
- grad_kgain: float32 [128], P('dp')
Inputs may be any that keep to these rules, and one draw needn't show every extreme that they name: `seg_ids`: in each aligned block of 1024 slots (the slots of one index of dp) the live slots come first and padding (-1) fills the rest; a live slot holds the index in its block of its sequence's first slot, so ids never fall within a block. One block per draw is a single sequence of 1024 slots; the next block (the first one, if it is the last) is full, its last slot a sequence of one slot; every other block ends in padding.
All inputs are finite; a program needn't handle non-finite values.
Results may differ from a plain program's by a relative error of at most 0.02.
Values may be sent and summed in bfloat16 or wider, within the bound.
No kernel may reach another device: no remote copies, remote signals or barrier semaphores. Data moves between devices by JAX's collectives and lax.ppermute only.
A program may use at most 256 MiB of HBM per device.

v0:
```python
import jax
import jax.numpy as jnp
from jax import lax
from jax.sharding import PartitionSpec as P

EPS = 1e-06
THETA = 1000000.0


def lowered(value):
    return lax.optimization_barrier(value.astype(jnp.bfloat16)).astype(jnp.float32)


def norm_fwd(value):
    factor = lax.rsqrt(jnp.mean(value * value, -1, keepdims=True) + EPS)
    return (value * factor, factor)


def norm_back(d_hat, v_hat, factor):
    return factor * (d_hat - v_hat * jnp.mean(d_hat * v_hat, -1, keepdims=True))


def rotate(value, cosine, sine):
    half = value.shape[-1] // 2
    turned = jnp.concatenate([-value[..., half:], value[..., :half]], -1)
    return value * cosine + turned * sine


def rotate_back(grad, cosine, sine):
    half = grad.shape[-1] // 2
    weighted = grad * sine
    turned = jnp.concatenate([-weighted[..., half:], weighted[..., :half]], -1)
    return grad * cosine - turned


def inner_dot(left, right):
    return lax.dot_general(
        left, right, (((0,), (0,)), ((), ())), preferred_element_type=jnp.float32
    )


def outer_dot(left, right):
    return lax.dot_general(
        left, right, (((1,), (1,)), ((), ())), preferred_element_type=jnp.float32
    )


def on_device(
    tokens,
    seg_ids,
    cotangent,
    attn_gain,
    w_query,
    w_key,
    w_value,
    w_out,
    mlp_gain,
    w_gate,
    w_up,
    w_down,
    query_gain,
    key_gain,
):
    count = tokens.shape[0]
    head_size = query_gain.shape[0]
    q_count = w_query.shape[1] // head_size
    kv_count = w_key.shape[1] // head_size
    group = q_count // kv_count
    scale = head_size ** (-0.5)
    x_full = tokens.astype(jnp.float32)
    x_hat, r_x = norm_fwd(x_full)
    normed = (x_hat * attn_gain).astype(jnp.bfloat16)
    q_lin = jnp.dot(normed, w_query, preferred_element_type=jnp.float32).reshape(
        count, q_count, head_size
    )
    k_lin = jnp.dot(normed, w_key, preferred_element_type=jnp.float32).reshape(
        count, kv_count, head_size
    )
    values = (
        jnp.dot(normed, w_value, preferred_element_type=jnp.float32)
        .astype(jnp.bfloat16)
        .reshape(count, kv_count, head_size)
    )
    q_hat, r_q = norm_fwd(q_lin)
    k_hat, r_k = norm_fwd(k_lin)
    index = jnp.arange(count, dtype=jnp.int32)
    place = jnp.where(seg_ids >= 0, index - seg_ids, index).astype(jnp.float32)
    freq = THETA ** (-(jnp.arange(head_size // 2, dtype=jnp.float32) * 2.0) / head_size)
    turn = place[:, None] * freq[None, :]
    turn = jnp.concatenate([turn, turn], -1)[:, None, :]
    cosine = jnp.cos(turn)
    sine = jnp.sin(turn)
    queries = (
        (rotate(q_hat * query_gain, cosine, sine) * scale)
        .astype(jnp.bfloat16)
        .reshape(count, kv_count, group, head_size)
    )
    keys = rotate(k_hat * key_gain, cosine, sine).astype(jnp.bfloat16)
    allowed = (seg_ids[:, None] == seg_ids[None, :]) & (index[None, :] <= index[:, None])

    def scores_of():
        raw = jnp.einsum("qgrd,kgd->grqk", queries, keys, preferred_element_type=jnp.float32)
        return jnp.where(allowed, raw, -1e30)

    scores = scores_of()
    top = jnp.max(scores, -1, keepdims=True)
    expo = jnp.exp(scores - top)
    total = jnp.sum(expo, -1, keepdims=True)
    lse = top + jnp.log(total)
    probs = (expo / total).astype(jnp.bfloat16)
    attended = jnp.einsum("grqk,kgd->qgrd", probs, values, preferred_element_type=jnp.float32)
    attended = attended.reshape(count, q_count * head_size).astype(jnp.bfloat16)
    resid = x_full + lax.psum(
        jnp.dot(attended, w_out, preferred_element_type=jnp.float32), "tensor"
    )
    resid_hat, r_resid = norm_fwd(resid)
    inner = (resid_hat * mlp_gain).astype(jnp.bfloat16)
    gate = jnp.dot(inner, w_gate, preferred_element_type=jnp.float32)
    up = jnp.dot(inner, w_up, preferred_element_type=jnp.float32)
    sig = jax.nn.sigmoid(gate)
    hidden = (gate * sig * up).astype(jnp.bfloat16)
    mixed = (
        resid
        + lax.psum(
            jnp.dot(hidden, w_down, preferred_element_type=jnp.float32).astype(jnp.bfloat16),
            "tensor",
        ).astype(jnp.float32)
    ).astype(jnp.bfloat16)
    live = (seg_ids >= 0).astype(jnp.float32)[:, None]
    grad_in = cotangent.astype(jnp.float32) * live
    grad_low = grad_in.astype(jnp.bfloat16)
    grad_down = inner_dot(hidden, grad_low)
    d_hidden = outer_dot(grad_low, w_down)
    d_gate = (d_hidden * up * (sig * (1.0 + gate * (1.0 - sig)))).astype(jnp.bfloat16)
    d_up = (d_hidden * gate * sig).astype(jnp.bfloat16)
    grad_gate = inner_dot(inner, d_gate)
    grad_up = inner_dot(inner, d_up)
    d_inner = lax.psum(outer_dot(d_gate, w_gate) + outer_dot(d_up, w_up), "tensor")
    grad_mlp_gain = jnp.sum(d_inner * resid_hat, 0)
    d_resid = grad_in + norm_back(d_inner * mlp_gain, resid_hat, r_resid)
    d_branch = d_resid.astype(jnp.bfloat16)
    grad_out = inner_dot(attended, d_branch)
    d_attended = (
        outer_dot(d_branch, w_out).astype(jnp.bfloat16).reshape(count, kv_count, group, head_size)
    )
    kept = jnp.exp(scores_of() - lse)
    kept_low = kept.astype(jnp.bfloat16)
    d_values = jnp.einsum(
        "grqk,qgrd->kgd", kept_low, d_attended, preferred_element_type=jnp.float32
    )
    d_values = d_values.astype(jnp.bfloat16).reshape(count, kv_count * head_size)
    d_probs = jnp.einsum("qgrd,kgd->grqk", d_attended, values, preferred_element_type=jnp.float32)
    d_scores = (kept * (d_probs - jnp.sum(kept * d_probs, -1, keepdims=True))).astype(jnp.bfloat16)
    d_queries = lowered(
        jnp.einsum("grqk,kgd->qgrd", d_scores, keys, preferred_element_type=jnp.float32).reshape(
            count, q_count, head_size
        )
    )
    d_keys = lowered(
        jnp.einsum("grqk,qgrd->kgd", d_scores, queries, preferred_element_type=jnp.float32)
    )
    q_grad = rotate_back(d_queries * scale, cosine, sine)
    k_grad = rotate_back(d_keys, cosine, sine)
    qgain_part = jnp.sum(q_grad * q_hat, (0, 1))
    kgain_part = jnp.sum(k_grad * k_hat, (0, 1))
    d_q_lin = (
        norm_back(q_grad * query_gain, q_hat, r_q)
        .reshape(count, q_count * head_size)
        .astype(jnp.bfloat16)
    )
    d_k_lin = (
        norm_back(k_grad * key_gain, k_hat, r_k)
        .reshape(count, kv_count * head_size)
        .astype(jnp.bfloat16)
    )
    grad_query = inner_dot(normed, d_q_lin)
    grad_key = inner_dot(normed, d_k_lin)
    grad_value = inner_dot(normed, d_values)
    normed_part = (
        outer_dot(d_q_lin, w_query) + outer_dot(d_k_lin, w_key) + outer_dot(d_values, w_value)
    )
    d_normed, grad_qgain, grad_kgain = (
        lax.psum(normed_part.astype(jnp.bfloat16), "tensor").astype(jnp.float32),
        lax.psum(qgain_part.astype(jnp.bfloat16), "tensor").astype(jnp.float32),
        lax.psum(kgain_part.astype(jnp.bfloat16), "tensor").astype(jnp.float32),
    )
    grad_attn_gain = jnp.sum(d_normed * x_hat, 0)
    grad_tokens = (d_resid + norm_back(d_normed * attn_gain, x_hat, r_x)).astype(jnp.bfloat16)
    (
        grad_query,
        grad_key,
        grad_value,
        grad_out,
        grad_attn_gain,
        grad_qgain,
        grad_kgain,
        grad_gate,
        grad_up,
        grad_down,
        grad_mlp_gain,
    ) = (
        lax.psum_scatter(
            grad_query.astype(jnp.bfloat16), "dp", scatter_dimension=0, tiled=True
        ).astype(jnp.float32),
        lax.psum_scatter(
            grad_key.astype(jnp.bfloat16), "dp", scatter_dimension=0, tiled=True
        ).astype(jnp.float32),
        lax.psum_scatter(
            grad_value.astype(jnp.bfloat16), "dp", scatter_dimension=0, tiled=True
        ).astype(jnp.float32),
        lax.psum_scatter(
            grad_out.astype(jnp.bfloat16), "dp", scatter_dimension=1, tiled=True
        ).astype(jnp.float32),
        lax.psum_scatter(
            grad_attn_gain.astype(jnp.bfloat16), "dp", scatter_dimension=0, tiled=True
        ).astype(jnp.float32),
        lax.psum_scatter(
            grad_qgain.astype(jnp.bfloat16), "dp", scatter_dimension=0, tiled=True
        ).astype(jnp.float32),
        lax.psum_scatter(
            grad_kgain.astype(jnp.bfloat16), "dp", scatter_dimension=0, tiled=True
        ).astype(jnp.float32),
        lax.psum_scatter(
            grad_gate.astype(jnp.bfloat16), "dp", scatter_dimension=0, tiled=True
        ).astype(jnp.float32),
        lax.psum_scatter(
            grad_up.astype(jnp.bfloat16), "dp", scatter_dimension=0, tiled=True
        ).astype(jnp.float32),
        lax.psum_scatter(
            grad_down.astype(jnp.bfloat16), "dp", scatter_dimension=1, tiled=True
        ).astype(jnp.float32),
        lax.psum_scatter(
            grad_mlp_gain.astype(jnp.bfloat16), "dp", scatter_dimension=0, tiled=True
        ).astype(jnp.float32),
    )
    return (
        mixed,
        grad_tokens,
        grad_attn_gain,
        grad_query,
        grad_key,
        grad_value,
        grad_out,
        grad_mlp_gain,
        grad_gate,
        grad_up,
        grad_down,
        grad_qgain,
        grad_kgain,
    )


def solution(mesh):
    return jax.shard_map(
        on_device,
        mesh=mesh,
        in_specs=(
            P("dp", None),
            P("dp"),
            P("dp", None),
            P(),
            P(None, "tensor"),
            P(None, "tensor"),
            P(None, "tensor"),
            P("tensor", None),
            P(),
            P(None, "tensor"),
            P(None, "tensor"),
            P("tensor", None),
            P(),
            P(),
        ),
        out_specs=(
            P("dp", None),
            P("dp", None),
            P("dp"),
            P("dp", "tensor"),
            P("dp", "tensor"),
            P("dp", "tensor"),
            P("tensor", "dp"),
            P("dp"),
            P("dp", "tensor"),
            P("dp", "tensor"),
            P("tensor", "dp"),
            P("dp"),
            P("dp"),
        ),
        check_vma=False,
    )
```

profile of v0, /device:TPU:0, one launch (start us, length us, event | category | flops | bytes accessed | tf_op | source)
XLA Modules:
  0.0 1303.1 jit_solution(4772996404018166752)
XLA Ops:
  30.9 8.6 fusion.4
  39.5 9.2 fusion.3
  64.5 155.1 %all-reduce.11.cloned.1.call-done = f32[1024,2048]{1,0:T(8,128)} async-done(((f32[1024,2048]{1,0:T(8,128)}), f32[1024,2048]{1,0:T(8,128)}) %all-reduce.11.cloned.1.call-update) | async-done | bytes 8388624 | tf_op jit(solution)/shard_map/psum | solution.py:113
  228.5 12.1 fusion.57
  240.6 10.4 fusion.56
  251.1 17.0 %multiply_convert_fusion.1 = (bf16[1024,1536]{1,0:T(8,128)(2,1)}, bf16[1024,1536]{1,0:T(8,128)(2,1)S(1)}, bf16[1024,1536]{1,0:T(8,128)(2,1)}) fusion(f32[1024,1536]{1,0:T(8,128)} %fusion.56, f32[1024,1536]{1,0:T(8,128)} %fusion.57, bf16[1536,2048]{1,0:T(8,128)(2,1)} %param.25, bf16[1024,2048]{1,0:T(8,128)(2,1)} %param.16, f32[1024]{0:T(1024)S(1)} %fusion.52), kind=kOutput, calls=%fused_computation.43 | convolution fusion | flops 6473908224 | bytes 32509952 | tf_op jit(solution)/shard_map/dot_general | solution.py:43
  268.0 10.0 fusion.58
  278.0 10.9 convolution_add_fusion
  289.0 11.4 convolution_convert_fusion.3
  300.5 141.7 %all-reduce.13.cloned.1.call-done = f32[1024,2048]{1,0:T(8,128)} async-done(((f32[1024,2048]{1,0:T(8,128)}), f32[1024,2048]{1,0:T(8,128)}) %all-reduce.13.cloned.1.call-update) | async-done | bytes 8388624 | tf_op jit(solution)/shard_map/psum | solution.py:138
  470.8 11.9 fusion
  482.7 12.3 fusion.2
  536.4 11.4 convolution_convert_fusion
  547.9 11.5 convolution_convert_fusion.1
  559.7 11.6 convolution_convert_fusion.2
  575.6 147.0 %all-reduce.15.cloned.1.call-done = (bf16[1024,2048]{1,0:T(8,128)(2,1)}, bf16[1024,2048]{1,0:T(8,128)(2,1)}) async-done(((bf16[1024,2048]{1,0:T(8,128)(2,1)}, bf16[1024,2048]{1,0:T(8,128)(2,1)}), (bf16[1024,2048]{1,0:T(8,128)(2,1)}, bf16[1024,2048]{1,0:T(8,128)(2,1)})) %all-reduce.15.cloned.1.call-update) | async-done | bytes 8388624 | tf_op jit(solution)/shard_map/psum | solution.py:124
  727.5 22.5 %all-reduce.4 = (bf16[2048]{0:T(1024)(128)(2,1)S(1)}, bf16[2048]{0:T(1024)(128)(2,1)S(1)}, bf16[128]{0:T(256)(128)(2,1)S(1)}, bf16[128]{0:T(256)(128)(2,1)S(1)}) all-reduce(bf16[2048]{0:T(1024)(128)(2,1)S(1)} %get-tuple-element.15, bf16[2048]{0:T(1024)(128)(2,1)S(1)} %get-tuple-element.13, ...), channel_id=2, replica_groups=mesh['dp'=8,'tensor'=4] {'dp'}, use_global_device_ids=true, to_apply=%region_16.17.clone | all-reduce | flops 4352 | bytes 17408
  750.2 40.2 %reduce-scatter.10.cloned.1.call-done = bf16[256,256]{1,0:T(8,128)(2,1)} async-done(((bf16[2048,256]{1,0:T(8,128)(2,1)}), bf16[256,256]{1,0:T(8,128)(2,1)}) %reduce-scatter.10.cloned.1.call-update) | async-done | bytes 131088 | tf_op jit(solution)/shard_map/reduce_scatter | solution.py:205
  798.7 62.1 %reduce-scatter.14.cloned.1.call-done = bf16[512,256]{1,0:T(8,128)(2,1)} async-done(((bf16[512,2048]{1,0:T(8,128)(2,1)}), bf16[512,256]{1,0:T(8,128)(2,1)}) %reduce-scatter.14.cloned.1.call-update) | async-done | bytes 262160 | tf_op jit(solution)/shard_map/reduce_scatter | solution.py:211
  862.7 68.4 %reduce-scatter.8.cloned.1.call-done = bf16[256,512]{1,0:T(8,128)(2,1)} async-done(((bf16[2048,512]{1,0:T(8,128)(2,1)}), bf16[256,512]{1,0:T(8,128)(2,1)}) %reduce-scatter.8.cloned.1.call-update) | async-done | bytes 262160 | tf_op jit(solution)/shard_map/reduce_scatter | solution.py:202
  933.5 16.0 %fusion.13 = (bf16[1024,2048]{1,0:T(8,128)(2,1)}, bf16[1024,2048]{1,0:T(8,128)(2,1)}) fusion(f32[1024,2048]{1,0:T(8,128)} %copy-done.6, bf16[1024,2048]{1,0:T(8,128)(2,1)} %get-tuple-element.28, bf16[1024,2048]{1,0:T(8,128)(2,1)} %param.14, f32[1024]{0:T(1024)S(1)} %broadcast_multiply_fusion.5, f32[2048]{0:T(1024)S(1)} %copy-done.44, ...), kind=kLoop, calls=%fused_computation.23 | loop fusion | flops 25165824 | bytes 37765120 | tf_op jit(solution)/shard_map/convert_element_type | solution.py:188
  949.6 102.5 %reduce-scatter.20.cloned.1.call-done = bf16[1536,256]{1,0:T(8,128)(2,1)} async-done(((bf16[1536,2048]{1,0:T(8,128)(2,1)}), bf16[1536,256]{1,0:T(8,128)(2,1)}) %reduce-scatter.20.cloned.1.call-update) | async-done | bytes 786448 | tf_op jit(solution)/shard_map/reduce_scatter | solution.py:229
  1054.5 118.3 %reduce-scatter.18.cloned.1.call-done = bf16[256,1536]{1,0:T(8,128)(2,1)} async-done(((bf16[2048,1536]{1,0:T(8,128)(2,1)}), bf16[256,1536]{1,0:T(8,128)(2,1)}) %reduce-scatter.18.cloned.1.call-update) | async-done | bytes 786448 | tf_op jit(solution)/shard_map/reduce_scatter | solution.py:226
  1175.3 118.1 %reduce-scatter.16.cloned.1.call-done = bf16[256,1536]{1,0:T(8,128)(2,1)} async-done(((bf16[2048,1536]{1,0:T(8,128)(2,1)}), bf16[256,1536]{1,0:T(8,128)(2,1)}) %reduce-scatter.16.cloned.1.call-update) | async-done | bytes 786448 | tf_op jit(solution)/shard_map/reduce_scatter | solution.py:223
  (202 shorter events, 146.1 us)
Async XLA Ops:
  7.2 16.0 %copy-start = (bf16[2048,512]{1,0:T(8,128)(2,1)S(1)}, bf16[2048,512]{1,0:T(8,128)(2,1)}, u32[]{:S(2)}) copy-start(bf16[2048,512]{1,0:T(8,128)(2,1)} %param.18) | copy-start | bytes 6291460
  7.2 9.1 copy-start.43
  7.2 212.3 %all-reduce.11.cloned.1.call-start = ((), (), s32[]{:S(2)}) async-start(), calls=%async_computation.7 | async-start | bytes 16777216 | tf_op jit(solution)/shard_map/psum | solution.py:113
  7.3 9.1 copy-start.2
  29.9 9.6 copy-start.17
  48.7 9.5 copy-start.52
  63.8 378.3 %all-reduce.13.cloned.1.call-start = ((), (), s32[]{:S(2)}) async-start(), calls=%async_computation.8 | async-start | bytes 16777216 | tf_op jit(solution)/shard_map/psum | solution.py:138
  64.5 160.8 %copy-start.42 = (f32[2048]{0:T(1024)S(1)}, f32[2048]{0:T(1024)}, u32[]{:S(2)}) copy-start(f32[2048]{0:T(1024)} %param.22) | copy-start | bytes 24580
  228.5 12.1 copy-start.21
  268.0 10.0 copy-start.55
  268.0 10.0 copy-start.56
  289.0 284.9 %reduce-scatter.12.cloned.1.call-start = ((), (), s32[]{:S(2)}) async-start(), calls=%async_computation.11 | async-start | bytes 1179648 | tf_op jit(solution)/shard_map/reduce_scatter | solution.py:208
  442.1 9.4 copy-start.20
  470.8 30.1 %copy-start.36 = (bf16[2,128,1024]{2,1,0:T(8,128)(2,1)}, bf16[2,128,1024]{2,1,0:T(8,128)(2,1)S(1)}, u32[]{:S(2)}) copy-start(bf16[2,128,1024]{2,1,0:T(8,128)(2,1)S(1)} %fusion.42) | copy-start | bytes 1572868
  482.7 12.3 copy-start.14
  503.3 219.3 %all-reduce.15.cloned.1.call-start = ((), (), s32[]{:S(2)}) async-start(), calls=%async_computation.16 | async-start | bytes 16777216 | tf_op jit(solution)/shard_map/psum | solution.py:124
  516.8 273.7 %reduce-scatter.10.cloned.1.call-start = ((), (), s32[]{:S(2)}) async-start(), calls=%async_computation.10 | async-start | bytes 1179648 | tf_op jit(solution)/shard_map/reduce_scatter | solution.py:205
  522.4 338.5 %reduce-scatter.14.cloned.1.call-start = ((), (), s32[]{:S(2)}) async-start(), calls=%async_computation.12 | async-start | bytes 2359296 | tf_op jit(solution)/shard_map/reduce_scatter | solution.py:211
  530.0 401.0 %reduce-scatter.8.cloned.1.call-start = ((), (), s32[]{:S(2)}) async-start(), calls=%async_computation.9 | async-start | bytes 2359296 | tf_op jit(solution)/shard_map/reduce_scatter | solution.py:202
  536.3 515.8 %reduce-scatter.20.cloned.1.call-start = ((), (), s32[]{:S(2)}) async-start(), calls=%async_computation.15 | async-start | bytes 7077888 | tf_op jit(solution)/shard_map/reduce_scatter | solution.py:229
  547.8 625.0 %reduce-scatter.18.cloned.1.call-start = ((), (), s32[]{:S(2)}) async-start(), calls=%async_computation.14 | async-start | bytes 7077888 | tf_op jit(solution)/shard_map/reduce_scatter | solution.py:226
  559.4 733.9 %reduce-scatter.16.cloned.1.call-start = ((), (), s32[]{:S(2)}) async-start(), calls=%async_computation.13 | async-start | bytes 7077888 | tf_op jit(solution)/shard_map/reduce_scatter | solution.py:223
  571.3 151.2 %copy-start.44 = (f32[2048]{0:T(1024)S(1)}, f32[2048]{0:T(1024)}, u32[]{:S(2)}) copy-start(f32[2048]{0:T(1024)} %param.17) | copy-start | bytes 24580
  571.3 151.2 %copy-start.46 = (f32[1024]{0:T(1024)S(1)}, f32[1024]{0:T(1024)}, u32[]{:S(2)}) copy-start(f32[1024]{0:T(1024)} %copy-done.45) | copy-start | bytes 12292
  (43 other events, 145.8 us)
Sparse Core Ops, SparseCore 0:
  63.9 155.5 all-reduce.10
  289.1 153.0 all-reduce.12
  503.4 63.6 reduce-scatter.11
  570.3 152.2 all-reduce.14
  726.8 63.6 reduce-scatter.9
  793.8 66.9 reduce-scatter.13
  864.4 66.6 reduce-scatter.7
  934.7 117.3 reduce-scatter.19
  1055.7 117.0 reduce-scatter.17
  1176.2 117.0 reduce-scatter.15
where the time goes:
time: 1310 us; the launch traced here: 1300 us
  waiting for transfers between devices  954 us (73%)
  matrix products  195 us (15%)
  other arithmetic  98.2 us (7%)
  blocking collectives  28.2 us (2%)
  between operations  16.8 us (1%)
    psum x1, waiting for transfers between devices, on_device(): lax.psum(jnp.dot(attended, w_out, preferred_element_type=jnp.float32), 't...  155 us
    psum x1, waiting for transfers between devices, on_device(): lax.psum(jnp.dot(hidden, w_down, preferred_element_type=jnp.float32).asty...  147 us
    psum x1, waiting for transfers between devices, on_device(): lax.psum(outer_dot(d_gate, w_gate) + outer_dot(d_up, w_up), 'tensor')  142 us
    reduce_scatter x1, waiting for transfers between devices, on_device(): lax.psum_scatter(grad_up.astype(jnp.bfloat16), 'dp', scatter_dimension=0,...  118 us
    reduce_scatter x1, waiting for transfers between devices, on_device(): lax.psum_scatter(grad_gate.astype(jnp.bfloat16), 'dp', scatter_dimension=...  118 us
    reduce_scatter x1, waiting for transfers between devices, on_device(): lax.psum_scatter(grad_down.astype(jnp.bfloat16), 'dp', scatter_dimension=...  103 us
    reduce_scatter x1, waiting for transfers between devices, on_device(): lax.psum_scatter(grad_query.astype(jnp.bfloat16), 'dp', scatter_dimension...  68.4 us
    reduce_scatter x1, waiting for transfers between devices, on_device(): lax.psum_scatter(grad_out.astype(jnp.bfloat16), 'dp', scatter_dimension=1...  62.1 us
  transfers between devices with their start and end apart: 10, of which 9 were waited for; matrix products, arithmetic and copies ran while one was open for 9% of the time, Pallas kernels for 0%

commit v1 on v0

--- a/solution.py
+++ b/solution.py
@@ -1,10 +1,15 @@
+import functools
+
 import jax
 import jax.numpy as jnp
+import numpy as np
 from jax import lax
 from jax.sharding import PartitionSpec as P
 
 EPS = 1e-06
 THETA = 1000000.0
+CORE_SWAP = ((0, 1), (1, 0), (2, 3), (3, 2))
+CHIP_SWAP = ((0, 2), (1, 3), (2, 0), (3, 1))
 
 
 def lowered(value):
@@ -45,7 +50,62 @@
     )
 
 
+def to_core(value):
+    return lax.ppermute(value, "tensor", CORE_SWAP)
+
+
+def to_chip(value):
+    return lax.ppermute(value, "tensor", CHIP_SWAP)
+
+
+def ring_of(n):
+    order = list(range(0, n, 2)) + [i for i in range(n - 1, 0, -1) if i % 2]
+    place = [0] * n
+    for spot, index in enumerate(order):
+        place[index] = spot
+    ahead = tuple((order[i], order[(i + 1) % n]) for i in range(n))
+    back = tuple((b, a) for a, b in ahead)
+    return order, place, ahead, back
+
+
+def ring_scatter(n, part, dim):
+    order, place, ahead, back = ring_of(n)
+    spot = jnp.asarray(np.array(place, np.int32))[lax.axis_index("dp")]
+    order = jnp.asarray(np.array(order, np.int32))
+    size = part.shape[dim] // n
+    other = 1 - dim
+    wide = part.shape[other] // 2
+
+    def piece(where, side):
+        begin = [0, 0]
+        extent = [0, 0]
+        begin[dim] = order[where % n] * size
+        extent[dim] = size
+        begin[other] = side * wide
+        extent[other] = wide
+        return lax.dynamic_slice(part, begin, extent)
+
+    held = [piece(spot - 1 + n, 0), piece(spot + 1, 1)]
+    for step in range(n - 1):
+        for side, pairs in ((0, ahead), (1, back)):
+            came = lax.ppermute(held[side], "dp", pairs)
+            where = spot + 2 * n - 2 - step if side == 0 else spot + 2 + step
+            held[side] = came.astype(jnp.float32) + piece(where, side).astype(jnp.float32)
+            if step < n - 2:
+                held[side] = held[side].astype(jnp.bfloat16)
+    return jnp.concatenate(held, other)
+
+
+def all_sum_dp(n, value):
+    step = 1
+    while step < n:
+        value = value + lax.ppermute(value, "dp", tuple((i, i ^ step) for i in range(n)))
+        step *= 2
+    return value
+
+
 def on_device(
+    n,
     tokens,
     seg_ids,
     cotangent,
@@ -62,11 +122,32 @@
     key_gain,
 ):
     count = tokens.shape[0]
+    half = count // 2
     head_size = query_gain.shape[0]
     q_count = w_query.shape[1] // head_size
     kv_count = w_key.shape[1] // head_size
     group = q_count // kv_count
     scale = head_size ** (-0.5)
+    core = lax.axis_index("tensor") % 2
+    scatter = functools.partial(ring_scatter, n)
+
+    def mine(value):
+        return lax.dynamic_slice_in_dim(value, core * half, half, 0)
+
+    def other(value):
+        return lax.dynamic_slice_in_dim(value, (1 - core) * half, half, 0)
+
+    def ordered(first, second):
+        return jnp.where(
+            core == 0, jnp.concatenate([first, second], 0), jnp.concatenate([second, first], 0)
+        )
+
+    def summed(part_mine, part_other):
+        near = part_mine + to_core(part_other.astype(jnp.bfloat16)).astype(jnp.float32)
+        near = near.astype(jnp.bfloat16)
+        far = to_chip(near)
+        return near.astype(jnp.float32) + far.astype(jnp.float32)
+
     x_full = tokens.astype(jnp.float32)
     x_hat, r_x = norm_fwd(x_full)
     normed = (x_hat * attn_gain).astype(jnp.bfloat16)
@@ -110,38 +191,43 @@
     probs = (expo / total).astype(jnp.bfloat16)
     attended = jnp.einsum("grqk,kgd->qgrd", probs, values, preferred_element_type=jnp.float32)
     attended = attended.reshape(count, q_count * head_size).astype(jnp.bfloat16)
-    resid = x_full + lax.psum(
-        jnp.dot(attended, w_out, preferred_element_type=jnp.float32), "tensor"
+    attended_mine, attended_other = mine(attended), other(attended)
+    x_mine = mine(tokens).astype(jnp.float32)
+    resid = x_mine + summed(
+        jnp.dot(attended_mine, w_out, preferred_element_type=jnp.float32),
+        jnp.dot(attended_other, w_out, preferred_element_type=jnp.float32),
     )
     resid_hat, r_resid = norm_fwd(resid)
-    inner = (resid_hat * mlp_gain).astype(jnp.bfloat16)
+    inner_mine = (resid_hat * mlp_gain).astype(jnp.bfloat16)
+    inner = jnp.concatenate([inner_mine, to_core(inner_mine)], 0)
     gate = jnp.dot(inner, w_gate, preferred_element_type=jnp.float32)
     up = jnp.dot(inner, w_up, preferred_element_type=jnp.float32)
     sig = jax.nn.sigmoid(gate)
     hidden = (gate * sig * up).astype(jnp.bfloat16)
-    mixed = (
-        resid
-        + lax.psum(
-            jnp.dot(hidden, w_down, preferred_element_type=jnp.float32).astype(jnp.bfloat16),
-            "tensor",
-        ).astype(jnp.float32)
-    ).astype(jnp.bfloat16)
-    live = (seg_ids >= 0).astype(jnp.float32)[:, None]
-    grad_in = cotangent.astype(jnp.float32) * live
-    grad_low = grad_in.astype(jnp.bfloat16)
-    grad_down = inner_dot(hidden, grad_low)
+    live = seg_ids >= 0
+    grad_mine = jnp.where(mine(live)[:, None], mine(cotangent), 0)
+    grad_other = jnp.where(other(live)[:, None], other(cotangent), 0)
+    grad_low = jnp.concatenate([grad_mine, grad_other], 0)
+    grad_down = scatter(inner_dot(hidden, grad_low).astype(jnp.bfloat16), 1)
+    mixed_part = jnp.dot(hidden, w_down, preferred_element_type=jnp.float32)
+    mixed = (resid + summed(mixed_part[:half], mixed_part[half:])).astype(jnp.bfloat16)
+    mixed = ordered(mixed, to_core(mixed))
     d_hidden = outer_dot(grad_low, w_down)
     d_gate = (d_hidden * up * (sig * (1.0 + gate * (1.0 - sig)))).astype(jnp.bfloat16)
     d_up = (d_hidden * gate * sig).astype(jnp.bfloat16)
-    grad_gate = inner_dot(inner, d_gate)
-    grad_up = inner_dot(inner, d_up)
-    d_inner = lax.psum(outer_dot(d_gate, w_gate) + outer_dot(d_up, w_up), "tensor")
+    grad_gate = scatter(inner_dot(inner, d_gate).astype(jnp.bfloat16), 0)
+    grad_up = scatter(inner_dot(inner, d_up).astype(jnp.bfloat16), 0)
+    d_inner = outer_dot(d_gate, w_gate) + outer_dot(d_up, w_up)
+    d_inner = summed(d_inner[:half], d_inner[half:])
     grad_mlp_gain = jnp.sum(d_inner * resid_hat, 0)
-    d_resid = grad_in + norm_back(d_inner * mlp_gain, resid_hat, r_resid)
-    d_branch = d_resid.astype(jnp.bfloat16)
-    grad_out = inner_dot(attended, d_branch)
-    d_attended = (
-        outer_dot(d_branch, w_out).astype(jnp.bfloat16).reshape(count, kv_count, group, head_size)
+    d_resid = grad_mine.astype(jnp.float32) + norm_back(d_inner * mlp_gain, resid_hat, r_resid)
+    d_branch_mine = d_resid.astype(jnp.bfloat16)
+    d_branch = jnp.concatenate([d_branch_mine, to_core(d_branch_mine)], 0)
+    attended_mo = jnp.concatenate([attended_mine, attended_other], 0)
+    grad_out = scatter(inner_dot(attended_mo, d_branch).astype(jnp.bfloat16), 1)
+    d_attended = outer_dot(d_branch, w_out).astype(jnp.bfloat16)
+    d_attended = ordered(d_attended[:half], d_attended[half:]).reshape(
+        count, kv_count, group, head_size
     )
     kept = jnp.exp(scores_of() - lse)
     kept_low = kept.astype(jnp.bfloat16)
@@ -173,86 +259,50 @@
         .reshape(count, kv_count * head_size)
         .astype(jnp.bfloat16)
     )
-    grad_query = inner_dot(normed, d_q_lin)
-    grad_key = inner_dot(normed, d_k_lin)
-    grad_value = inner_dot(normed, d_values)
-    normed_part = (
-        outer_dot(d_q_lin, w_query) + outer_dot(d_k_lin, w_key) + outer_dot(d_values, w_value)
-    )
-    d_normed, grad_qgain, grad_kgain = (
-        lax.psum(normed_part.astype(jnp.bfloat16), "tensor").astype(jnp.float32),
-        lax.psum(qgain_part.astype(jnp.bfloat16), "tensor").astype(jnp.float32),
-        lax.psum(kgain_part.astype(jnp.bfloat16), "tensor").astype(jnp.float32),
-    )
-    grad_attn_gain = jnp.sum(d_normed * x_hat, 0)
-    grad_tokens = (d_resid + norm_back(d_normed * attn_gain, x_hat, r_x)).astype(jnp.bfloat16)
-    (
+    d_lin = jnp.concatenate([d_q_lin, d_k_lin, d_values], 1)
+    w_lin = jnp.concatenate([w_query, w_key, w_value], 1)
+    grad_lin = scatter(inner_dot(normed, d_lin).astype(jnp.bfloat16), 0)
+    q_cols, k_cols = q_count * head_size, kv_count * head_size
+    grad_query = grad_lin[:, :q_cols]
+    grad_key = grad_lin[:, q_cols : q_cols + k_cols]
+    grad_value = grad_lin[:, q_cols + k_cols :]
+    d_normed = summed(outer_dot(mine(d_lin), w_lin), outer_dot(other(d_lin), w_lin))
+    x_hat_mine, r_x_mine = norm_fwd(x_mine)
+    grad_attn_gain = jnp.sum(d_normed * x_hat_mine, 0)
+    grad_tokens = (d_resid + norm_back(d_normed * attn_gain, x_hat_mine, r_x_mine)).astype(
+        jnp.bfloat16
+    )
+    grad_tokens = ordered(grad_tokens, to_core(grad_tokens))
+    heads = jnp.concatenate([qgain_part, kgain_part])
+    heads = heads + to_chip(heads)
+    gains = jnp.concatenate([grad_mlp_gain, grad_attn_gain, heads])
+    gains = all_sum_dp(n, gains + to_core(gains))
+    width = mlp_gain.shape[0]
+    my_dp = lax.axis_index("dp")
+
+    def own(begin, size):
+        return lax.dynamic_slice(gains, (begin + my_dp * (size // n),), (size // n,))
+
+    return (
+        mixed,
+        grad_tokens,
+        own(width, width),
         grad_query,
         grad_key,
         grad_value,
         grad_out,
-        grad_attn_gain,
-        grad_qgain,
-        grad_kgain,
+        own(0, width),
         grad_gate,
         grad_up,
         grad_down,
-        grad_mlp_gain,
-    ) = (
-        lax.psum_scatter(
-            grad_query.astype(jnp.bfloat16), "dp", scatter_dimension=0, tiled=True
-        ).astype(jnp.float32),
-        lax.psum_scatter(
-            grad_key.astype(jnp.bfloat16), "dp", scatter_dimension=0, tiled=True
-        ).astype(jnp.float32),
-        lax.psum_scatter(
-            grad_value.astype(jnp.bfloat16), "dp", scatter_dimension=0, tiled=True
-        ).astype(jnp.float32),
-        lax.psum_scatter(
-            grad_out.astype(jnp.bfloat16), "dp", scatter_dimension=1, tiled=True
-        ).astype(jnp.float32),
-        lax.psum_scatter(
-            grad_attn_gain.astype(jnp.bfloat16), "dp", scatter_dimension=0, tiled=True
-        ).astype(jnp.float32),
-        lax.psum_scatter(
-            grad_qgain.astype(jnp.bfloat16), "dp", scatter_dimension=0, tiled=True
-        ).astype(jnp.float32),
-        lax.psum_scatter(
-            grad_kgain.astype(jnp.bfloat16), "dp", scatter_dimension=0, tiled=True
-        ).astype(jnp.float32),
-        lax.psum_scatter(
-            grad_gate.astype(jnp.bfloat16), "dp", scatter_dimension=0, tiled=True
-        ).astype(jnp.float32),
-        lax.psum_scatter(
-            grad_up.astype(jnp.bfloat16), "dp", scatter_dimension=0, tiled=True
-        ).astype(jnp.float32),
-        lax.psum_scatter(
-            grad_down.astype(jnp.bfloat16), "dp", scatter_dimension=1, tiled=True
-        ).astype(jnp.float32),
-        lax.psum_scatter(
-            grad_mlp_gain.astype(jnp.bfloat16), "dp", scatter_dimension=0, tiled=True
-        ).astype(jnp.float32),
-    )
-    return (
-        mixed,
-        grad_tokens,
-        grad_attn_gain,
-        grad_query,
-        grad_key,
-        grad_value,
-        grad_out,
-        grad_mlp_gain,
-        grad_gate,
-        grad_up,
-        grad_down,
-        grad_qgain,
-        grad_kgain,
+        own(2 * width, head_size),
+        own(2 * width + head_size, head_size),
     )
 
 
 def solution(mesh):
     return jax.shard_map(
-        on_device,
+        functools.partial(on_device, mesh.shape["dp"]),
         mesh=mesh,
         in_specs=(
             P("dp", None),

time: 1310 us -> 628 us (0.48)
  waiting for transfers between devices: 954 us -> 203 us
  starting transfers between devices: 0.88 us -> 86.4 us
  blocking collectives: 28.2 us -> 0 us
  matrix products: 195 us -> 176 us
  local copies, waits for them, and re-layouts: 10.3 us -> 28.1 us
    reduce_scatter x7 -> x0, waiting for transfers between devices: 510 us -> none  [the longest x1 118 us: on_device(): lax.psum_scatter(grad_up.astype(jnp.bfloat16), 'dp', scatter_dimension=0,...]
    psum x3 -> x0, waiting for transfers between devices: 444 us -> none  [the longest x1 155 us: on_device(): lax.psum(jnp.dot(attended, w_out, preferred_element_type=jnp.float32), 't...]
    ppermute x0 -> x87, waiting for transfers between devices: none -> 203 us  [the longest x70 102 us: ring_scatter(): came = lax.ppermute(held[side], 'dp', pairs)]
    ppermute x0 -> x87, starting transfers between devices: none -> 86.4 us  [the longest x70 76.6 us: ring_scatter(): came = lax.ppermute(held[side], 'dp', pairs)]
    unnamed x1 -> x0, blocking collectives: 22.5 us -> none
    dot_general x7 -> x5, matrix products: 55 us -> 38.2 us  [inner_dot(): lax.dot_general(left, right, (((0,), (0,)), ((), ())), preferred_element_...]
    convert_element_type x14 -> x35, other arithmetic: 33.7 us -> 41.4 us  [the longest x30 24.9 us: ring_scatter(): held[side] = held[side].astype(jnp.bfloat16)]
    dot_general x7 -> x6, matrix products: 50.5 us -> 43.5 us  [outer_dot(): lax.dot_general(left, right, (((1,), (1,)), ((), ())), preferred_element_...]
  transfers between devices with their start and end apart: 10 -> 87, of which waited for: 9 -> 43; matrix products, arithmetic and copies ran while one was open for 9% -> 24% of each run, Pallas kernels for 0% -> 0%
where the time goes in v1:
time: 628 us; the launch traced here: 622 us
  waiting for transfers between devices  203 us (32%)
  matrix products  176 us (28%)
  other arithmetic  108 us (17%)
  starting transfers between devices  86.4 us (14%)
  local copies, waits for them, and re-layouts  28.1 us (4%)
  between operations  21 us (3%)
    ppermute x70, waiting for transfers between devices, ring_scatter(): came = lax.ppermute(held[side], 'dp', pairs)  102 us
    ppermute x5, waiting for transfers between devices, to_chip(): return lax.ppermute(value, 'tensor', CHIP_SWAP)  88.9 us
    ppermute x70, starting transfers between devices, ring_scatter(): came = lax.ppermute(held[side], 'dp', pairs)  76.6 us
    dot_general x6, matrix products, outer_dot(): lax.dot_general(left, right, (((1,), (1,)), ((), ())), preferred_element_...  43.5 us
    dot_general x5, matrix products, inner_dot(): lax.dot_general(left, right, (((0,), (0,)), ((), ())), preferred_element_...  38.2 us
    convert_element_type x30, other arithmetic, ring_scatter(): held[side] = held[side].astype(jnp.bfloat16)  24.9 us
    unnamed x164, local copies, waits for them, and re-layouts  17.5 us
    dot_general x1, matrix products, on_device(): gate = jnp.dot(inner, w_gate, preferred_element_type=jnp.float32)  16.5 us
  transfers between devices with their start and end apart: 87, of which 43 were waited for; matrix products, arithmetic and copies ran while one was open for 24% of the time, Pallas kernels for 0%

profile of v1, /device:TPU:0, one launch (start us, length us, event | category | flops | bytes accessed | tf_op | source)
XLA Modules:
  0.0 622.3 jit_solution(2251868573248485770)
XLA Ops:
  6.7 5.5 multiply_reduce_fusion.5
  25.5 8.6 %fusion.4 = (f32[2,2,1024]{2,1,0:T(2,128)S(1)}, f32[2,1024,1024,2]{2,1,3,0:T(8,128)}) fusion(pred[1024,1024]{0,1:T(8,128)(4,1)S(1)} %fusion.25, bf16[1024,2,128,1]{0,2,3,1:T(8,128)(2,1)S(1)} %fusion.55, bf16[1024,2,2,128]{0,3,2,1:T(8,128)(2,1)S(1)} %fusion.33), kind=kOutput, calls=%fused_computation.10 | convolution fusion | flops 1082126336 | bytes 19415040 | tf_op jit(solution)/shard_map/qgrd,kgd->grqk/dot_general | solution.py:183
  34.1 8.8 %fusion.3 = f32[2,2,1024]{2,1,0:T(2,128)S(1)} fusion(f32[2,1024,1024,2]{2,1,3,0:T(8,128)} %get-tuple-element.167, f32[2,2,1024]{2,1,0:T(2,128)S(1)} %get-tuple-element.166, pred[1024,1024]{0,1:T(8,128)(4,1)S(1)} %fusion.25), kind=kLoop, calls=%fused_computation.9 | loop fusion | flops 12578816 | bytes 17858560 | tf_op jit(solution)/shard_map/reduce_sum | solution.py:189
  42.9 9.3 %fusion.34 = bf16[2,128,2,1024]{3,1,2,0:T(8,128)(2,1)} fusion(bf16[1024,2,128,1]{0,2,3,1:T(8,128)(2,1)} %bitcast.168, f32[2,1024,1024,2]{2,1,3,0:T(8,128)} %get-tuple-element.167, f32[2,2,1024]{2,1,0:T(2,128)S(1)} %fusion.3, f32[2,2,1024]{2,1,0:T(2,128)S(1)} %get-tuple-element.166, pred[1024,1024]{0,1:T(8,128)(4,1)S(1)} %fusion.25), kind=kOutput, calls=%fused_computation.90 | convolution fusion | flops 1091043328 | bytes 19431424 | tf_op jit(solution)/shard_map/grqk,kgd->qgrd/dot_general | solution.py:192
  90.3 21.3 %collective-permute-done.1 = bf16[512,2048]{1,0:T(8,128)(2,1)} collective-permute-done((bf16[512,2048]{1,0:T(8,128)(2,1)}, bf16[512,2048]{1,0:T(8,128)(2,1)}, u32[]{:S(2)}, u32[]{:S(2)}) %collective-permute-start.1) | collective-permute-done | bytes 2097184 | tf_op jit(solution)/shard_map/ppermute | solution.py:58
  116.4 8.6 %fusion.29 = f32[1024,1536]{1,0:T(8,128)} fusion(bf16[1536,2048]{1,0:T(8,128)(2,1)S(1)} %bitcast.173, bf16[512,2048]{1,0:T(8,128)(2,1)S(1)} %get-tuple-element.107, bf16[512,2048]{1,0:T(8,128)(2,1)S(1)} %get-tuple-element.106), kind=kOutput, calls=%fused_computation.71 | convolution fusion | flops 6450839552 | bytes 16777216 | tf_op jit(solution)/shard_map/dot_general | solution.py:48
  125.0 9.3 %fusion.68 = f32[1024,1536]{1,0:T(8,128)} fusion(bf16[2048,1536]{1,0:T(8,128)(2,1)S(1)} %bitcast.177, bf16[512,2048]{1,0:T(8,128)(2,1)} %collective-permute-done.2, bf16[512,2048]{1,0:T(8,128)(2,1)S(1)} %multiply_convert_fusion.3), kind=kOutput, calls=%fused_computation.239 | convolution fusion | flops 6450839552 | bytes 16777216 | tf_op jit(solution)/shard_map/dot_general | solution.py:204
  134.3 16.5 %multiply_convert_fusion = (bf16[1024,1536]{1,0:T(8,128)(2,1)}, bf16[1024,1536]{1,0:T(8,128)(2,1)}, bf16[1024,1536]{1,0:T(8,128)(2,1)}) fusion(f32[1024,1536]{1,0:T(8,128)} %fusion.29, f32[1024,1536]{1,0:T(8,128)} %fusion.68, bf16[2048,1536]{1,0:T(8,128)(2,1)} %param.33, bf16[512,2048]{1,0:T(8,128)(2,1)} %collective-permute-done.2, ...), kind=kOutput, calls=%fused_computation.23 | convolution fusion | flops 6476005376 | bytes 32505856 | tf_op jit(solution)/shard_map/dot_general | solution.py:203
  150.8 9.0 %convolution_convert_fusion = bf16[1536,2048]{1,0:T(8,128)(2,1)S(1)} fusion(bf16[1024,1536]{1,0:T(8,128)(2,1)} %get-tuple-element.38, bf16[512,2048]{1,0:T(8,128)(2,1)S(1)} %get-tuple-element.107, bf16[512,2048]{1,0:T(8,128)(2,1)S(1)} %get-tuple-element.106), kind=kOutput, calls=%fused_computation.20 | convolution fusion | flops 6453985280 | bytes 13631488 | tf_op jit(solution)/shard_map/dot_general | solution.py:42
  159.8 13.1 %fusion.83 = f32[1024,2048]{1,0:T(8,128)} fusion(bf16[1024,1536]{1,0:T(8,128)(2,1)S(1)} %copy-done.71, bf16[1536,2048]{1,0:T(8,128)(2,1)} %param.35), kind=kOutput, calls=%fused_computation.250 | convolution fusion | flops 6442450944 | bytes 17825792 | tf_op jit(solution)/shard_map/dot_general | solution.py:212
  175.1 9.3 %convolution_convert_fusion.1 = bf16[2048,1536]{0,1:T(8,128)(2,1)S(1)} fusion(bf16[1024,1536]{1,0:T(8,128)(2,1)} %get-tuple-element.36, bf16[512,2048]{1,0:T(8,128)(2,1)} %collective-permute-done.2, bf16[512,2048]{1,0:T(8,128)(2,1)S(1)} %multiply_convert_fusion.3), kind=kOutput, calls=%fused_computation.21 | convolution fusion | flops 6453985280 | bytes 13631488 | tf_op jit(solution)/shard_map/dot_general | solution.py:42
  187.1 10.3 %fusion.84 = f32[1024,2048]{1,0:T(8,128)} fusion(bf16[1024,1536]{1,0:T(8,128)(2,1)} %get-tuple-element.37, bf16[2048,1536]{1,0:T(8,128)(2,1)S(1)} %bitcast.175), kind=kOutput, calls=%fused_computation.251 | convolution fusion | flops 6442450944 | bytes 17825792 | tf_op jit(solution)/shard_map/dot_general | solution.py:48
  197.4 9.1 %convolution_convert_fusion.2 = bf16[2048,1536]{0,1:T(8,128)(2,1)S(1)} fusion(bf16[1024,1536]{1,0:T(8,128)(2,1)} %get-tuple-element.37, bf16[512,2048]{1,0:T(8,128)(2,1)} %collective-permute-done.2, bf16[512,2048]{1,0:T(8,128)(2,1)S(1)} %multiply_convert_fusion.3), kind=kOutput, calls=%fused_computation.22 | convolution fusion | flops 6453985280 | bytes 13631488 | tf_op jit(solution)/shard_map/dot_general | solution.py:42
  208.5 13.2 %convolution_add_fusion = f32[1024,2048]{1,0:T(8,128)} fusion(f32[1024,2048]{1,0:T(8,128)} %fusion.84, bf16[1024,1536]{1,0:T(8,128)(2,1)} %get-tuple-element.36, bf16[2048,1536]{1,0:T(8,128)(2,1)} %param.34), kind=kOutput, calls=%fused_computation.65 | convolution fusion | flops 6444548096 | bytes 26214400 | tf_op jit(solution)/shard_map/dot_general | solution.py:48
  233.8 5.2 collective-permute-done.52
  282.8 6.8 %collective-permute-done.54 = bf16[256,768]{0,1:T(8,128)(2,1)S(1)} collective-permute-done((bf16[256,768]{0,1:T(8,128)(2,1)S(1)}, bf16[256,768]{0,1:T(8,128)(2,1)S(1)}, u32[]{:S(2)}, u32[]{:S(2)}) %collective-permute-start.54) | collective-permute-done | bytes 393248 | tf_op jit(solution)/shard_map/ppermute | solution.py:91
  292.8 5.2 collective-permute-done.83
  393.5 11.8 %fusion = (f32[2,2,1024]{2,1,0:T(2,128)S(1)}, f32[2,1024,1024,2]{2,1,3,0:T(8,128)}) fusion(f32[2,1024,1024,2]{2,1,3,0:T(8,128)} %get-tuple-element.167, f32[2,2,1024]{2,1,0:T(2,128)S(1)} %copy-done.49, pred[1024,1024]{0,1:T(8,128)(4,1)S(1)} %copy-done.6, bf16[1024,2,128,1]{0,2,3,1:T(8,128)(2,1)S(1)} %bitcast.169, bf16[1024,2,2,128]{0,3,2,1:T(8,128)(2,1)S(1)} %bitcast.163), kind=kOutput, calls=%fused_computation.2 | convolution fusion | flops 1090514944 | bytes 36208640 | tf_op jit(solution)/shard_map/qgrd,kgd->grqk/dot_general | solution.py:238
  405.3 12.0 %fusion.2 = bf16[2,2,1024,1024]{2,3,1,0:T(8,128)(2,1)S(1)} fusion(f32[2,1024,1024,2]{2,1,3,0:T(8,128)} %get-tuple-element.169, f32[2,1024,1024,2]{2,1,3,0:T(8,128)} %get-tuple-element.167, f32[2,2,1024]{2,1,0:T(2,128)S(1)} %get-tuple-element.168, f32[2,2,1024]{2,1,0:T(2,128)S(1)} %copy-done.49, pred[1024,1024]{0,1:T(8,128)(4,1)S(1)} %copy-done.6), kind=kLoop, calls=%fused_computation.4 | loop fusion | flops 20971520 | bytes 43024384 | tf_op jit(solution)/shard_map/convert_element_type | solution.py:239
  421.6 8.1 %fusion.40 = bf16[2,128,1024]{2,1,0:T(8,128)(2,1)S(1)} fusion(bf16[1024,2,2,128]{0,3,2,1:T(8,128)(2,1)S(1)} %bitcast.164, f32[2,1024,1024,2]{2,1,3,0:T(8,128)} %get-tuple-element.167, f32[2,2,1024]{2,1,0:T(2,128)S(1)} %copy-done.49, pred[1024,1024]{0,1:T(8,128)(4,1)S(1)} %copy-done.6), kind=kOutput, calls=%fused_computation.98 | convolution fusion | flops 1086586880 | bytes 19415040 | tf_op jit(solution)/shard_map/grqk,qgrd->kgd/dot_general | solution.py:234
  448.7 6.8 %convolution_convert_fusion.3 = bf16[2048,1024]{1,0:T(8,128)(2,1)S(1)} fusion(bf16[1024,256]{0,1:T(8,128)(2,1)S(1)} %bitcast.171, bf16[1024,256]{0,1:T(8,128)(2,1)S(1)} %bitcast.166, bf16[1024,512]{0,1:T(8,128)(2,1)S(1)} %bitcast.162, bf16[1024,2048]{1,0:T(8,128)(2,1)S(1)} %copy-done.12, f32[2048]{0:T(1024)S(1)} %copy-done.56, f32[1024]{0:T(1024)S(1)} %copy-done.68), kind=kOutput, calls=%fused_computation.66 | convolution fusion | flops 4311744512 | bytes 10498048 | tf_op jit(solution)/shard_map/dot_general | solution.py:42
  460.7 5.3 add_convert_fusion
  494.6 62.9 %collective-permute-done.12 = f32[256]{0:T(256)S(1)} collective-permute-done((f32[256]{0:T(256)S(1)}, f32[256]{0:T(256)S(1)}, u32[]{:S(2)}, u32[]{:S(2)}) %collective-permute-start.12) | collective-permute-done | bytes 1056 | tf_op jit(solution)/shard_map/ppermute | solution.py:58
  574.1 7.6 %fusion.20 = (bf16[512,2048]{1,0:T(8,128)(2,1)S(1)}, bf16[512,2048]{1,0:T(8,128)(2,1)S(1)}) fusion(bf16[512,2048]{1,0:T(8,128)(2,1)} %collective-permute-done.10, bf16[512,2048]{1,0:T(8,128)(2,1)} %add_convert_fusion, f32[512]{0:T(512)S(1)} %broadcast_multiply_fusion.5, f32[2048]{0:T(1024)S(1)} %copy-done.57, f32[512]{0:T(512)S(1)} %copy-done.58, ...), kind=kLoop, calls=%fused_computation.37 | loop fusion | flops 27262976 | bytes 25190404 | tf_op jit(solution)/shard_map/convert_element_type | solution.py:272
  (452 shorter events, 317.7 us)
Async XLA Ops:
  62.6 49.1 %collective-permute-start.1 = (bf16[512,2048]{1,0:T(8,128)(2,1)}, bf16[512,2048]{1,0:T(8,128)(2,1)}, u32[]{:S(2)}, u32[]{:S(2)}) collective-permute-start(bf16[512,2048]{1,0:T(8,128)(2,1)} %add_convert_fusion.2), channel_id=1, source_target_pairs={{0,2},{1,3},{2,0},{3,1},{4,6},{5,7},{6,4},{7,5},{8,10},{9,11},{10,... | collective-permute-start | bytes 6291464 | tf_op jit(solution)/shard_map/ppermute | solution.py:58
  173.0 54.0 %collective-permute-start.73 = (bf16[768,256]{1,0:T(8,128)(2,1)S(1)}, bf16[768,256]{1,0:T(8,128)(2,1)S(1)}, u32[]{:S(2)}, u32[]{:S(2)}) collective-permute-start(bf16[768,256]{1,0:T(8,128)(2,1)S(1)} %get-tuple-element.53), channel_id=1, source_target_pairs={{0,8},{8,16},{16,24},{24,28},{28,20},{20,12},{12,4},{4,0},{1,9},{9... | collective-permute-start | bytes 1179656 | tf_op jit(solution)/shard_map/ppermute | solution.py:91
  174.9 52.4 %collective-permute-start.80 = (bf16[768,256]{1,0:T(8,128)(2,1)S(1)}, bf16[768,256]{1,0:T(8,128)(2,1)S(1)}, u32[]{:S(2)}, u32[]{:S(2)}) collective-permute-start(bf16[768,256]{1,0:T(8,128)(2,1)S(1)} %get-tuple-element.54), channel_id=1, source_target_pairs={{8,0},{16,8},{24,16},{28,24},{20,28},{12,20},{4,12},{0,4},{9,1},{1... | collective-permute-start | bytes 1179656 | tf_op jit(solution)/shard_map/ppermute | solution.py:91
  184.6 44.0 %collective-permute-start.59 = (bf16[256,768]{0,1:T(8,128)(2,1)S(1)}, bf16[256,768]{0,1:T(8,128)(2,1)S(1)}, u32[]{:S(2)}, u32[]{:S(2)}) collective-permute-start(bf16[256,768]{0,1:T(8,128)(2,1)S(1)} %get-tuple-element.69), channel_id=1, source_target_pairs={{0,8},{8,16},{16,24},{24,28},{28,20},{20,12},{12,4},{4,0},{1,9},{9... | collective-permute-start | bytes 1179656 | tf_op jit(solution)/shard_map/ppermute | solution.py:91
  186.4 44.0 %collective-permute-start.66 = (bf16[256,768]{0,1:T(8,128)(2,1)S(1)}, bf16[256,768]{0,1:T(8,128)(2,1)S(1)}, u32[]{:S(2)}, u32[]{:S(2)}) collective-permute-start(bf16[256,768]{0,1:T(8,128)(2,1)S(1)} %get-tuple-element.70), channel_id=1, source_target_pairs={{8,0},{16,8},{24,16},{28,24},{20,28},{12,20},{4,12},{0,4},{9,1},{1... | collective-permute-start | bytes 1179656 | tf_op jit(solution)/shard_map/ppermute | solution.py:91
  206.6 25.4 %collective-permute-start.45 = (bf16[256,768]{0,1:T(8,128)(2,1)S(1)}, bf16[256,768]{0,1:T(8,128)(2,1)S(1)}, u32[]{:S(2)}, u32[]{:S(2)}) collective-permute-start(bf16[256,768]{0,1:T(8,128)(2,1)S(1)} %get-tuple-element.85), channel_id=1, source_target_pairs={{0,8},{8,16},{16,24},{24,28},{28,20},{20,12},{12,4},{4,0},{1,9},{9... | collective-permute-start | bytes 1179656 | tf_op jit(solution)/shard_map/ppermute | solution.py:91
  227.2 72.7 %collective-permute-start.6 = (bf16[512,2048]{1,0:T(8,128)(2,1)S(1)}, bf16[512,2048]{1,0:T(8,128)(2,1)S(1)}, u32[]{:S(2)}, u32[]{:S(2)}) collective-permute-start(bf16[512,2048]{1,0:T(8,128)(2,1)S(1)} %slice.95), channel_id=1, source_target_pairs={{0,1},{1,0},{2,3},{3,2},{4,5},{5,4},{6,7},{7,6},{8,9},{9,8},{10,11... | collective-permute-start | bytes 6291464 | tf_op jit(solution)/shard_map/ppermute | solution.py:54
  282.7 59.3 %collective-permute-start.3 = (bf16[512,2048]{1,0:T(8,128)(2,1)S(1)}, bf16[512,2048]{1,0:T(8,128)(2,1)S(1)}, u32[]{:S(2)}, u32[]{:S(2)}) collective-permute-start(bf16[512,2048]{1,0:T(8,128)(2,1)S(1)} %slice.96), channel_id=1, source_target_pairs={{0,1},{1,0},{2,3},{3,2},{4,5},{5,4},{6,7},{7,6},{8,9},{9,8},{10,11... | collective-permute-start | bytes 6291464 | tf_op jit(solution)/shard_map/ppermute | solution.py:54
  306.5 44.9 %collective-permute-start.7 = (bf16[512,2048]{1,0:T(8,128)(2,1)S(1)}, bf16[512,2048]{1,0:T(8,128)(2,1)S(1)}, u32[]{:S(2)}, u32[]{:S(2)}) collective-permute-start(bf16[512,2048]{1,0:T(8,128)(2,1)S(1)} %fusion.23), channel_id=1, source_target_pairs={{0,2},{1,3},{2,0},{3,1},{4,6},{5,7},{6,4},{7,5},{8,10},{9,11},{10,... | collective-permute-start | bytes 6291464 | tf_op jit(solution)/shard_map/ppermute | solution.py:58
  331.7 24.6 %collective-permute-start.78 = (bf16[768,256]{1,0:T(8,128)(2,1)S(1)}, bf16[768,256]{1,0:T(8,128)(2,1)S(1)}, u32[]{:S(2)}, u32[]{:S(2)}) collective-permute-start(bf16[768,256]{1,0:T(8,128)(2,1)S(1)} %get-tuple-element.43), channel_id=1, source_target_pairs={{0,8},{8,16},{16,24},{24,28},{28,20},{20,12},{12,4},{4,0},{1,9},{9... | collective-permute-start | bytes 1179656 | tf_op jit(solution)/shard_map/ppermute | solution.py:91
  334.7 22.2 %collective-permute-start.85 = (bf16[768,256]{1,0:T(8,128)(2,1)S(1)}, bf16[768,256]{1,0:T(8,128)(2,1)S(1)}, u32[]{:S(2)}, u32[]{:S(2)}) collective-permute-start(bf16[768,256]{1,0:T(8,128)(2,1)S(1)} %get-tuple-element.44), channel_id=1, source_target_pairs={{8,0},{16,8},{24,16},{28,24},{20,28},{12,20},{4,12},{0,4},{9,1},{1... | collective-permute-start | bytes 1179656 | tf_op jit(solution)/shard_map/ppermute | solution.py:91
  340.2 18.0 %collective-permute-start.64 = (bf16[256,768]{0,1:T(8,128)(2,1)S(1)}, bf16[256,768]{0,1:T(8,128)(2,1)S(1)}, u32[]{:S(2)}, u32[]{:S(2)}) collective-permute-start(bf16[256,768]{0,1:T(8,128)(2,1)S(1)} %get-tuple-element.59), channel_id=1, source_target_pairs={{0,8},{8,16},{16,24},{24,28},{28,20},{20,12},{12,4},{4,0},{1,9},{9... | collective-permute-start | bytes 1179656 | tf_op jit(solution)/shard_map/ppermute | solution.py:91
  342.0 17.8 %collective-permute-start.71 = (bf16[256,768]{0,1:T(8,128)(2,1)S(1)}, bf16[256,768]{0,1:T(8,128)(2,1)S(1)}, u32[]{:S(2)}, u32[]{:S(2)}) collective-permute-start(bf16[256,768]{0,1:T(8,128)(2,1)S(1)} %get-tuple-element.60), channel_id=1, source_target_pairs={{8,0},{16,8},{24,16},{28,24},{20,28},{12,20},{4,12},{0,4},{9,1},{1... | collective-permute-start | bytes 1179656 | tf_op jit(solution)/shard_map/ppermute | solution.py:91
  356.9 32.9 %collective-permute-start.8 = (bf16[512,2048]{1,0:T(8,128)(2,1)S(1)}, bf16[512,2048]{1,0:T(8,128)(2,1)S(1)}, u32[]{:S(2)}, u32[]{:S(2)}) collective-permute-start(bf16[512,2048]{1,0:T(8,128)(2,1)S(1)} %fusion.70), channel_id=1, source_target_pairs={{0,1},{1,0},{2,3},{3,2},{4,5},{5,4},{6,7},{7,6},{8,9},{9,8},{10,11... | collective-permute-start | bytes 6291464 | tf_op jit(solution)/shard_map/ppermute | solution.py:54
  458.4 18.7 %collective-permute-start.33 = (bf16[256,256]{1,0:T(8,128)(2,1)}, bf16[256,256]{1,0:T(8,128)(2,1)S(1)}, u32[]{:S(2)}, u32[]{:S(2)}) collective-permute-start(bf16[256,256]{1,0:T(8,128)(2,1)} %get-tuple-element.118), channel_id=1, source_target_pairs={{0,8},{8,16},{16,24},{24,28},{28,20},{20,12},{12,4},{4,0},{1,9},{9... | collective-permute-start | bytes 393224 | tf_op jit(solution)/shard_map/ppermute | solution.py:91
  460.0 17.7 %collective-permute-start.40 = (bf16[256,256]{1,0:T(8,128)(2,1)S(1)}, bf16[256,256]{1,0:T(8,128)(2,1)S(1)}, u32[]{:S(2)}, u32[]{:S(2)}) collective-permute-start(bf16[256,256]{1,0:T(8,128)(2,1)S(1)} %get-tuple-element.119), channel_id=1, source_target_pairs={{8,0},{16,8},{24,16},{28,24},{20,28},{12,20},{4,12},{0,4},{9,1},{1... | collective-permute-start | bytes 393224 | tf_op jit(solution)/shard_map/ppermute | solution.py:91
  466.0 103.7 %collective-permute-start.10 = (bf16[512,2048]{1,0:T(8,128)(2,1)}, bf16[512,2048]{1,0:T(8,128)(2,1)}, u32[]{:S(2)}, u32[]{:S(2)}) collective-permute-start(bf16[512,2048]{1,0:T(8,128)(2,1)} %add_convert_fusion), channel_id=1, source_target_pairs={{0,2},{1,3},{2,0},{3,1},{4,6},{5,7},{6,4},{7,5},{8,10},{9,11},{10,... | collective-permute-start | bytes 6291464 | tf_op jit(solution)/shard_map/ppermute | solution.py:58
  477.1 96.9 %collective-permute-start.4 = (bf16[512,2048]{1,0:T(8,128)(2,1)}, bf16[512,2048]{1,0:T(8,128)(2,1)S(1)}, u32[]{:S(2)}, u32[]{:S(2)}) collective-permute-start(bf16[512,2048]{1,0:T(8,128)(2,1)} %fusion.24), channel_id=1, source_target_pairs={{0,2},{1,3},{2,0},{3,1},{4,6},{5,7},{6,4},{7,5},{8,10},{9,11},{10,... | collective-permute-start | bytes 6291464 | tf_op jit(solution)/shard_map/ppermute | solution.py:58
  487.1 70.5 %collective-permute-start.12 = (f32[256]{0:T(256)S(1)}, f32[256]{0:T(256)S(1)}, u32[]{:S(2)}, u32[]{:S(2)}) collective-permute-start(f32[256]{0:T(256)S(1)} %pad_maximum_fusion.16), channel_id=1, source_target_pairs={{0,2},{1,3},{2,0},{3,1},{4,6},{5,7},{6,4},{7,5},{8,10},{9,11},{10,... | collective-permute-start | bytes 3080 | tf_op jit(solution)/shard_map/ppermute | solution.py:58
  489.3 69.9 %collective-permute-start.35 = (bf16[256,256]{1,0:T(8,128)(2,1)S(1)}, bf16[256,256]{1,0:T(8,128)(2,1)S(1)}, u32[]{:S(2)}, u32[]{:S(2)}) collective-permute-start(bf16[256,256]{1,0:T(8,128)(2,1)S(1)} %get-tuple-element.114), channel_id=1, source_target_pairs={{0,8},{8,16},{16,24},{24,28},{28,20},{20,12},{12,4},{4,0},{1,9},{9... | collective-permute-start | bytes 393224 | tf_op jit(solution)/shard_map/ppermute | solution.py:91
  493.0 66.6 %collective-permute-start.42 = (bf16[256,256]{1,0:T(8,128)(2,1)S(1)}, bf16[256,256]{1,0:T(8,128)(2,1)S(1)}, u32[]{:S(2)}, u32[]{:S(2)}) collective-permute-start(bf16[256,256]{1,0:T(8,128)(2,1)S(1)} %get-tuple-element.115), channel_id=1, source_target_pairs={{8,0},{16,8},{24,16},{28,24},{20,28},{12,20},{4,12},{0,4},{9,1},{1... | collective-permute-start | bytes 393224 | tf_op jit(solution)/shard_map/ppermute | solution.py:91
  560.9 20.9 %collective-permute-start.36 = (bf16[256,256]{1,0:T(8,128)(2,1)S(1)}, bf16[256,256]{1,0:T(8,128)(2,1)S(1)}, u32[]{:S(2)}, u32[]{:S(2)}) collective-permute-start(bf16[256,256]{1,0:T(8,128)(2,1)S(1)} %get-tuple-element.112), channel_id=1, source_target_pairs={{0,8},{8,16},{16,24},{24,28},{28,20},{20,12},{12,4},{4,0},{1,9},{9... | collective-permute-start | bytes 393224 | tf_op jit(solution)/shard_map/ppermute | solution.py:91
  581.7 33.1 %collective-permute-start.11 = (bf16[512,2048]{1,0:T(8,128)(2,1)S(1)}, bf16[512,2048]{1,0:T(8,128)(2,1)S(1)}, u32[]{:S(2)}, u32[]{:S(2)}) collective-permute-start(bf16[512,2048]{1,0:T(8,128)(2,1)S(1)} %get-tuple-element.103), channel_id=1, source_target_pairs={{0,1},{1,0},{2,3},{3,2},{4,5},{5,4},{6,7},{7,6},{8,9},{9,8},{10,11... | collective-permute-start | bytes 6291464 | tf_op jit(solution)/shard_map/ppermute | solution.py:54
  588.8 29.5 %collective-permute-start.5 = (bf16[512,2048]{1,0:T(8,128)(2,1)S(1)}, bf16[512,2048]{1,0:T(8,128)(2,1)S(1)}, u32[]{:S(2)}, u32[]{:S(2)}) collective-permute-start(bf16[512,2048]{1,0:T(8,128)(2,1)S(1)} %get-tuple-element.104), channel_id=1, source_target_pairs={{0,1},{1,0},{2,3},{3,2},{4,5},{5,4},{6,7},{7,6},{8,9},{9,8},{10,11... | collective-permute-start | bytes 6291464 | tf_op jit(solution)/shard_map/ppermute | solution.py:54
  (143 other events, 2693.0 us)

commit v2 on v1

v2 whole, which is shorter than its diff:
```python
import functools

import jax
import jax.numpy as jnp
import numpy as np
from jax import lax
from jax.experimental import pallas as pl
from jax.experimental.pallas import tpu as pltpu
from jax.sharding import PartitionSpec as P

EPS = 1e-06
THETA = 1000000.0
CORE_SWAP = ((0, 1), (1, 0), (2, 3), (3, 2))
CHIP_SWAP = ((0, 2), (1, 3), (2, 0), (3, 1))
BLOCK = 256
MIB = 1024 * 1024
COST = pl.CostEstimate(flops=0, bytes_accessed=0, transcendentals=0)


def dot_nn(left, right):
    return jnp.dot(left, right, preferred_element_type=jnp.float32)


def dot_nt(left, right):
    return lax.dot_general(
        left, right, (((1,), (1,)), ((), ())), preferred_element_type=jnp.float32
    )


def dot_tn(left, right):
    return lax.dot_general(
        left, right, (((0,), (0,)), ((), ())), preferred_element_type=jnp.float32
    )


def hbm(value):
    return pltpu.with_memory_space_constraint(value, pltpu.HBM)


def row_mean(value):
    return jnp.mean(value, -1, keepdims=True)


def front_kernel(
    x_ref, gain_ref, wq_ref, wk_ref, wv_ref, cos_ref, sin_ref, qg_ref, kg_ref,
    normed_ref, q_ref, k_ref, v_ref, ql_ref, kl_ref,
):
    size = cos_ref.shape[1]
    x = x_ref[...].astype(jnp.float32)
    factor = lax.rsqrt(row_mean(x * x) + EPS)
    normed = (x * factor * gain_ref[...]).astype(jnp.bfloat16)
    normed_ref[...] = normed
    cosine, sine = cos_ref[...], sin_ref[...]

    def heads(lin, gain, scale, lin_ref, out_ref):
        lin_ref[...] = lin
        for head in range(lin.shape[1] // size):
            cols = slice(head * size, (head + 1) * size)
            part = lin[:, cols]
            scaled = part * lax.rsqrt(row_mean(part * part) + EPS) * gain
            turned = scaled * cosine + pltpu.roll(scaled, size // 2, 1) * sine
            out_ref[:, cols] = (turned * scale).astype(jnp.bfloat16)

    heads(dot_nn(normed, wq_ref[...]), qg_ref[...], size ** (-0.5), ql_ref, q_ref)
    heads(dot_nn(normed, wk_ref[...]), kg_ref[...], 1.0, kl_ref, k_ref)
    v_ref[...] = dot_nn(normed, wv_ref[...]).astype(jnp.bfloat16)


def front(tokens, gain, wq, wk, wv, cosine, sine, q_gain, k_gain):
    count, width = tokens.shape
    size = cosine.shape[1]
    q_cols, k_cols = wq.shape[1], wk.shape[1]

    def rows(cols):
        return pl.BlockSpec((BLOCK, cols), lambda i: (i, 0))

    def whole(*shape):
        return pl.BlockSpec(shape, lambda i: (0,) * len(shape))

    def out(cols, kind):
        return pltpu.HBM((count, cols), kind)

    return pl.pallas_call(
        front_kernel,
        grid=(count // BLOCK,),
        in_specs=[
            rows(width), whole(1, width), whole(width, q_cols), whole(width, k_cols),
            whole(width, k_cols), rows(size), rows(size), whole(1, size), whole(1, size),
        ],
        out_specs=[rows(width), rows(q_cols), rows(k_cols), rows(k_cols), rows(q_cols), rows(k_cols)],
        out_shape=[
            out(width, jnp.bfloat16), out(q_cols, jnp.bfloat16), out(k_cols, jnp.bfloat16),
            out(k_cols, jnp.bfloat16), out(q_cols, jnp.float32), out(k_cols, jnp.float32),
        ],
        compiler_params=pltpu.CompilerParams(vmem_limit_bytes=40 * MIB),
        cost_estimate=COST,
        name="front",
    )(tokens, gain[None, :], wq, wk, wv, cosine, sine, q_gain[None, :], k_gain[None, :])


def pair_rows(value, size):
    return jnp.concatenate([value[:, i : i + size] for i in range(0, value.shape[1], size)], 0)


def placed(number, core_ref):
    spot = number // 2 * 2 + (core_ref[0] ^ (number % 2))
    return pl.ds(pl.multiple_of(spot * BLOCK, BLOCK), BLOCK)


def attend_kernel(first, q_ref, k_ref, v_ref, col_ref, row_ref, out_ref, *prob_refs):
    size = k_ref.shape[1]
    group = q_ref.shape[1] // size
    for number, prob_ref in enumerate(prob_refs):
        begin = (first + number) * BLOCK
        reach = begin + BLOCK
        rows = slice(number * BLOCK, (number + 1) * BLOCK)
        here = lax.broadcasted_iota(jnp.int32, (BLOCK, reach), 0) + begin
        there = lax.broadcasted_iota(jnp.int32, (BLOCK, reach), 1)
        allowed = (col_ref[rows, :] == row_ref[:, :reach]) & (there <= here)
        bias = jnp.where(allowed, 0.0, -1e30)
        queries = q_ref[rows, :]
        for head in range(group):
            cols = slice(head * size, (head + 1) * size)
            expo = jnp.exp(dot_nt(queries[:, cols], k_ref[:reach, :]) + bias)
            share = 1.0 / jnp.sum(expo, -1, keepdims=True)
            probs = (expo * share).astype(jnp.bfloat16)
            prob_ref[0, head * BLOCK : (head + 1) * BLOCK, :] = probs
            out_ref[rows, cols] = dot_nn(probs, v_ref[:reach, :]).astype(jnp.bfloat16)


def attend(queries, keys, values, seg_ids, part, parts):
    count = queries.shape[0]
    size = 128
    heads = keys.shape[1] // size
    group = queries.shape[1] // keys.shape[1]
    rows = count // parts
    blocks = rows // BLOCK
    first = part * blocks
    reach = (part + 1) * rows
    spans = [(first + i + 1) * BLOCK for i in range(blocks)]
    return pl.pallas_call(
        functools.partial(attend_kernel, first),
        grid=(heads,),
        in_specs=[
            pl.BlockSpec((rows, group * size), lambda g: (part, g)),
            pl.BlockSpec((reach, size), lambda g: (0, g)),
            pl.BlockSpec((reach, size), lambda g: (0, g)),
            pl.BlockSpec((rows, 1), lambda g: (part, 0)),
            pl.BlockSpec((1, reach), lambda g: (0, 0)),
        ],
        out_specs=[pl.BlockSpec((rows, group * size), lambda g: (0, g))]
        + [pl.BlockSpec((1, group * BLOCK, span), lambda g: (g, 0, 0)) for span in spans],
        out_shape=[jax.ShapeDtypeStruct((rows, heads * group * size), jnp.bfloat16)]
        + [pltpu.HBM((heads, group * BLOCK, span), jnp.bfloat16) for span in spans],
        compiler_params=pltpu.CompilerParams(vmem_limit_bytes=40 * MIB),
        cost_estimate=COST,
        name="attend",
    )(hbm(queries), hbm(keys), hbm(values), seg_ids[:, None], seg_ids[None, :])


def attend_back_kernel(blocks, *refs):
    core_ref, g_ref, q_ref, k_ref, v_ref, ql_ref, kl_ref, cos_ref, sin_ref, qg_ref, kg_ref = refs[:11]
    prob_refs = refs[11 : 11 + blocks]
    dq_out, dk_out, dv_out, gains_ref, dk_ref, dv_ref = refs[-6:]
    size = k_ref.shape[1]
    group = q_ref.shape[1] // size

    def turned_back(value, rows):
        value = value.astype(jnp.bfloat16).astype(jnp.float32)
        return value * cos_ref[rows, :] - pltpu.roll(value, size // 2, 1) * sin_ref[rows, :]

    def unnorm(grad, lin, gain):
        factor = lax.rsqrt(row_mean(lin * lin) + EPS)
        hat = lin * factor
        scaled = grad * gain
        back = factor * (scaled - hat * row_mean(scaled * hat))
        return back.astype(jnp.bfloat16), jnp.sum(grad * hat, 0, keepdims=True)

    dk_ref[...] = jnp.zeros_like(dk_ref)
    dv_ref[...] = jnp.zeros_like(dv_ref)
    q_sum = jnp.zeros((1, size), jnp.float32)
    for number in range(blocks):
        rows = slice(number * BLOCK, (number + 1) * BLOCK)
        reach = (number + 1) * BLOCK
        for head in range(group):
            cols = slice(head * size, (head + 1) * size)
            grad = g_ref[placed(number, core_ref), cols]
            probs = prob_refs[number][0, head * BLOCK : (head + 1) * BLOCK, :]
            d_probs = dot_nt(grad, v_ref[:reach, :])
            probs_wide = probs.astype(jnp.float32)
            both = probs_wide * d_probs
            d_scores = (both - probs_wide * jnp.sum(both, -1, keepdims=True)).astype(jnp.bfloat16)
            dv_ref[:reach, :] += dot_tn(probs, grad)
            dk_ref[:reach, :] += dot_tn(d_scores, q_ref[rows, cols])
            d_query = dot_nn(d_scores, k_ref[:reach, :])
            turned = turned_back(d_query, rows)
            back, total = unnorm(turned * size ** (-0.5), ql_ref[rows, cols], qg_ref[...])
            dq_out[rows, cols] = back
            q_sum = q_sum + total
    turned = turned_back(dk_ref[...], slice(None))
    back, k_sum = unnorm(turned, kl_ref[...], kg_ref[...])
    dk_out[...] = back
    dv_out[...] = dv_ref[...].astype(jnp.bfloat16)
    gains_ref[0:1, :] = q_sum
    gains_ref[1:2, :] = k_sum
    gains_ref[2:, :] = jnp.zeros((6, size), jnp.float32)


def attend_back(core, grad, queries, keys, values, q_lin, k_lin, cosine, sine, q_gain, k_gain, probs, g, before):
    count = queries.shape[0]
    size = cosine.shape[1]
    group = queries.shape[1] // keys.shape[1]
    blocks = len(probs)

    def cols(width):
        return pl.BlockSpec((count, width), lambda i: (0, g))

    def whole(rows):
        return pl.BlockSpec((rows, size), lambda i: (0, 0))

    return pl.pallas_call(
        functools.partial(attend_back_kernel, blocks),
        grid=(1,),
        in_specs=[
            pl.BlockSpec(memory_space=pltpu.SMEM),
            cols(group * size), cols(group * size), cols(size), cols(size), cols(group * size),
            cols(size), whole(count), whole(count), whole(1), whole(1),
        ]
        + [pl.BlockSpec((1, *p.shape[1:]), lambda i: (g, 0, 0)) for p in probs]
        + [pl.BlockSpec(memory_space=pl.ANY)] * len(before),
        out_specs=[cols(group * size), cols(size), cols(size), whole(8)],
        out_shape=[
            jax.ShapeDtypeStruct(queries.shape, jnp.bfloat16),
            jax.ShapeDtypeStruct(keys.shape, jnp.bfloat16),
            jax.ShapeDtypeStruct(keys.shape, jnp.bfloat16),
            jax.ShapeDtypeStruct((8, size), jnp.float32),
        ],
        input_output_aliases={11 + blocks + i: i for i in range(len(before))},
        scratch_shapes=[pltpu.VMEM((count, size), jnp.float32)] * 2,
        compiler_params=pltpu.CompilerParams(vmem_limit_bytes=40 * MIB),
        cost_estimate=COST,
        name="attend_back",
    )(
        core, grad, hbm(queries), hbm(keys), hbm(values), hbm(q_lin), hbm(k_lin), cosine, sine,
        q_gain[None, :], k_gain[None, :], *[hbm(p) for p in probs], *before,
    )


def feed_kernel(mine_ref, other_ref, wg_ref, wu_ref, dh_ref, *refs):
    inner_ref, hidden_ref, dg_ref, du_ref = refs[-4:]
    inner = jnp.concatenate([mine_ref[...], other_ref[...]], 0)

    @pl.when(pl.program_id(0) == 0)
    def _():
        inner_ref[...] = inner

    gate = dot_nn(inner, wg_ref[...])
    up = dot_nn(inner, wu_ref[...])
    sig = 1.0 / (1.0 + jnp.exp(-gate))
    silu = gate * sig
    d_hidden = dh_ref[...].astype(jnp.float32)
    hidden_ref[...] = (silu * up).astype(jnp.bfloat16)
    du_ref[...] = (d_hidden * silu).astype(jnp.bfloat16)
    dg_ref[...] = (d_hidden * up * (sig + silu * (1.0 - sig))).astype(jnp.bfloat16)


def feed(mine, other, w_gate, w_up, d_hidden, part, before, cols=512):
    rows, width = mine.shape
    count, units = d_hidden.shape
    here = pl.BlockSpec((2 * rows, width), lambda j: (part, 0))
    block = pl.BlockSpec((2 * rows, cols), lambda j: (part, j))
    weight = pl.BlockSpec((width, cols), lambda j: (0, j))
    half = pl.BlockSpec((rows, width), lambda j: (0, 0))
    out = jax.ShapeDtypeStruct((count, units), jnp.bfloat16)
    return pl.pallas_call(
        feed_kernel,
        grid=(units // cols,),
        in_specs=[half, half, weight, weight, block]
        + [pl.BlockSpec(memory_space=pl.ANY)] * len(before),
        out_specs=[here, block, block, block],
        out_shape=[jax.ShapeDtypeStruct((count, width), jnp.bfloat16), out, out, out],
        input_output_aliases={5 + i: i for i in range(len(before))},
        compiler_params=pltpu.CompilerParams(vmem_limit_bytes=40 * MIB),
        cost_estimate=COST,
        name="feed",
    )(mine, other, w_gate, w_up, d_hidden, *before)


ROWS = 128


def rows_call(kernel, name, rows, ins, outs):
    def spec(shape):
        if shape[0] == rows:
            return pl.BlockSpec((ROWS, shape[1]), lambda i: (i, 0))
        return pl.BlockSpec(shape, lambda i: (0, 0))

    return pl.pallas_call(
        kernel,
        grid=(rows // ROWS,),
        in_specs=[spec(a.shape) for a in ins],
        out_specs=[spec(o.shape) for o in outs],
        out_shape=outs,
        compiler_params=pltpu.CompilerParams(vmem_limit_bytes=24 * MIB),
        cost_estimate=COST,
        name=name,
    )(*ins)


def wide(ref):
    return ref[...].astype(jnp.float32)


def settle_kernel(x_ref, near_ref, far_ref, gain_ref, resid_ref, inner_ref):
    resid = wide(x_ref) + (wide(near_ref) + wide(far_ref))
    resid_ref[...] = resid
    factor = lax.rsqrt(row_mean(resid * resid) + EPS)
    inner_ref[...] = (resid * factor * gain_ref[...]).astype(jnp.bfloat16)


def settle(x, near, far, gain):
    rows, width = x.shape
    return rows_call(
        settle_kernel, "settle", rows, (x, near, far, gain[None, :]),
        [jax.ShapeDtypeStruct((rows, width), jnp.float32), jax.ShapeDtypeStruct((rows, width), jnp.bfloat16)],
    )


def unsettle_kernel(near_ref, far_ref, resid_ref, grad_ref, gain_ref, out_ref, low_ref, sum_ref):
    @pl.when(pl.program_id(0) == 0)
    def _():
        sum_ref[...] = jnp.zeros_like(sum_ref)

    resid = resid_ref[...].astype(jnp.float32)
    factor = lax.rsqrt(row_mean(resid * resid) + EPS)
    hat = resid * factor
    d_inner = wide(near_ref) + wide(far_ref)
    both = d_inner * hat
    sum_ref[0:1, :] += jnp.sum(both, 0, keepdims=True)
    scaled = d_inner * gain_ref[...]
    back = wide(grad_ref) + factor * (scaled - hat * row_mean(both * gain_ref[...]))
    out_ref[...] = back.astype(out_ref.dtype)
    if low_ref is not None:
        low_ref[...] = back.astype(jnp.bfloat16)


def last_kernel(near_ref, far_ref, resid_ref, grad_ref, gain_ref, out_ref, sum_ref):
    unsettle_kernel(near_ref, far_ref, resid_ref, grad_ref, gain_ref, out_ref, None, sum_ref)


def unsettle(near, far, resid, grad, gain):
    rows, width = near.shape
    return rows_call(
        unsettle_kernel, "unsettle", rows, (near, far, resid, grad, gain[None, :]),
        [
            jax.ShapeDtypeStruct((rows, width), jnp.float32),
            jax.ShapeDtypeStruct((rows, width), jnp.bfloat16),
            jax.ShapeDtypeStruct((8, width), jnp.float32),
        ],
    )


def unsettle_last(near, far, resid, grad, gain):
    rows, width = near.shape
    return rows_call(
        last_kernel, "unsettle_last", rows, (near, far, resid, grad, gain[None, :]),
        [jax.ShapeDtypeStruct((rows, width), jnp.bfloat16), jax.ShapeDtypeStruct((8, width), jnp.float32)],
    )


def live_rows_kernel(core_ref, value_ref, seg_ref, out_ref):
    out_ref[...] = jnp.where(seg_ref[...] >= 0, value_ref[...].astype(jnp.float32), 0.0).astype(jnp.bfloat16)


def live_rows(core, value, seg_ids):
    count, width = value.shape

    def from_block(i, core_ref):
        return (i ^ core_ref[0], 0)

    return pl.pallas_call(
        live_rows_kernel,
        grid_spec=pltpu.PrefetchScalarGridSpec(
            num_scalar_prefetch=1,
            grid=(count // BLOCK,),
            in_specs=[pl.BlockSpec((BLOCK, width), from_block), pl.BlockSpec((BLOCK, 1), from_block)],
            out_specs=pl.BlockSpec((BLOCK, width), lambda i, core_ref: (i, 0)),
        ),
        out_shape=jax.ShapeDtypeStruct((count, width), jnp.bfloat16),
        compiler_params=pltpu.CompilerParams(vmem_limit_bytes=24 * MIB),
        cost_estimate=COST,
        name="live_rows",
    )(core, value, seg_ids[:, None])


def ring_of(n):
    order = list(range(0, n, 2)) + [i for i in range(n - 1, 0, -1) if i % 2]
    place = [0] * n
    for spot, index in enumerate(order):
        place[index] = spot
    ahead = tuple((order[i], order[(i + 1) % n]) for i in range(n))
    back = tuple((b, a) for a, b in ahead)
    return order, place, ahead, back


def ring_table(n):
    order, place, _, _ = ring_of(n)
    table = [
        [[order[(place[i] - 1 - s) % n], order[(place[i] + 1 + s) % n]] for s in range(n)]
        for i in range(n)
    ]
    return jnp.asarray(np.array(table, np.int32).reshape(n, 2 * n))[lax.axis_index("dp")]


def ring_kernel(finish, step, *refs):
    where_ref, part_ref = refs[0], refs[-4]
    own_a, own_b, sem = refs[-3:]
    size, half = own_a.shape
    copies = []
    for side, own in enumerate((own_a, own_b)):
        begin = pl.multiple_of(where_ref[2 * step + side] * size, size)
        piece = part_ref.at[pl.ds(begin, size), pl.ds(side * half, half)]
        copies.append(pltpu.make_async_copy(piece, own, sem.at[side]))
    for copy in copies:
        copy.start()
    for copy in copies:
        copy.wait()
    finish(own_a, own_b, *refs[1:-4])


def ring_first(own_a, own_b, out_a_ref, out_b_ref):
    out_a_ref[...] = own_a[...]
    out_b_ref[...] = own_b[...]


def ring_add(own_a, own_b, came_a_ref, came_b_ref, out_a_ref, out_b_ref):
    out_a_ref[...] = (wide(came_a_ref) + wide(own_a)).astype(jnp.bfloat16)
    out_b_ref[...] = (wide(came_b_ref) + wide(own_b)).astype(jnp.bfloat16)


def ring_last(own_a, own_b, came_a_ref, came_b_ref, out_ref):
    half = own_a.shape[1]
    out_ref[:, :half] = wide(came_a_ref) + wide(own_a)
    out_ref[:, half:] = wide(came_b_ref) + wide(own_b)


def ring_last_turned(own_a, own_b, came_a_ref, came_b_ref, out_ref):
    half = own_a.shape[1]
    out_ref[:half, :] = (wide(came_a_ref) + wide(own_a)).T
    out_ref[half:, :] = (wide(came_b_ref) + wide(own_b)).T


def ring_last_lin(own_a, own_b, came_a_ref, came_b_ref, out_ref, q_ref, k_ref, v_ref):
    whole = jnp.concatenate([wide(came_a_ref) + wide(own_a), wide(came_b_ref) + wide(own_b)], 1)
    begin = 0
    for ref in (out_ref, q_ref, k_ref, v_ref):
        width = ref.shape[0] if ref is out_ref else ref.shape[1]
        part = whole[:, begin : begin + width]
        ref[...] = part.T if ref is out_ref else part
        begin += width


def ring_call(finish, n, where, step, came, part, out_shape):
    size, half = part.shape[0] // n, part.shape[1] // 2

    def kernel(*refs):
        outs = len(jax.tree.leaves(out_shape))
        ins = 1 + len(came)
        ring_kernel(
            finish, step, *refs[:ins], *refs[ins + 1 : ins + 1 + outs], refs[ins], *refs[ins + 1 + outs :]
        )

    return pl.pallas_call(
        kernel,
        in_specs=[pl.BlockSpec(memory_space=pltpu.SMEM)]
        + [pl.BlockSpec(memory_space=pltpu.VMEM)] * len(came)
        + [pl.BlockSpec(memory_space=pltpu.HBM)],
        out_specs=jax.tree.map(lambda o: pl.BlockSpec(memory_space=pltpu.VMEM), out_shape),
        out_shape=out_shape,
        scratch_shapes=[
            pltpu.VMEM((size, half), jnp.bfloat16),
            pltpu.VMEM((size, half), jnp.bfloat16),
            pltpu.SemaphoreType.DMA((2,)),
        ],
        compiler_params=pltpu.CompilerParams(vmem_limit_bytes=16 * MIB),
        cost_estimate=COST,
        name=finish.__name__,
    )(where, *came, hbm(part))


class Order:
    def __init__(self):
        self.last = None

    def run(self, piece, first, *rest):
        if self.last is not None:
            first, _ = lax.optimization_barrier((first, self.last))
        out = piece(first, *rest)
        self.last = jax.tree.leaves(out)[0]
        return out


    def tie(self, value):
        return lax.optimization_barrier((value, self.last))[0]


class Ring:
    def __init__(self, n, where, order, part, last, last_shapes):
        self.n, self.where, self.order, self.part = n, where, order, part
        self.last, self.last_shapes = last, last_shapes
        self.step_no = 0
        _, _, self.ahead, self.back = ring_of(n)
        size, half = part.shape[0] // n, part.shape[1] // 2
        self.out = [jax.ShapeDtypeStruct((size, half), jnp.bfloat16)] * 2
        self.send(self.call(ring_first, self.out))

    def call(self, finish, out):
        if self.step_no == 0:
            return self.order.run(
                lambda p: ring_call(finish, self.n, self.where, 0, (), p, out), self.part
            )
        return self.order.run(
            lambda a: ring_call(
                finish, self.n, self.where, self.step_no, (a, self.came[1]), self.part, out
            ),
            self.came[0],
        )

    def send(self, held):
        self.came = (lax.ppermute(held[0], "dp", self.ahead), lax.ppermute(held[1], "dp", self.back))

    def step(self):
        if self.step_no < self.n - 1:
            self.step_no += 1
            if self.step_no < self.n - 1:
                self.send(self.call(ring_add, self.out))
            else:
                self.result = self.call(self.last, self.last_shapes)

    def finish(self):
        while self.step_no < self.n - 1:
            self.step()
        return self.result


DOTS = {"nn": dot_nn, "nt": dot_nt, "tn": dot_tn}


def pairs_kernel(kind, outs, count, core_ref, *refs):
    out_refs = refs[-len(outs) :]
    for (spots, _), out_ref in zip(outs, out_refs):
        for i, spot in enumerate(spots):
            if spot < 0:
                rows = pl.ds(pl.multiple_of(((-1 - spot) ^ core_ref[0]) * BLOCK, BLOCK), BLOCK)
            else:
                rows = slice(spot * BLOCK, (spot + 1) * BLOCK)
            total = None
            for left_ref, right_ref in zip(refs[: 2 * count : 2], refs[1 : 2 * count : 2]):
                value = DOTS[kind](left_ref[rows, :], right_ref[...])
                total = value if total is None else total + value
            out_ref[i * BLOCK : (i + 1) * BLOCK, :] = total.astype(out_ref.dtype)


def pairs(core, kind, terms, outs, part=0, parts=1, before=(), cols=512):
    width = terms[0][1].shape[1 if kind == "nn" else 0]
    steps = width // cols // parts
    begin = part * steps
    ins, specs = [], []
    for left, right in terms:
        ins += [left, right]
        specs.append(pl.BlockSpec(left.shape, lambda j: (0, 0)))
        if kind == "nn":
            specs.append(pl.BlockSpec((right.shape[0], cols), lambda j: (0, begin + j)))
        else:
            specs.append(pl.BlockSpec((cols, right.shape[1]), lambda j: (begin + j, 0)))
    return pl.pallas_call(
        functools.partial(pairs_kernel, kind, outs, len(terms)),
        grid=(steps,),
        in_specs=[pl.BlockSpec(memory_space=pltpu.SMEM)]
        + specs
        + [pl.BlockSpec(memory_space=pl.ANY)] * len(before),
        out_specs=[pl.BlockSpec((len(o[0]) * BLOCK, cols), lambda j: (0, begin + j)) for o in outs],
        out_shape=[jax.ShapeDtypeStruct((len(o[0]) * BLOCK, width), o[1]) for o in outs],
        input_output_aliases={1 + len(ins) + i: i for i in range(len(before))},
        compiler_params=pltpu.CompilerParams(vmem_limit_bytes=40 * MIB),
        cost_estimate=COST,
        name="pairs",
    )(core, *[hbm(i) for i in ins], *before)


def near_kernel(mine_ref, came_ref, out_ref):
    out_ref[...] = (mine_ref[...] + wide(came_ref)).astype(jnp.bfloat16)


def near_add(came, mine):
    return rows_call(
        near_kernel, "near_add", mine.shape[0], (mine, came),
        [jax.ShapeDtypeStruct(mine.shape, jnp.bfloat16)],
    )[0]


def mixed_kernel(resid_ref, near_ref, far_ref, out_ref):
    out_ref[...] = (resid_ref[...] + (wide(near_ref) + wide(far_ref))).astype(jnp.bfloat16)


def nt_kernel(*refs):
    out_ref = refs[-1]
    begin = 0
    for left_ref in refs[1:-1]:
        rows = slice(begin, begin + left_ref.shape[0])
        out_ref[rows, :] = dot_nt(left_ref[...], refs[0][...]).astype(jnp.bfloat16)
        begin += left_ref.shape[0]


def times_turned(lefts, right, cols=512):
    rows = sum(left.shape[0] for left in lefts)
    return pl.pallas_call(
        nt_kernel,
        grid=(right.shape[0] // cols,),
        in_specs=[pl.BlockSpec((cols, right.shape[1]), lambda j: (j, 0))]
        + [pl.BlockSpec(left.shape, lambda j: (0, 0)) for left in lefts],
        out_specs=pl.BlockSpec((rows, cols), lambda j: (0, j)),
        out_shape=jax.ShapeDtypeStruct((rows, right.shape[0]), jnp.bfloat16),
        compiler_params=pltpu.CompilerParams(vmem_limit_bytes=40 * MIB),
        cost_estimate=COST,
        name="times_turned",
    )(right, *lefts)


def weight_grad_kernel(counts, *refs):
    out_ref = refs[-1]
    at, begin = 0, 0
    for lefts, rights in counts:
        left = refs[at][...]
        if lefts > 1:
            left = jnp.concatenate([ref[...] for ref in refs[at : at + lefts]], 0)
        for ref in refs[at + lefts : at + lefts + rights]:
            width = ref.shape[1]
            out_ref[:, begin : begin + width] = dot_tn(left, ref[...]).astype(jnp.bfloat16)
            begin += width
        at += lefts + rights


def weight_grad(groups, rows=256):
    width = groups[0][0][0].shape[1]
    ins, specs, cols = [], [], 0
    for lefts, rights in groups:
        ins += [*lefts, *rights]
        specs += [pl.BlockSpec((left.shape[0], rows), lambda i: (0, i)) for left in lefts]
        specs += [pl.BlockSpec(right.shape, lambda i: (0, 0)) for right in rights]
        cols += sum(right.shape[1] for right in rights)
    return pl.pallas_call(
        functools.partial(weight_grad_kernel, [(len(a), len(b)) for a, b in groups]),
        grid=(width // rows,),
        in_specs=specs,
        out_specs=pl.BlockSpec((rows, cols), lambda i: (i, 0)),
        out_shape=jax.ShapeDtypeStruct((width, cols), jnp.bfloat16),
        compiler_params=pltpu.CompilerParams(vmem_limit_bytes=32 * MIB),
        cost_estimate=COST,
        name="weight_grad",
    )(*[hbm(i) for i in ins])


def join_kernel(core_ref, mine_ref, other_ref, out_ref):
    @pl.when(pl.program_id(0) % 2 == 0)
    def _():
        out_ref[...] = mine_ref[...]

    @pl.when(pl.program_id(0) % 2 == 1)
    def _():
        out_ref[...] = other_ref[...]


def join(other, core, mine):
    rows, width = mine.shape
    block = pl.BlockSpec((BLOCK, width), lambda i, core_ref: (i >> 1, 0))
    return pl.pallas_call(
        join_kernel,
        grid_spec=pltpu.PrefetchScalarGridSpec(
            num_scalar_prefetch=1,
            grid=(2 * rows // BLOCK,),
            in_specs=[block, block],
            out_specs=pl.BlockSpec((BLOCK, width), lambda i, core_ref: (i ^ core_ref[0], 0)),
        ),
        out_shape=jax.ShapeDtypeStruct((2 * rows, width), mine.dtype),
        compiler_params=pltpu.CompilerParams(vmem_limit_bytes=24 * MIB),
        cost_estimate=COST,
        name="join",
    )(core, mine, other)


def to_core(value, pieces=1):
    share = value.shape[0] // pieces
    cut = [value[i * share : (i + 1) * share] for i in range(pieces)]
    came = [lax.ppermute(c, "tensor", CORE_SWAP) for c in cut]
    return jnp.concatenate(came, 0) if pieces > 1 else came[0]


def to_chip(value):
    return lax.ppermute(value, "tensor", CHIP_SWAP)


def low(value):
    return value.astype(jnp.bfloat16)


def all_sum_dp(n, value):
    step = 1
    while step < n:
        value = value + lax.ppermute(value, "dp", tuple((i, i ^ step) for i in range(n)))
        step *= 2
    return value


def on_device(
    n, tokens, seg_ids, cotangent, attn_gain, w_query, w_key, w_value, w_out, mlp_gain, w_gate, w_up,
    w_down, query_gain, key_gain,
):
    count, width = tokens.shape
    size = query_gain.shape[0]
    parts = 2
    rows = count // parts
    core_no = lax.axis_index("tensor") % 2
    core = core_no.astype(jnp.int32)[None]
    where = ring_table(n)
    order = Order()
    run = order.run

    def both_parts(piece):
        return [piece(j) for j in range(parts)]

    def own_rows(value, part, other=0):
        begin = part * rows + (core_no ^ other) * BLOCK
        return lax.dynamic_slice_in_dim(value, begin, BLOCK, 0)

    index = jnp.arange(count, dtype=jnp.int32)
    place = jnp.where(seg_ids >= 0, index - seg_ids, index).astype(jnp.float32)
    freq = THETA ** (-(jnp.arange(size // 2, dtype=jnp.float32) * 2.0) / size)
    turn = place[:, None] * freq[None, :]
    cosine, sine = jnp.cos(turn), jnp.sin(turn)
    cosine, sine = jnp.concatenate([cosine, cosine], -1), jnp.concatenate([-sine, sine], -1)

    normed, queries, keys, values, q_lin, k_lin = run(
        front, tokens, attn_gain, w_query, w_key, w_value, cosine, sine, query_gain, key_gain
    )
    wide_low = (jnp.float32, jnp.bfloat16)

    def mine_other(mine, other):
        return ((mine, wide_low[0]), (other, wide_low[1]))

    attended, probs, near, far = [], [], [], []
    for j in range(parts):
        out = run(lambda q: attend(q, keys, values, seg_ids, j, parts), queries)
        attended.append(out[0])
        probs += out[1:]
        mine, other = run(lambda a: pairs(core, "nn", [(a, w_out)], mine_other((-1,), (-2,))), out[0])
        near.append(run(near_add, to_core(other, 4), mine))
        far.append(to_chip(near[j]))

    grad_low = run(lambda c: live_rows(core, c, seg_ids), cotangent)
    d_hidden = run(lambda g: times_turned([g], w_down), grad_low)
    x_own = both_parts(lambda j: own_rows(tokens, j))

    resid, fed = [], ()
    for j in range(parts):
        held, inner_own = run(lambda f: settle(x_own[j], near[j], f, mlp_gain), far[j])
        resid.append(held)
        inner_other = to_core(inner_own, 4)
        fed = run(lambda o: feed(inner_own, o, w_gate, w_up, d_hidden, j, fed), inner_other)
    inner, hidden, d_gate, d_up = fed

    def shape(*extent):
        return jax.ShapeDtypeStruct(extent, jnp.float32)

    units, share = w_gate.shape[1], width // n
    q_cols, k_cols = w_query.shape[1], w_key.shape[1]
    active, results = [], {}

    def ring(name, part, last, last_shapes):
        active.append((name, Ring(n, where, order, part, last, last_shapes)))

    def tick():
        for item in list(active):
            item[1].step()
            if item[1].step_no == n - 1:
                results[item[0]] = item[1].result
                active.remove(item)

    down_part = run(lambda h: weight_grad([([grad_low], [h])]), hidden)
    ring("down", down_part, ring_last_turned, shape(units, share))
    made = ()
    for half in range(2):
        made = run(
            lambda d: pairs(
                core, "nt", [(d, w_gate), (d_up, w_up)], mine_other((0, 2), (1, 3)), half, 2, made
            ),
            d_gate,
        )
        tick()
    came3 = to_core(order.tie(made[1]))
    gate_part = run(lambda d: weight_grad([([inner], [d])]), d_gate)
    tick()
    near3 = run(near_add, came3, made[0])
    far3 = to_chip(near3)
    ring("gate", gate_part, ring_last, shape(share, units))
    up_part = run(lambda d: weight_grad([([inner], [d])]), d_up)
    tick()
    mixed_mine, mixed_other = run(
        lambda h: pairs(core, "nn", [(h, w_down)], mine_other((0, 2), (1, 3))), hidden
    )
    tick()
    blocks = [part[i : i + BLOCK] for part in attended for i in range(0, rows, BLOCK)]
    attended_mine_first = jnp.where(
        core_no == 0,
        jnp.concatenate(blocks, 0),
        jnp.concatenate([blocks[i ^ 1] for i in range(len(blocks))], 0),
    )
    grad_own = jnp.concatenate([grad_low[j * rows : j * rows + BLOCK] for j in range(parts)], 0)
    resid_own = jnp.concatenate(resid, 0)
    tick()
    d_resid, branch_own, mlp_sums = run(
        lambda f: unsettle(near3, f, resid_own, grad_own, mlp_gain), far3
    )
    both = to_core(jnp.concatenate([branch_own, order.tie(mixed_other)], 0))
    branch_other, came2 = both[: branch_own.shape[0]], both[branch_own.shape[0] :]
    tick()
    ring("up", up_part, ring_last, shape(share, units))
    near2 = run(near_add, came2, mixed_mine)
    far2 = to_chip(near2)
    d_branch = [b[j * BLOCK : (j + 1) * BLOCK] for j in range(parts) for b in (branch_own, branch_other)]
    d_attended = run(lambda d: times_turned([*d_branch[:-1], d], w_out), d_branch[-1])
    heads_count = k_cols // size
    d_lin, gain_sums = (), jnp.zeros((8, size), jnp.float32)
    for g in range(heads_count):
        *d_lin, total = run(
            lambda a: attend_back(
                core, a, queries, keys, values, q_lin, k_lin, cosine, sine, query_gain, key_gain,
                probs, g, d_lin,
            ),
            d_attended,
        )
        gain_sums = gain_sums + total
        tick()
    d_q_lin, d_k_lin, d_values = d_lin
    lin_part = run(
        lambda d: weight_grad([(d_branch, [attended_mine_first]), ([normed], [d, d_k_lin, d_values])]),
        d_q_lin,
    )
    mine, other = run(
        lambda d: pairs(
            core, "nt", [(d, w_query), (d_k_lin, w_key), (d_values, w_value)],
            mine_other((-1, -3), (-2, -4)),
        ),
        d_q_lin,
    )
    tick()
    ring(
        "lin", lin_part, ring_last_lin,
        [shape(q_cols, share), shape(share, q_cols), shape(share, k_cols), shape(share, k_cols)],
    )
    mixed = run(lambda f, n_, r: rows_call(
        mixed_kernel, "mixed", n_.shape[0], (r, n_, f), [jax.ShapeDtypeStruct(n_.shape, jnp.bfloat16)]
    )[0], far2, near2, resid_own)
    both = to_core(jnp.concatenate([mixed, order.tie(other)], 0))
    mixed_far, came4 = both[: mixed.shape[0]], both[mixed.shape[0] :]
    tick()
    near4 = run(near_add, came4, mine)
    far4 = to_chip(near4)
    mixed = run(join, mixed_far, core, mixed)
    tick()
    tick()
    tick()
    grad_tokens, attn_sums = run(
        lambda f: unsettle_last(near4, f, jnp.concatenate(x_own, 0), d_resid, attn_gain), far4
    )
    grad_tokens_other = to_core(grad_tokens)
    heads_sum = gain_sums[:2].reshape(-1)
    heads_sum = heads_sum + to_chip(heads_sum)
    gains = jnp.concatenate([mlp_sums[0], attn_sums[0], heads_sum])
    tick()
    grad_tokens = run(join, grad_tokens_other, core, grad_tokens)
    gains = all_sum_dp(n, gains + to_core(gains))
    while active:
        tick()
    my_dp = lax.axis_index("dp")

    def own(begin, extent):
        return lax.dynamic_slice(gains, (begin + my_dp * (extent // n),), (extent // n,))

    grad_out, grad_query, grad_key, grad_value = results["lin"]
    return (
        mixed,
        grad_tokens,
        own(width, width),
        grad_query,
        grad_key,
        grad_value,
        grad_out,
        own(0, width),
        results["gate"],
        results["up"],
        results["down"],
        own(2 * width, size),
        own(2 * width + size, size),
    )


def solution(mesh):
    rows, cols = P("dp", "tensor"), P("tensor", "dp")
    return jax.shard_map(
        functools.partial(on_device, mesh.shape["dp"]),
        mesh=mesh,
        in_specs=(
            P("dp", None), P("dp"), P("dp", None), P(), P(None, "tensor"), P(None, "tensor"),
            P(None, "tensor"), P("tensor", None), P(), P(None, "tensor"), P(None, "tensor"),
            P("tensor", None), P(), P(),
        ),
        out_specs=(
            P("dp", None), P("dp", None), P("dp"), rows, rows, rows, cols, P("dp"), rows, rows, cols,
            P("dp"), P("dp"),
        ),
        check_vma=False,
    )
```

time: 628 us -> 485 us (0.77)
  Pallas kernels: 0 us -> 254 us
  matrix products: 176 us -> 0 us
  waiting for transfers between devices: 203 us -> 102 us
  other arithmetic: 108 us -> 8.14 us
  between operations: 21 us -> 2.41 us
  starting transfers between devices: 86.4 us -> 70.1 us
  local copies, waits for them, and re-layouts: 28.1 us -> 43.2 us
    pallas_call x0 -> x64, Pallas kernels: none -> 254 us  [the longest x32 68.4 us: ring_call(): pl.pallas_call(kernel, in_specs=[pl.BlockSpec(memory_space=pltpu.SMEM)] +...]
    dot_general x25 -> x0, matrix products: 176 us -> none  [the longest x6 43.5 us: outer_dot(): lax.dot_general(left, right, (((1,), (1,)), ((), ())), preferred_element_...]
    ppermute x5 -> x6, waiting for transfers between devices: 88.9 us -> 1.26 us  [to_chip(): return lax.ppermute(value, 'tensor', CHIP_SWAP)]
    convert_element_type x40 -> x0, other arithmetic: 56 us -> none  [the longest x30 24.9 us: ring_scatter(): held[side] = held[side].astype(jnp.bfloat16)]
    reduce_sum x7 -> x0, other arithmetic: 23.4 us -> none  [the longest x1 8.78 us: on_device(): total = jnp.sum(expo, -1, keepdims=True)]
    ppermute x79 -> x77, waiting for transfers between devices: 106 us -> 86.9 us  [the longest x28 61.8 us: send(): lax.ppermute(held[0], 'dp', self.ahead)]
    unnamed x164 -> x135, local copies, waits for them, and re-layouts: 17.5 us -> 35.3 us
    ppermute x79 -> x77, starting transfers between devices: 77.5 us -> 60.9 us  [the longest x28 40.2 us: send(): lax.ppermute(held[0], 'dp', self.ahead)]
  transfers between devices with their start and end apart: 87 -> 86, of which waited for: 43 -> 46; matrix products, arithmetic and copies ran while one was open for 24% -> 2% of each run, Pallas kernels for 0% -> 39%
where the time goes in v2:
time: 485 us; the launch traced here: 480 us
  Pallas kernels  254 us (52%)
  waiting for transfers between devices  102 us (21%)
  starting transfers between devices  70.1 us (14%)
  local copies, waits for them, and re-layouts  43.2 us (9%)
  other arithmetic  8.14 us (2%)
    pallas_call x32, Pallas kernels, ring_call(): pl.pallas_call(kernel, in_specs=[pl.BlockSpec(memory_space=pltpu.SMEM)] +...  68.4 us
    ppermute x28, waiting for transfers between devices, send(): lax.ppermute(held[0], 'dp', self.ahead)  61.8 us
    pallas_call x6, Pallas kernels, pairs(): pl.pallas_call(functools.partial(pairs_kernel, kind, outs, len(terms)), g...  46.7 us
    pallas_call x4, Pallas kernels, weight_grad(): pl.pallas_call(functools.partial(weight_grad_kernel, [(len(a), len(b)) fo...  44.9 us
    ppermute x28, starting transfers between devices, send(): lax.ppermute(held[0], 'dp', self.ahead)  40.2 us
    unnamed x135, local copies, waits for them, and re-layouts  35.3 us
    pallas_call x2, Pallas kernels, feed(): pl.pallas_call(feed_kernel, grid=(units // cols,), in_specs=[half, half,...  23.7 us
    ppermute x28, waiting for transfers between devices, send(): lax.ppermute(held[1], 'dp', self.back)  18.8 us
  transfers between devices with their start and end apart: 86, of which 46 were waited for; matrix products, arithmetic and copies ran while one was open for 2% of the time, Pallas kernels for 39%

profile of v2, /device:TPU:0, one launch (start us, length us, event | category | flops | bytes accessed | tf_op | source)
XLA Modules:
  0.0 479.9 jit_solution(16042810409063896413)
XLA Ops:
  8.1 8.1 %front.1 = (bf16[1024,2048]{1,0:T(8,128)(2,1)}, bf16[1024,512]{1,0:T(8,128)(2,1)}, bf16[1024,256]{1,0:T(8,128)(2,1)}, bf16[1024,256]{1,0:T(8,128)(2,1)}, f32[1024,512]{1,0:T(8,128)}, /*index=5*/f32[1024,256]{1,0:T(8,128)}) custom-call(bf16[1024,2048]{1,0:T(8,128)(2,1)S(1)} %copy-done.18, f32[1,2048]{1,0:T(1,128)S(1)} %bitcast.23, ...), custom_call_target="tpu_custom_call" | custom-call | tf_op jit(solution)/shard_map/front/pallas_call | solution.py:83
  16.5 4.9 %attend.2 = (bf16[512,512]{1,0:T(8,128)(2,1)S(1)}, bf16[2,512,256]{2,1,0:T(8,128)(2,1)}, bf16[2,512,512]{2,1,0:T(8,128)(2,1)}) custom-call(bf16[1024,512]{1,0:T(8,128)(2,1)} %get-tuple-element.198.q_ref.refs_2_, bf16[1024,256]{1,0:T(8,128)(2,1)} %get-tuple-element.191.k_ref.refs_3_, bf16[1024,256]{1,0:T(8,128)(2,1)} %get-tuple-element.192.v_ref.refs_4_, ...), custom_call_target="tpu_custom_call" | custom-call | tf_op jit(solution)/shard_map/attend/pallas_call | solution.py:141
  32.0 6.5 %attend.3 = (bf16[512,512]{1,0:T(8,128)(2,1)S(1)}, bf16[2,512,768]{2,1,0:T(8,128)(2,1)}, bf16[2,512,1024]{2,1,0:T(8,128)(2,1)}) custom-call(bf16[1024,512]{1,0:T(8,128)(2,1)} %get-tuple-element.198.q_ref.refs_2_, bf16[1024,256]{1,0:T(8,128)(2,1)} %get-tuple-element.191.k_ref.refs_3_, bf16[1024,256]{1,0:T(8,128)(2,1)} %get-tuple-element.192.v_ref.refs_4_, ...), custom_call_target="tpu_custom_call" | custom-call | tf_op jit(solution)/shard_map/attend/pallas_call | solution.py:141
  55.4 7.3 %times_turned.2.dh_ref = bf16[1024,1536]{1,0:T(8,128)(2,1)S(1)} custom-call(bf16[1536,2048]{1,0:T(8,128)(2,1)S(1)} %bitcast.16, bf16[1024,2048]{1,0:T(8,128)(2,1)S(1)} %live_rows.1.refs_1_.refs_0_), custom_call_target="tpu_custom_call" | custom-call | tf_op jit(solution)/shard_map/times_turned/pallas_call | solution.py:617
  67.1 12.2 %feed.2 = (bf16[1024,2048]{1,0:T(8,128)(2,1)}, bf16[1024,1536]{1,0:T(8,128)(2,1)S(1)}, bf16[1024,1536]{1,0:T(8,128)(2,1)S(1)}, bf16[1024,1536]{1,0:T(8,128)(2,1)S(1)}) custom-call(bf16[256,2048]{1,0:T(8,128)(2,1)S(1)} %get-tuple-element.208.mine_ref, bf16[256,2048]{1,0:T(8,128)(2,1)S(1)} %pad_maximum_fusion.6.other_ref, bf16[2048,1536]{1,0:T(8,128)(2,1)} %refs_1_.9, ...), custom_call_target="tpu_custom_call" | custom-call | tf_op jit(solution)/shard_map/feed/pallas_call | solution.py:275
  94.4 11.5 %feed.3 = (bf16[1024,2048]{1,0:T(8,128)(2,1)}, bf16[1024,1536]{1,0:T(8,128)(2,1)S(1)}, bf16[1024,1536]{1,0:T(8,128)(2,1)S(1)}, bf16[1024,1536]{1,0:T(8,128)(2,1)S(1)}) custom-call(bf16[256,2048]{1,0:T(8,128)(2,1)S(1)} %copy-done.46, ...), custom_call_target="tpu_custom_call", output_to_operand_aliasing={{0}: (5, {}), {1}: (6, {}), {2}: (7, {}), {3}: (8, {})} | custom-call | tf_op jit(solution)/shard_map/feed/pallas_call | solution.py:275
  107.6 12.5 %weight_grad.4.refs_1_.refs_3_ = bf16[2048,1536]{1,0:T(8,128)(2,1)S(1)} custom-call(bf16[1024,2048]{1,0:T(8,128)(2,1)} %copy-done.4, bf16[1024,1536]{1,0:T(8,128)(2,1)} %copy-done.12), custom_call_target="tpu_custom_call" | custom-call | tf_op jit(solution)/shard_map/weight_grad/pallas_call | solution.py:652
  126.6 10.9 %pairs.8 = (f32[512,2048]{1,0:T(8,128)S(1)}, bf16[512,2048]{1,0:T(8,128)(2,1)S(1)}) custom-call(s32[1]{0:T(128)} %bitcast.core_ref.refs_0_, bf16[1024,1536]{1,0:T(8,128)(2,1)} %copy-done.6, bf16[2048,1536]{1,0:T(8,128)(2,1)} %refs_1_.9, bf16[1024,1536]{1,0:T(8,128)(2,1)} %copy-done.9, bf16[2048,1536]{1,0:T(8,128)(2,1)} %refs_3_.4), custom_call_target="tpu_custom_call" | custom-call | tf_op jit(solution)/shard_map/pairs/pallas_call | solution.py:576
  141.4 10.9 %pairs.9 = (f32[512,2048]{1,0:T(8,128)S(1)}, bf16[512,2048]{1,0:T(8,128)(2,1)S(1)}) custom-call(s32[1]{0:T(128)} %bitcast.core_ref.refs_0_, bf16[1024,1536]{1,0:T(8,128)(2,1)} %copy-done.6, bf16[2048,1536]{1,0:T(8,128)(2,1)} %refs_1_.9, bf16[1024,1536]{1,0:T(8,128)(2,1)} %copy-done.9, ...), custom_call_target="tpu_custom_call", output_to_operand_aliasing={{0}: (5, {}), {1}: (6, {})} | custom-call | tf_op jit(solution)/shard_map/pairs/pallas_call | solution.py:576
  156.4 10.3 %weight_grad.5.refs_1_.refs_3_ = bf16[2048,1536]{1,0:T(8,128)(2,1)S(1)} custom-call(bf16[1024,2048]{1,0:T(8,128)(2,1)} %get-tuple-element.219.refs_0_, bf16[1024,1536]{1,0:T(8,128)(2,1)} %copy-done.6), custom_call_target="tpu_custom_call" | custom-call | tf_op jit(solution)/shard_map/weight_grad/pallas_call | solution.py:652
  176.4 10.7 %weight_grad.6.refs_1_.refs_3_ = bf16[2048,1536]{1,0:T(8,128)(2,1)S(1)} custom-call(bf16[1024,2048]{1,0:T(8,128)(2,1)} %get-tuple-element.219.refs_0_, bf16[1024,1536]{1,0:T(8,128)(2,1)} %copy-done.9), custom_call_target="tpu_custom_call" | custom-call | tf_op jit(solution)/shard_map/weight_grad/pallas_call | solution.py:652
  196.4 10.0 %pairs.10 = (f32[512,2048]{1,0:T(8,128)S(1)}, bf16[512,2048]{1,0:T(8,128)(2,1)S(1)}) custom-call(s32[1]{0:T(128)} %bitcast.core_ref.refs_0_, bf16[1024,1536]{1,0:T(8,128)(2,1)} %copy-done.12, bf16[1536,2048]{1,0:T(8,128)(2,1)} %refs_1_.10), custom_call_target="tpu_custom_call" | custom-call | tf_op jit(solution)/shard_map/pairs/pallas_call | solution.py:576
  215.6 4.8 collective-permute-done.35.refs_1_
  238.6 7.9 %collective-permute-done.40.refs_1_ = bf16[256,768]{1,0:T(8,128)(2,1)S(1)} collective-permute-done((bf16[256,768]{1,0:T(8,128)(2,1)S(1)}, bf16[256,768]{1,0:T(8,128)(2,1)S(1)}, u32[]{:S(2)}, u32[]{:S(2)}) %collective-permute-start.40) | collective-permute-done | bytes 393248 | tf_op jit(solution)/shard_map/ppermute | solution.py:530
  273.1 9.0 %attend_back.2 = (bf16[1024,512]{1,0:T(8,128)(2,1)S(1)}, bf16[1024,256]{1,0:T(8,128)(2,1)S(1)}, bf16[1024,256]{1,0:T(8,128)(2,1)S(1)}, f32[8,128]{1,0:T(8,128)S(1)}) custom-call(s32[1]{0:T(128)} %bitcast.core_ref.refs_0_, bf16[1024,512]{1,0:T(8,128)(2,1)S(1)} %times_turned.3.refs_1_, bf16[1024,512]{1,0:T(8,128)(2,1)} %get-tuple-element.198.q_ref.refs_2_, ...), custom_call_target="tpu_custom_call" | custom-call | tf_op jit(solution)/shard_map/attend_back/pallas_call | solution.py:221
  295.0 9.0 %attend_back.3 = (bf16[1024,512]{1,0:T(8,128)(2,1)S(1)}, bf16[1024,256]{1,0:T(8,128)(2,1)S(1)}, bf16[1024,256]{1,0:T(8,128)(2,1)S(1)}, f32[8,128]{1,0:T(8,128)S(1)}) custom-call(s32[1]{0:T(128)} %bitcast.core_ref.refs_0_, bf16[1024,512]{1,0:T(8,128)(2,1)S(1)} %times_turned.3.refs_1_, ...), custom_call_target="tpu_custom_call", output_to_operand_aliasing={{0}: (15, {}), {1}: (16, {}), {2}: (17, {})} | custom-call | tf_op jit(solution)/shard_map/attend_back/pallas_call | solution.py:221
  314.6 11.4 %weight_grad.7.refs_1_.refs_3_ = bf16[2048,1536]{1,0:T(8,128)(2,1)S(1)} custom-call(bf16[256,2048]{1,0:T(8,128)(2,1)} %copy-done.25, bf16[256,2048]{1,0:T(8,128)(2,1)} %copy-done.27, bf16[256,2048]{1,0:T(8,128)(2,1)} %copy-done.24, bf16[256,2048]{1,0:T(8,128)(2,1)} %copy-done.26, bf16[1024,512]{1,0:T(8,128)(2,1)} %maximum_select_fusion.refs_4_, ...), custom_call_target="tpu_custom_call" | custom-call | tf_op jit(solution)/shard_map/weight_grad/pallas_call | solution.py:652
  328.7 7.5 %pairs.11 = (f32[512,2048]{1,0:T(8,128)S(1)}, bf16[512,2048]{1,0:T(8,128)(2,1)S(1)}) custom-call(s32[1]{0:T(128)} %bitcast.core_ref.refs_0_, bf16[1024,512]{1,0:T(8,128)(2,1)} %copy-done.17, bf16[2048,512]{1,0:T(8,128)(2,1)} %refs_1_.11, bf16[1024,256]{1,0:T(8,128)(2,1)} %copy-done.37, bf16[2048,256]{1,0:T(8,128)(2,1)} %refs_3_.5, ...), custom_call_target="tpu_custom_call" | custom-call | tf_op jit(solution)/shard_map/pairs/pallas_call | solution.py:576
  351.2 7.9 %collective-permute-done.58.refs_1_ = bf16[256,768]{1,0:T(8,128)(2,1)S(1)} collective-permute-done((bf16[256,768]{1,0:T(8,128)(2,1)S(1)}, bf16[256,768]{1,0:T(8,128)(2,1)S(1)}, u32[]{:S(2)}, u32[]{:S(2)}) %collective-permute-start.58) | collective-permute-done | bytes 393248 | tf_op jit(solution)/shard_map/ppermute | solution.py:530
  362.6 4.5 collective-permute-done.57.refs_1_
  378.3 5.3 %collective-permute-done.63.refs_1_ = bf16[256,768]{1,0:T(8,128)(2,1)S(1)} collective-permute-done((bf16[256,768]{1,0:T(8,128)(2,1)S(1)}, bf16[256,768]{1,0:T(8,128)(2,1)S(1)}, u32[]{:S(2)}, u32[]{:S(2)}) %collective-permute-start.63) | collective-permute-done | bytes 393248 | tf_op jit(solution)/shard_map/ppermute | solution.py:530
  387.1 5.0 %collective-permute-done.62.refs_1_ = bf16[256,768]{1,0:T(8,128)(2,1)S(1)} collective-permute-done((bf16[256,768]{1,0:T(8,128)(2,1)S(1)}, bf16[256,768]{1,0:T(8,128)(2,1)S(1)}, u32[]{:S(2)}, u32[]{:S(2)}) %collective-permute-start.62) | collective-permute-done | bytes 393248 | tf_op jit(solution)/shard_map/ppermute | solution.py:530
  432.4 9.4 %collective-permute-done.75.refs_1_ = bf16[256,768]{1,0:T(8,128)(2,1)S(1)} collective-permute-done((bf16[256,768]{1,0:T(8,128)(2,1)S(1)}, bf16[256,768]{1,0:T(8,128)(2,1)S(1)}, u32[]{:S(2)}, u32[]{:S(2)}) %collective-permute-start.75) | collective-permute-done | bytes 393248 | tf_op jit(solution)/shard_map/ppermute | solution.py:530
  460.6 6.3 %collective-permute-done.79 = f32[4352]{0:T(1024)S(1)} collective-permute-done((f32[4352]{0:T(1024)S(1)}, f32[4352]{0:T(1024)S(1)}, u32[]{:S(2)}, u32[]{:S(2)}) %collective-permute-start.79) | collective-permute-done | bytes 17440 | tf_op jit(solution)/shard_map/ppermute | solution.py:710
  (388 shorter events, 274.1 us)
Async XLA Ops:
  29.1 33.6 %collective-permute-start.4 = (bf16[256,2048]{1,0:T(8,128)(2,1)S(1)}, bf16[256,2048]{1,0:T(8,128)(2,1)S(1)}, u32[]{:S(2)}, u32[]{:S(2)}) collective-permute-start(bf16[256,2048]{1,0:T(8,128)(2,1)S(1)} %near_add.5.near_ref), channel_id=1, source_target_pairs={{0,2},{1,3},{2,0},{3,1},{4,6},{5,7},{6,4},{7,5},{8,10},{9,11},{10,... | collective-permute-start | bytes 3145736 | tf_op jit(solution)/shard_map/ppermute | solution.py:700
  49.5 31.5 %collective-permute-start.9 = (bf16[256,2048]{1,0:T(8,128)(2,1)S(1)}, bf16[256,2048]{1,0:T(8,128)(2,1)}, u32[]{:S(2)}, u32[]{:S(2)}) collective-permute-start(bf16[256,2048]{1,0:T(8,128)(2,1)S(1)} %near_add.6.near_ref), channel_id=1, source_target_pairs={{0,2},{1,3},{2,0},{3,1},{4,6},{5,7},{6,4},{7,5},{8,10},{9,11},{10,... | collective-permute-start | bytes 3145736 | tf_op jit(solution)/shard_map/ppermute | solution.py:700
  170.0 58.2 %collective-permute-start.29 = (bf16[512,2048]{1,0:T(8,128)(2,1)S(1)}, bf16[512,2048]{1,0:T(8,128)(2,1)S(1)}, u32[]{:S(2)}, u32[]{:S(2)}) collective-permute-start(bf16[512,2048]{1,0:T(8,128)(2,1)S(1)} %near_add.7.near_ref), channel_id=1, source_target_pairs={{0,2},{1,3},{2,0},{3,1},{4,6},{5,7},{6,4},{7,5},{8,10},{9,11},{10,... | collective-permute-start | bytes 6291464 | tf_op jit(solution)/shard_map/ppermute | solution.py:700
  234.5 24.9 %collective-permute-start.38 = (bf16[1024,2048]{1,0:T(8,128)(2,1)S(1)}, bf16[1024,2048]{1,0:T(8,128)(2,1)S(1)}, u32[]{:S(2)}, u32[]{:S(2)}) collective-permute-start(bf16[1024,2048]{1,0:T(8,128)(2,1)S(1)} %pad_maximum_fusion), channel_id=1, source_target_pairs={{0,1},{1,0},{2,3},{3,2},{4,5},{5,4},{6,7},{7,6},{8,9},{9,8},{10,11... | collective-permute-start | bytes 12582920 | tf_op jit(solution)/shard_map/ppermute | solution.py:695
  236.5 17.9 %collective-permute-start.39 = (bf16[256,768]{1,0:T(8,128)(2,1)S(1)}, bf16[256,768]{1,0:T(8,128)(2,1)S(1)}, u32[]{:S(2)}, u32[]{:S(2)}) collective-permute-start(bf16[256,768]{1,0:T(8,128)(2,1)S(1)} %get-tuple-element.265), channel_id=1, source_target_pairs={{0,8},{8,16},{16,24},{24,28},{28,20},{20,12},{12,4},{4,0},{1,9},{9... | collective-permute-start | bytes 1179656 | tf_op jit(solution)/shard_map/ppermute | solution.py:530
  238.1 17.6 %collective-permute-start.42 = (bf16[256,768]{1,0:T(8,128)(2,1)S(1)}, bf16[256,768]{1,0:T(8,128)(2,1)S(1)}, u32[]{:S(2)}, u32[]{:S(2)}) collective-permute-start(bf16[256,768]{1,0:T(8,128)(2,1)S(1)} %get-tuple-element.274), channel_id=1, source_target_pairs={{8,0},{16,8},{24,16},{28,24},{20,28},{12,20},{4,12},{0,4},{9,1},{1... | collective-permute-start | bytes 1179656 | tf_op jit(solution)/shard_map/ppermute | solution.py:530
  261.6 81.5 %collective-permute-start.43 = (bf16[512,2048]{1,0:T(8,128)(2,1)}, bf16[512,2048]{1,0:T(8,128)(2,1)}, u32[]{:S(2)}, u32[]{:S(2)}) collective-permute-start(bf16[512,2048]{1,0:T(8,128)(2,1)} %near_add.8.near_ref), channel_id=1, source_target_pairs={{0,2},{1,3},{2,0},{3,1},{4,6},{5,7},{6,4},{7,5},{8,10},{9,11},{10,... | collective-permute-start | bytes 6291464 | tf_op jit(solution)/shard_map/ppermute | solution.py:700
  263.1 19.0 %collective-permute-start.45 = (bf16[256,768]{1,0:T(8,128)(2,1)S(1)}, bf16[256,768]{1,0:T(8,128)(2,1)S(1)}, u32[]{:S(2)}, u32[]{:S(2)}) collective-permute-start(bf16[256,768]{1,0:T(8,128)(2,1)S(1)} %get-tuple-element.275), channel_id=1, source_target_pairs={{0,8},{8,16},{16,24},{24,28},{28,20},{20,12},{12,4},{4,0},{1,9},{9... | collective-permute-start | bytes 1179656 | tf_op jit(solution)/shard_map/ppermute | solution.py:530
  264.7 21.8 %collective-permute-start.44 = (bf16[256,768]{1,0:T(8,128)(2,1)S(1)}, bf16[256,768]{1,0:T(8,128)(2,1)S(1)}, u32[]{:S(2)}, u32[]{:S(2)}) collective-permute-start(bf16[256,768]{1,0:T(8,128)(2,1)S(1)} %get-tuple-element.277), channel_id=1, source_target_pairs={{0,8},{8,16},{16,24},{24,28},{28,20},{20,12},{12,4},{4,0},{1,9},{9... | collective-permute-start | bytes 1179656 | tf_op jit(solution)/shard_map/ppermute | solution.py:530
  266.7 20.2 %collective-permute-start.47 = (bf16[256,768]{1,0:T(8,128)(2,1)S(1)}, bf16[256,768]{1,0:T(8,128)(2,1)S(1)}, u32[]{:S(2)}, u32[]{:S(2)}) collective-permute-start(bf16[256,768]{1,0:T(8,128)(2,1)S(1)} %get-tuple-element.292), channel_id=1, source_target_pairs={{8,0},{16,8},{24,16},{28,24},{20,28},{12,20},{4,12},{0,4},{9,1},{1... | collective-permute-start | bytes 1179656 | tf_op jit(solution)/shard_map/ppermute | solution.py:530
  284.8 19.2 %collective-permute-start.49 = (bf16[256,768]{1,0:T(8,128)(2,1)}, bf16[256,768]{1,0:T(8,128)(2,1)S(1)}, u32[]{:S(2)}, u32[]{:S(2)}) collective-permute-start(bf16[256,768]{1,0:T(8,128)(2,1)} %get-tuple-element.290), channel_id=1, source_target_pairs={{0,8},{8,16},{16,24},{24,28},{28,20},{20,12},{12,4},{4,0},{1,9},{9... | collective-permute-start | bytes 1179656 | tf_op jit(solution)/shard_map/ppermute | solution.py:530
  289.6 18.8 %collective-permute-start.48 = (bf16[256,768]{1,0:T(8,128)(2,1)}, bf16[256,768]{1,0:T(8,128)(2,1)}, u32[]{:S(2)}, u32[]{:S(2)}) collective-permute-start(bf16[256,768]{1,0:T(8,128)(2,1)} %get-tuple-element.293), channel_id=1, source_target_pairs={{0,8},{8,16},{16,24},{24,28},{28,20},{20,12},{12,4},{4,0},{1,9},{9... | collective-permute-start | bytes 1179656 | tf_op jit(solution)/shard_map/ppermute | solution.py:530
  306.7 29.6 %collective-permute-start.53 = (bf16[256,768]{1,0:T(8,128)(2,1)S(1)}, bf16[256,768]{1,0:T(8,128)(2,1)S(1)}, u32[]{:S(2)}, u32[]{:S(2)}) collective-permute-start(bf16[256,768]{1,0:T(8,128)(2,1)S(1)} %get-tuple-element.300), channel_id=1, source_target_pairs={{0,8},{8,16},{16,24},{24,28},{28,20},{20,12},{12,4},{4,0},{1,9},{9... | collective-permute-start | bytes 1179656 | tf_op jit(solution)/shard_map/ppermute | solution.py:530
  308.4 27.9 %collective-permute-start.54 = (bf16[256,768]{1,0:T(8,128)(2,1)S(1)}, bf16[256,768]{1,0:T(8,128)(2,1)S(1)}, u32[]{:S(2)}, u32[]{:S(2)}) collective-permute-start(bf16[256,768]{1,0:T(8,128)(2,1)S(1)} %get-tuple-element.310), channel_id=1, source_target_pairs={{8,0},{16,8},{24,16},{28,24},{20,28},{12,20},{4,12},{0,4},{9,1},{1... | collective-permute-start | bytes 1179656 | tf_op jit(solution)/shard_map/ppermute | solution.py:530
  311.2 28.0 %collective-permute-start.52 = (bf16[256,768]{1,0:T(8,128)(2,1)S(1)}, bf16[256,768]{1,0:T(8,128)(2,1)S(1)}, u32[]{:S(2)}, u32[]{:S(2)}) collective-permute-start(bf16[256,768]{1,0:T(8,128)(2,1)S(1)} %get-tuple-element.303), channel_id=1, source_target_pairs={{0,8},{8,16},{16,24},{24,28},{28,20},{20,12},{12,4},{4,0},{1,9},{9... | collective-permute-start | bytes 1179656 | tf_op jit(solution)/shard_map/ppermute | solution.py:530
  312.9 26.4 %collective-permute-start.55 = (bf16[256,768]{1,0:T(8,128)(2,1)S(1)}, bf16[256,768]{1,0:T(8,128)(2,1)S(1)}, u32[]{:S(2)}, u32[]{:S(2)}) collective-permute-start(bf16[256,768]{1,0:T(8,128)(2,1)S(1)} %get-tuple-element.312), channel_id=1, source_target_pairs={{8,0},{16,8},{24,16},{28,24},{20,28},{12,20},{4,12},{0,4},{9,1},{1... | collective-permute-start | bytes 1179656 | tf_op jit(solution)/shard_map/ppermute | solution.py:530
  347.0 23.2 %collective-permute-start.56 = (bf16[1024,2048]{1,0:T(8,128)(2,1)S(1)}, bf16[1024,2048]{1,0:T(8,128)(2,1)S(1)}, u32[]{:S(2)}, u32[]{:S(2)}) collective-permute-start(bf16[1024,2048]{1,0:T(8,128)(2,1)S(1)} %pad_maximum_fusion.1), channel_id=1, source_target_pairs={{0,1},{1,0},{2,3},{3,2},{4,5},{5,4},{6,7},{7,6},{8,9},{9,8},{10,11... | collective-permute-start | bytes 12582920 | tf_op jit(solution)/shard_map/ppermute | solution.py:695
  349.2 17.9 %collective-permute-start.57 = (bf16[256,768]{1,0:T(8,128)(2,1)S(1)}, bf16[256,768]{1,0:T(8,128)(2,1)S(1)}, u32[]{:S(2)}, u32[]{:S(2)}) collective-permute-start(bf16[256,768]{1,0:T(8,128)(2,1)S(1)} %get-tuple-element.315), channel_id=1, source_target_pairs={{0,8},{8,16},{16,24},{24,28},{28,20},{20,12},{12,4},{4,0},{1,9},{9... | collective-permute-start | bytes 1179656 | tf_op jit(solution)/shard_map/ppermute | solution.py:530
  371.0 55.6 %collective-permute-start.61 = (bf16[512,2048]{1,0:T(8,128)(2,1)S(1)}, bf16[512,2048]{1,0:T(8,128)(2,1)S(1)}, u32[]{:S(2)}, u32[]{:S(2)}) collective-permute-start(bf16[512,2048]{1,0:T(8,128)(2,1)S(1)} %near_add.9.near_ref), channel_id=1, source_target_pairs={{0,2},{1,3},{2,0},{3,1},{4,6},{5,7},{6,4},{7,5},{8,10},{9,11},{10,... | collective-permute-start | bytes 6291464 | tf_op jit(solution)/shard_map/ppermute | solution.py:700
  373.6 18.5 %collective-permute-start.62 = (bf16[256,768]{1,0:T(8,128)(2,1)S(1)}, bf16[256,768]{1,0:T(8,128)(2,1)S(1)}, u32[]{:S(2)}, u32[]{:S(2)}) collective-permute-start(bf16[256,768]{1,0:T(8,128)(2,1)S(1)} %get-tuple-element.324), channel_id=1, source_target_pairs={{0,8},{8,16},{16,24},{24,28},{28,20},{20,12},{12,4},{4,0},{1,9},{9... | collective-permute-start | bytes 1179656 | tf_op jit(solution)/shard_map/ppermute | solution.py:530
  374.8 17.7 %collective-permute-start.65 = (bf16[256,768]{1,0:T(8,128)(2,1)S(1)}, bf16[256,768]{1,0:T(8,128)(2,1)S(1)}, u32[]{:S(2)}, u32[]{:S(2)}) collective-permute-start(bf16[256,768]{1,0:T(8,128)(2,1)S(1)} %get-tuple-element.331), channel_id=1, source_target_pairs={{8,0},{16,8},{24,16},{28,24},{20,28},{12,20},{4,12},{0,4},{9,1},{1... | collective-permute-start | bytes 1179656 | tf_op jit(solution)/shard_map/ppermute | solution.py:530
  430.2 19.9 %collective-permute-start.74 = (bf16[512,2048]{1,0:T(8,128)(2,1)S(1)}, bf16[512,2048]{1,0:T(8,128)(2,1)S(1)}, u32[]{:S(2)}, u32[]{:S(2)}) collective-permute-start(bf16[512,2048]{1,0:T(8,128)(2,1)S(1)} %get-tuple-element.345.mine_ref), channel_id=1, source_target_pairs={{0,1},{1,0},{2,3},{3,2},{4,5},{5,4},{6,7},{7,6},{8,9},{9,8},{10,11... | collective-permute-start | bytes 6291464 | tf_op jit(solution)/shard_map/ppermute | solution.py:695
  457.3 19.4 %collective-permute-start.84 = (bf16[256,768]{1,0:T(8,128)(2,1)S(1)}, bf16[256,768]{1,0:T(8,128)(2,1)S(1)}, u32[]{:S(2)}, u32[]{:S(2)}) collective-permute-start(bf16[256,768]{1,0:T(8,128)(2,1)S(1)} %get-tuple-element.356), channel_id=1, source_target_pairs={{0,8},{8,16},{16,24},{24,28},{28,20},{20,12},{12,4},{4,0},{1,9},{9... | collective-permute-start | bytes 1179656 | tf_op jit(solution)/shard_map/ppermute | solution.py:530
  457.9 18.7 %collective-permute-start.85 = (bf16[256,768]{1,0:T(8,128)(2,1)S(1)}, bf16[256,768]{1,0:T(8,128)(2,1)S(1)}, u32[]{:S(2)}, u32[]{:S(2)}) collective-permute-start(bf16[256,768]{1,0:T(8,128)(2,1)S(1)} %get-tuple-element.358), channel_id=1, source_target_pairs={{8,0},{16,8},{24,16},{28,24},{20,28},{12,20},{4,12},{0,4},{9,1},{1... | collective-permute-start | bytes 1179656 | tf_op jit(solution)/shard_map/ppermute | solution.py:530
  (129 other events, 887.4 us)

commit v3 on v2

--- a/solution.py
+++ b/solution.py
@@ -95,7 +95,10 @@
         compiler_params=pltpu.CompilerParams(vmem_limit_bytes=40 * MIB),
         cost_estimate=COST,
         name="front",
-    )(tokens, gain[None, :], wq, wk, wv, cosine, sine, q_gain[None, :], k_gain[None, :])
+    )(
+        hbm(tokens), gain[None, :], hbm(wq), hbm(wk), hbm(wv), cosine, sine, q_gain[None, :],
+        k_gain[None, :],
+    )
 
 
 def pair_rows(value, size):
@@ -246,9 +249,10 @@
     )
 
 
-def feed_kernel(mine_ref, other_ref, wg_ref, wu_ref, dh_ref, *refs):
+def feed_kernel(count, *refs):
+    lefts, (wg_ref, wu_ref, dh_ref) = refs[:count], refs[count : count + 3]
     inner_ref, hidden_ref, dg_ref, du_ref = refs[-4:]
-    inner = jnp.concatenate([mine_ref[...], other_ref[...]], 0)
+    inner = jnp.concatenate([ref[...] for ref in lefts], 0)
 
     @pl.when(pl.program_id(0) == 0)
     def _():
@@ -264,26 +268,27 @@
     dg_ref[...] = (d_hidden * up * (sig + silu * (1.0 - sig))).astype(jnp.bfloat16)
 
 
-def feed(mine, other, w_gate, w_up, d_hidden, part, before, cols=512):
-    rows, width = mine.shape
+def feed(first, others, w_gate, w_up, d_hidden, part, before, cols=768):
+    lefts = [first, *others]
+    rows, width = sum(left.shape[0] for left in lefts), first.shape[1]
     count, units = d_hidden.shape
-    here = pl.BlockSpec((2 * rows, width), lambda j: (part, 0))
-    block = pl.BlockSpec((2 * rows, cols), lambda j: (part, j))
+    here = pl.BlockSpec((rows, width), lambda j: (part, 0))
+    block = pl.BlockSpec((rows, cols), lambda j: (part, j))
     weight = pl.BlockSpec((width, cols), lambda j: (0, j))
-    half = pl.BlockSpec((rows, width), lambda j: (0, 0))
-    out = jax.ShapeDtypeStruct((count, units), jnp.bfloat16)
-    return pl.pallas_call(
-        feed_kernel,
+    out = pltpu.HBM((count, units), jnp.bfloat16)
+    return pl.pallas_call(
+        functools.partial(feed_kernel, len(lefts)),
         grid=(units // cols,),
-        in_specs=[half, half, weight, weight, block]
+        in_specs=[pl.BlockSpec(left.shape, lambda j: (0, 0)) for left in lefts]
+        + [weight, weight, block]
         + [pl.BlockSpec(memory_space=pl.ANY)] * len(before),
         out_specs=[here, block, block, block],
-        out_shape=[jax.ShapeDtypeStruct((count, width), jnp.bfloat16), out, out, out],
-        input_output_aliases={5 + i: i for i in range(len(before))},
+        out_shape=[pltpu.HBM((count, width), jnp.bfloat16), out, out, out],
+        input_output_aliases={len(lefts) + 3 + i: i for i in range(len(before))},
         compiler_params=pltpu.CompilerParams(vmem_limit_bytes=40 * MIB),
         cost_estimate=COST,
         name="feed",
-    )(mine, other, w_gate, w_up, d_hidden, *before)
+    )(*lefts, hbm(w_gate), hbm(w_up), hbm(d_hidden), *[hbm(array) for array in before])
 
 
 ROWS = 128
@@ -311,41 +316,56 @@
     return ref[...].astype(jnp.float32)
 
 
-def settle_kernel(x_ref, near_ref, far_ref, gain_ref, resid_ref, inner_ref):
+def settle_kernel(x_ref, near_ref, far_ref, gain_ref, resid_ref, *inner_refs):
     resid = wide(x_ref) + (wide(near_ref) + wide(far_ref))
     resid_ref[...] = resid
     factor = lax.rsqrt(row_mean(resid * resid) + EPS)
-    inner_ref[...] = (resid * factor * gain_ref[...]).astype(jnp.bfloat16)
+    inner = (resid * factor * gain_ref[...]).astype(jnp.bfloat16)
+    for j, inner_ref in enumerate(inner_refs):
+
+        @pl.when(pl.program_id(0) == j)
+        def _():
+            inner_ref[...] = inner
 
 
 def settle(x, near, far, gain):
     rows, width = x.shape
-    return rows_call(
-        settle_kernel, "settle", rows, (x, near, far, gain[None, :]),
-        [jax.ShapeDtypeStruct((rows, width), jnp.float32), jax.ShapeDtypeStruct((rows, width), jnp.bfloat16)],
-    )
+    pieces = rows // ROWS
+    block = pl.BlockSpec((ROWS, width), lambda i: (i, 0))
+    return pl.pallas_call(
+        settle_kernel,
+        grid=(pieces,),
+        in_specs=[block, block, block, pl.BlockSpec((1, width), lambda i: (0, 0))],
+        out_specs=[block] + [pl.BlockSpec((ROWS, width), lambda i: (0, 0))] * pieces,
+        out_shape=[jax.ShapeDtypeStruct((rows, width), jnp.float32)]
+        + [jax.ShapeDtypeStruct((ROWS, width), jnp.bfloat16)] * pieces,
+        compiler_params=pltpu.CompilerParams(vmem_limit_bytes=24 * MIB),
+        cost_estimate=COST,
+        name="settle",
+    )(x, near, far, gain[None, :])
 
 
 def unsettle_kernel(near_ref, far_ref, resid_ref, grad_ref, gain_ref, out_ref, low_ref, sum_ref):
-    @pl.when(pl.program_id(0) == 0)
-    def _():
-        sum_ref[...] = jnp.zeros_like(sum_ref)
-
     resid = resid_ref[...].astype(jnp.float32)
     factor = lax.rsqrt(row_mean(resid * resid) + EPS)
     hat = resid * factor
     d_inner = wide(near_ref) + wide(far_ref)
     both = d_inner * hat
-    sum_ref[0:1, :] += jnp.sum(both, 0, keepdims=True)
     scaled = d_inner * gain_ref[...]
     back = wide(grad_ref) + factor * (scaled - hat * row_mean(both * gain_ref[...]))
     out_ref[...] = back.astype(out_ref.dtype)
     if low_ref is not None:
         low_ref[...] = back.astype(jnp.bfloat16)
 
-
-def last_kernel(near_ref, far_ref, resid_ref, grad_ref, gain_ref, out_ref, sum_ref):
-    unsettle_kernel(near_ref, far_ref, resid_ref, grad_ref, gain_ref, out_ref, None, sum_ref)
+        @pl.when(pl.program_id(0) == 0)
+        def _():
+            sum_ref[...] = jnp.zeros_like(sum_ref)
+
+        sum_ref[0:1, :] += jnp.sum(both, 0, keepdims=True)
+
+
+def last_kernel(near_ref, far_ref, resid_ref, grad_ref, gain_ref, out_ref):
+    unsettle_kernel(near_ref, far_ref, resid_ref, grad_ref, gain_ref, out_ref, None, None)
 
 
 def unsettle(near, far, resid, grad, gain):
@@ -364,8 +384,8 @@
     rows, width = near.shape
     return rows_call(
         last_kernel, "unsettle_last", rows, (near, far, resid, grad, gain[None, :]),
-        [jax.ShapeDtypeStruct((rows, width), jnp.bfloat16), jax.ShapeDtypeStruct((8, width), jnp.float32)],
-    )
+        [jax.ShapeDtypeStruct((rows, width), jnp.bfloat16)],
+    )[0]
 
 
 def live_rows_kernel(core_ref, value_ref, seg_ref, out_ref):
@@ -412,80 +432,172 @@
     return jnp.asarray(np.array(table, np.int32).reshape(n, 2 * n))[lax.axis_index("dp")]
 
 
-def ring_kernel(finish, step, *refs):
-    where_ref, part_ref = refs[0], refs[-4]
-    own_a, own_b, sem = refs[-3:]
-    size, half = own_a.shape
-    copies = []
-    for side, own in enumerate((own_a, own_b)):
-        begin = pl.multiple_of(where_ref[2 * step + side] * size, size)
-        piece = part_ref.at[pl.ds(begin, size), pl.ds(side * half, half)]
-        copies.append(pltpu.make_async_copy(piece, own, sem.at[side]))
-    for copy in copies:
-        copy.start()
-    for copy in copies:
-        copy.wait()
-    finish(own_a, own_b, *refs[1:-4])
-
-
-def ring_first(own_a, own_b, out_a_ref, out_b_ref):
-    out_a_ref[...] = own_a[...]
-    out_b_ref[...] = own_b[...]
-
-
-def ring_add(own_a, own_b, came_a_ref, came_b_ref, out_a_ref, out_b_ref):
-    out_a_ref[...] = (wide(came_a_ref) + wide(own_a)).astype(jnp.bfloat16)
-    out_b_ref[...] = (wide(came_b_ref) + wide(own_b)).astype(jnp.bfloat16)
-
-
-def ring_last(own_a, own_b, came_a_ref, came_b_ref, out_ref):
-    half = own_a.shape[1]
-    out_ref[:, :half] = wide(came_a_ref) + wide(own_a)
-    out_ref[:, half:] = wide(came_b_ref) + wide(own_b)
-
-
-def ring_last_turned(own_a, own_b, came_a_ref, came_b_ref, out_ref):
-    half = own_a.shape[1]
-    out_ref[:half, :] = (wide(came_a_ref) + wide(own_a)).T
-    out_ref[half:, :] = (wide(came_b_ref) + wide(own_b)).T
-
-
-def ring_last_lin(own_a, own_b, came_a_ref, came_b_ref, out_ref, q_ref, k_ref, v_ref):
-    whole = jnp.concatenate([wide(came_a_ref) + wide(own_a), wide(came_b_ref) + wide(own_b)], 1)
-    begin = 0
-    for ref in (out_ref, q_ref, k_ref, v_ref):
-        width = ref.shape[0] if ref is out_ref else ref.shape[1]
-        part = whole[:, begin : begin + width]
-        ref[...] = part.T if ref is out_ref else part
+def ring_first(value_a, value_b, out_a_ref, out_b_ref):
+    out_a_ref[...] = value_a.astype(jnp.bfloat16)
+    out_b_ref[...] = value_b.astype(jnp.bfloat16)
+
+
+def ring_last(turned, value_a, value_b, *out_refs):
+    whole = jnp.concatenate([value_a, value_b], 1)
+    begin, rows = 0, out_refs[0].shape[1 if turned[0] else 0]
+    for flag, ref in zip(turned, out_refs):
+        width = ref.shape[0] if flag else ref.shape[1]
+        part = whole[:rows, begin : begin + width]
+        ref[...] = part.T if flag else part
         begin += width
-
-
-def ring_call(finish, n, where, step, came, part, out_shape):
-    size, half = part.shape[0] // n, part.shape[1] // 2
-
-    def kernel(*refs):
-        outs = len(jax.tree.leaves(out_shape))
-        ins = 1 + len(came)
-        ring_kernel(
-            finish, step, *refs[:ins], *refs[ins + 1 : ins + 1 + outs], refs[ins], *refs[ins + 1 + outs :]
-        )
+    if len(out_refs) > len(turned):
+        out_refs[-1][...] = whole[rows:, :]
+
+
+def ring_sum_call(finish, name, came, part, out_shape):
+    def kernel(came_a_ref, came_b_ref, a_ref, b_ref, *out_refs):
+        finish(wide(came_a_ref) + wide(a_ref), wide(came_b_ref) + wide(b_ref), *out_refs)
+
+    vmem = pl.BlockSpec(memory_space=pltpu.VMEM)
+    return pl.pallas_call(
+        kernel,
+        in_specs=[vmem] * 4,
+        out_specs=jax.tree.map(lambda o: vmem, out_shape),
+        out_shape=out_shape,
+        compiler_params=pltpu.CompilerParams(vmem_limit_bytes=16 * MIB),
+        cost_estimate=COST,
+        name=name,
+    )(*came, *part)
+
+
+EXTRA = 16
+
+
+def ring_call(finish, name, n, where, step, came, source, out_shape):
+    sizes, half = [part.shape[0] // n for part in source], source[0].shape[1] // 2
+    outs = len(jax.tree.leaves(out_shape))
+
+    def kernel(where_ref, *refs):
+        came_refs, part_refs = refs[: len(came)], refs[len(came) :][: len(source)]
+        out_refs, owns, sem = refs[len(came) + len(source) :][:outs], refs[-3:-1], refs[-1]
+        copies = []
+        for side, own in enumerate(owns):
+            row = 0
+            for size, part_ref in zip(sizes, part_refs):
+                begin = pl.multiple_of(where_ref[2 * step + side] * size, size)
+                copies.append(
+                    pltpu.make_async_copy(
+                        part_ref.at[pl.ds(begin, size), pl.ds(side * half, half)],
+                        own.at[pl.ds(row, size), :],
+                        sem.at[len(copies)],
+                    )
+                )
+                row += size
+        for copy in copies:
+            copy.start()
+        for copy in copies:
+            copy.wait()
+        values = [wide(own) for own in owns]
+        if came:
+            values = [value + wide(ref) for value, ref in zip(values, came_refs)]
+        finish(*values, *out_refs)
 
     return pl.pallas_call(
         kernel,
         in_specs=[pl.BlockSpec(memory_space=pltpu.SMEM)]
         + [pl.BlockSpec(memory_space=pltpu.VMEM)] * len(came)
-        + [pl.BlockSpec(memory_space=pltpu.HBM)],
+        + [pl.BlockSpec(memory_space=pltpu.HBM)] * len(source),
         out_specs=jax.tree.map(lambda o: pl.BlockSpec(memory_space=pltpu.VMEM), out_shape),
         out_shape=out_shape,
-        scratch_shapes=[
-            pltpu.VMEM((size, half), jnp.bfloat16),
-            pltpu.VMEM((size, half), jnp.bfloat16),
-            pltpu.SemaphoreType.DMA((2,)),
-        ],
+        scratch_shapes=[pltpu.VMEM((sum(sizes), half), jnp.bfloat16)] * 2
+        + [pltpu.SemaphoreType.DMA((2 * len(source),))],
         compiler_params=pltpu.CompilerParams(vmem_limit_bytes=16 * MIB),
         cost_estimate=COST,
-        name=finish.__name__,
-    )(where, *came, hbm(part))
+        name=name,
+    )(where, *came, *[hbm(part) for part in source])
+
+
+def ring_sides(groups):
+    half = sum(right.shape[1] for _, rights in groups for right in rights) // 2
+    sides, filled, number = ([], []), 0, 0
+    for group, (_, rights) in enumerate(groups):
+        for right in rights:
+            begin = 0
+            while begin < right.shape[1]:
+                side = filled // half
+                width = min(right.shape[1] - begin, (side + 1) * half - filled)
+                sides[side].append((group, number, begin, width))
+                begin += width
+                filled += width
+            number += 1
+    return sides, half
+
+
+def ring_mm_call(finish, name, n, where, step, came, groups, out_shape):
+    lefts = [left for group, _ in groups for left in group]
+    rights = [right for _, group in groups for right in group]
+    count = sum(left.shape[0] for left in groups[0][0])
+    size = lefts[0].shape[1] // n
+    sides, half = ring_sides(groups)
+    outs = len(jax.tree.leaves(out_shape))
+    used = [sorted({term[0] for term in side}) for side in sides]
+
+    def kernel(where_ref, *refs):
+        came_refs, refs = refs[: len(came)], refs[len(came) :]
+        left_refs, refs = refs[: len(lefts)], refs[len(lefts) :]
+        right_refs, refs = refs[: len(rights)], refs[len(rights) :]
+        out_refs, refs = refs[:outs], refs[outs:]
+        right_bufs, left_bufs, sem = refs[:2], list(refs[2:-1]), refs[-1]
+        waits, chunks = ([], []), ({}, {})
+        for side in range(2):
+            begin = pl.multiple_of(where_ref[2 * step + side] * size, size)
+            at = 0
+            for group in used[side]:
+                buffer = left_bufs.pop(0)
+                chunks[side][group] = buffer
+                first = sum(len(g[0]) for g in groups[:group])
+                row = 0
+                for ref in left_refs[first : first + len(groups[group][0])]:
+                    rows = ref.shape[0]
+                    copy = pltpu.make_async_copy(
+                        ref.at[:, pl.ds(begin, size)], buffer.at[pl.ds(row, rows), :], sem.at[side]
+                    )
+                    copy.start()
+                    waits[side].append(copy)
+                    row += rows
+            for _, number, column, width in sides[side]:
+                copy = pltpu.make_async_copy(
+                    right_refs[number].at[:, pl.ds(column, width)],
+                    right_bufs[side].at[:, pl.ds(at, width)],
+                    sem.at[side],
+                )
+                copy.start()
+                waits[side].append(copy)
+                at += width
+        values = []
+        for side in range(2):
+            for copy in waits[side]:
+                copy.wait()
+            products, at = [], 0
+            for group in used[side]:
+                width = sum(term[3] for term in sides[side] if term[0] == group)
+                products.append(
+                    dot_tn(chunks[side][group][...], right_bufs[side][:, at : at + width])
+                )
+                at += width
+            value = jnp.concatenate(products, 1) if len(products) > 1 else products[0]
+            values.append(value + wide(came_refs[side]) if came else value)
+        finish(*values, *out_refs)
+
+    return pl.pallas_call(
+        kernel,
+        in_specs=[pl.BlockSpec(memory_space=pltpu.SMEM)]
+        + [pl.BlockSpec(memory_space=pltpu.VMEM)] * len(came)
+        + [pl.BlockSpec(memory_space=pltpu.HBM)] * (len(lefts) + len(rights)),
+        out_specs=jax.tree.map(lambda o: pl.BlockSpec(memory_space=pltpu.VMEM), out_shape),
+        out_shape=out_shape,
+        scratch_shapes=[pltpu.VMEM((count, half), jnp.bfloat16)] * 2
+        + [pltpu.VMEM((count, size), jnp.bfloat16)] * (len(used[0]) + len(used[1]))
+        + [pltpu.SemaphoreType.DMA((2,))],
+        compiler_params=pltpu.CompilerParams(vmem_limit_bytes=32 * MIB),
+        cost_estimate=COST,
+        name=name,
+    )(where, *came, *[hbm(i) for i in lefts + rights])
 
 
 class Order:
@@ -505,49 +617,74 @@
 
 
 class Ring:
-    def __init__(self, n, where, order, part, last, last_shapes):
-        self.n, self.where, self.order, self.part = n, where, order, part
-        self.last, self.last_shapes = last, last_shapes
+    def __init__(self, n, where, order, groups, ahead_made, turned, last_shapes):
+        self.n, self.where, self.order = n, where, order
+        self.last, self.last_shapes = functools.partial(ring_last, turned), last_shapes
         self.step_no = 0
         _, _, self.ahead, self.back = ring_of(n)
-        size, half = part.shape[0] // n, part.shape[1] // 2
+        size = groups[0][0][0].shape[1] // n
+        half = sum(right.shape[1] for _, rights in groups for right in rights) // 2
+        self.ahead_made = ahead_made and size % 128 == 0
+        if self.ahead_made:
+            self.piece, self.source = ring_mm_call, groups
+        else:
+            (lefts, (first, *others)), *more = groups
+            self.piece = ring_call
+            self.source = [order.run(lambda r: weight_grad([(lefts, [r, *others]), *more]), first)]
         self.out = [jax.ShapeDtypeStruct((size, half), jnp.bfloat16)] * 2
-        self.send(self.call(ring_first, self.out))
-
-    def call(self, finish, out):
-        if self.step_no == 0:
+
+    def add(self, extra):
+        self.source.append(extra)
+        rows, half = self.out[0].shape
+        self.out = [jax.ShapeDtypeStruct((rows + EXTRA, half), jnp.bfloat16)] * 2
+        self.last_shapes = [*self.last_shapes, jax.ShapeDtypeStruct((EXTRA, 2 * half), jnp.float32)]
+
+    def begin(self):
+        self.send(self.make(0))
+
+    def make(self, step):
+        return self.order.run(
+            lambda w: self.piece(
+                ring_first, "ring_first", self.n, w, step, (), self.source, self.out
+            ),
+            self.where,
+        )
+
+    def call(self, finish, name, out):
+        if self.ahead_made:
             return self.order.run(
-                lambda p: ring_call(finish, self.n, self.where, 0, (), p, out), self.part
+                lambda a: ring_sum_call(finish, name, (a, self.came[1]), self.part, out), self.came[0]
             )
         return self.order.run(
-            lambda a: ring_call(
-                finish, self.n, self.where, self.step_no, (a, self.came[1]), self.part, out
+            lambda a: self.piece(
+                finish, name, self.n, self.where, self.step_no, (a, self.came[1]), self.source, out
             ),
             self.came[0],
         )
 
     def send(self, held):
         self.came = (lax.ppermute(held[0], "dp", self.ahead), lax.ppermute(held[1], "dp", self.back))
+
+    def prepare(self):
+        if self.ahead_made and self.step_no < self.n - 1:
+            self.part = self.make(self.step_no + 1)
 
     def step(self):
         if self.step_no < self.n - 1:
             self.step_no += 1
             if self.step_no < self.n - 1:
-                self.send(self.call(ring_add, self.out))
+                self.send(self.call(ring_first, "ring_add", self.out))
             else:
-                self.result = self.call(self.last, self.last_shapes)
-
-    def finish(self):
-        while self.step_no < self.n - 1:
-            self.step()
-        return self.result
+                self.result = self.call(self.last, "ring_last", self.last_shapes)
 
 
 DOTS = {"nn": dot_nn, "nt": dot_nt, "tn": dot_tn}
 
 
-def pairs_kernel(kind, outs, count, core_ref, *refs):
-    out_refs = refs[-len(outs) :]
+def pairs_kernel(kind, outs, count, weighed, core_ref, *refs):
+    out_refs = refs[-len(outs) - weighed :]
+    if weighed:
+        sums = jnp.zeros((1, out_refs[-1].shape[1]), jnp.float32)
     for (spots, _), out_ref in zip(outs, out_refs):
         for i, spot in enumerate(spots):
             if spot < 0:
@@ -559,9 +696,17 @@
                 value = DOTS[kind](left_ref[rows, :], right_ref[...])
                 total = value if total is None else total + value
             out_ref[i * BLOCK : (i + 1) * BLOCK, :] = total.astype(out_ref.dtype)
-
-
-def pairs(core, kind, terms, outs, part=0, parts=1, before=(), cols=512):
+            if weighed:
+                sums += jnp.sum(total * wide_at(refs[2 * count], rows), 0, keepdims=True)
+    if weighed:
+        out_refs[-1][...] = jnp.broadcast_to(sums, out_refs[-1].shape)
+
+
+def wide_at(ref, rows):
+    return ref[rows, :].astype(jnp.float32)
+
+
+def pairs(core, kind, terms, outs, part=0, parts=1, before=(), weights=None, cols=512):
     width = terms[0][1].shape[1 if kind == "nn" else 0]
     steps = width // cols // parts
     begin = part * steps
@@ -573,14 +718,20 @@
             specs.append(pl.BlockSpec((right.shape[0], cols), lambda j: (0, begin + j)))
         else:
             specs.append(pl.BlockSpec((cols, right.shape[1]), lambda j: (begin + j, 0)))
-    return pl.pallas_call(
-        functools.partial(pairs_kernel, kind, outs, len(terms)),
+    shapes = [(len(o[0]) * BLOCK, o[1]) for o in outs]
+    weighed = weights is not None
+    if weighed:
+        ins.append(weights)
+        specs.append(pl.BlockSpec((weights.shape[0], cols), lambda j: (0, begin + j)))
+        shapes.append((8, jnp.float32))
+    return pl.pallas_call(
+        functools.partial(pairs_kernel, kind, outs, len(terms), int(weighed)),
         grid=(steps,),
         in_specs=[pl.BlockSpec(memory_space=pltpu.SMEM)]
         + specs
         + [pl.BlockSpec(memory_space=pl.ANY)] * len(before),
-        out_specs=[pl.BlockSpec((len(o[0]) * BLOCK, cols), lambda j: (0, begin + j)) for o in outs],
-        out_shape=[jax.ShapeDtypeStruct((len(o[0]) * BLOCK, width), o[1]) for o in outs],
+        out_specs=[pl.BlockSpec((rows, cols), lambda j: (0, begin + j)) for rows, _ in shapes],
+        out_shape=[jax.ShapeDtypeStruct((rows, width), kind) for rows, kind in shapes],
         input_output_aliases={1 + len(ins) + i: i for i in range(len(before))},
         compiler_params=pltpu.CompilerParams(vmem_limit_bytes=40 * MIB),
         cost_estimate=COST,
@@ -588,15 +739,64 @@
     )(core, *[hbm(i) for i in ins], *before)
 
 
-def near_kernel(mine_ref, came_ref, out_ref):
-    out_ref[...] = (mine_ref[...] + wide(came_ref)).astype(jnp.bfloat16)
-
-
-def near_add(came, mine):
-    return rows_call(
-        near_kernel, "near_add", mine.shape[0], (mine, came),
-        [jax.ShapeDtypeStruct(mine.shape, jnp.bfloat16)],
-    )[0]
+def split_pair_kernel(core_ref, left_ref, right_ref, mine_ref, *other_refs):
+    for spot, own in ((1, False), (0, True)):
+        rows = pl.ds(pl.multiple_of((spot ^ core_ref[0]) * BLOCK, BLOCK), BLOCK)
+        value = dot_nn(left_ref[rows, :], right_ref[...])
+        if own:
+            mine_ref[...] = value
+        else:
+            for j, ref in enumerate(other_refs):
+                ref[...] = value[j * ROWS : (j + 1) * ROWS, :].astype(jnp.bfloat16)
+
+
+def split_pair(core, left, right, cols=512):
+    width = right.shape[1]
+
+    def block(rows):
+        return pl.BlockSpec((rows, cols), lambda j: (0, j))
+
+    pieces = BLOCK // ROWS
+    return pl.pallas_call(
+        split_pair_kernel,
+        grid=(width // cols,),
+        in_specs=[
+            pl.BlockSpec(memory_space=pltpu.SMEM),
+            pl.BlockSpec(left.shape, lambda j: (0, 0)),
+            block(right.shape[0]),
+        ],
+        out_specs=[block(BLOCK)] + [block(ROWS)] * pieces,
+        out_shape=[jax.ShapeDtypeStruct((BLOCK, width), jnp.float32)]
+        + [jax.ShapeDtypeStruct((ROWS, width), jnp.bfloat16)] * pieces,
+        compiler_params=pltpu.CompilerParams(vmem_limit_bytes=24 * MIB),
+        cost_estimate=COST,
+        name="split_pair",
+    )(core, left, right)
+
+
+def near_kernel(mine_ref, *refs):
+    out_ref = refs[-1]
+    for j, came_ref in enumerate(refs[:-1]):
+
+        @pl.when(pl.program_id(0) == j)
+        def _():
+            out_ref[...] = (mine_ref[...] + wide(came_ref)).astype(jnp.bfloat16)
+
+
+def near_add(first, others, mine):
+    came = [first, *others]
+    rows, width = came[0].shape
+    block = pl.BlockSpec((rows, width), lambda i: (i, 0))
+    return pl.pallas_call(
+        near_kernel,
+        grid=(len(came),),
+        in_specs=[block] + [pl.BlockSpec((rows, width), lambda i: (0, 0))] * len(came),
+        out_specs=block,
+        out_shape=jax.ShapeDtypeStruct(mine.shape, jnp.bfloat16),
+        compiler_params=pltpu.CompilerParams(vmem_limit_bytes=24 * MIB),
+        cost_estimate=COST,
+        name="near_add",
+    )(mine, *came)
 
 
 def mixed_kernel(resid_ref, near_ref, far_ref, out_ref):
@@ -620,7 +820,7 @@
         in_specs=[pl.BlockSpec((cols, right.shape[1]), lambda j: (j, 0))]
         + [pl.BlockSpec(left.shape, lambda j: (0, 0)) for left in lefts],
         out_specs=pl.BlockSpec((rows, cols), lambda j: (0, j)),
-        out_shape=jax.ShapeDtypeStruct((rows, right.shape[0]), jnp.bfloat16),
+        out_shape=pltpu.HBM((rows, right.shape[0]), jnp.bfloat16),
         compiler_params=pltpu.CompilerParams(vmem_limit_bytes=40 * MIB),
         cost_estimate=COST,
         name="times_turned",
@@ -661,39 +861,48 @@
     )(*[hbm(i) for i in ins])
 
 
-def join_kernel(core_ref, mine_ref, other_ref, out_ref):
+def join_kernel(core_ref, mine_ref, *refs):
+    out_ref = refs[-1]
+
     @pl.when(pl.program_id(0) % 2 == 0)
     def _():
         out_ref[...] = mine_ref[...]
 
-    @pl.when(pl.program_id(0) % 2 == 1)
-    def _():
-        out_ref[...] = other_ref[...]
-
-
-def join(other, core, mine):
+    for j, other_ref in enumerate(refs[:-1]):
+
+        @pl.when(pl.program_id(0) == 2 * j + 1)
+        def _():
+            out_ref[...] = other_ref[...]
+
+
+def join(first, others, core, mine):
     rows, width = mine.shape
-    block = pl.BlockSpec((BLOCK, width), lambda i, core_ref: (i >> 1, 0))
+    came = [first, *others]
     return pl.pallas_call(
         join_kernel,
         grid_spec=pltpu.PrefetchScalarGridSpec(
             num_scalar_prefetch=1,
             grid=(2 * rows // BLOCK,),
-            in_specs=[block, block],
+            in_specs=[pl.BlockSpec((BLOCK, width), lambda i, core_ref: (i >> 1, 0))]
+            + [pl.BlockSpec((BLOCK, width), lambda i, core_ref: (0, 0))] * len(came),
             out_specs=pl.BlockSpec((BLOCK, width), lambda i, core_ref: (i ^ core_ref[0], 0)),
         ),
         out_shape=jax.ShapeDtypeStruct((2 * rows, width), mine.dtype),
         compiler_params=pltpu.CompilerParams(vmem_limit_bytes=24 * MIB),
         cost_estimate=COST,
         name="join",
-    )(core, mine, other)
-
-
-def to_core(value, pieces=1):
+    )(core, mine, *came)
+
+
+def cut_up(value, pieces, swap):
     share = value.shape[0] // pieces
-    cut = [value[i * share : (i + 1) * share] for i in range(pieces)]
-    came = [lax.ppermute(c, "tensor", CORE_SWAP) for c in cut]
-    return jnp.concatenate(came, 0) if pieces > 1 else came[0]
+    return [
+        lax.ppermute(value[i * share : (i + 1) * share], "tensor", swap) for i in range(pieces)
+    ]
+
+
+def to_core(value):
+    return lax.ppermute(value, "tensor", CORE_SWAP)
 
 
 def to_chip(value):
@@ -702,14 +911,6 @@
 
 def low(value):
     return value.astype(jnp.bfloat16)
-
-
-def all_sum_dp(n, value):
-    step = 1
-    while step < n:
-        value = value + lax.ppermute(value, "dp", tuple((i, i ^ step) for i in range(n)))
-        step *= 2
-    return value
 
 
 def on_device(
@@ -753,20 +954,25 @@
         out = run(lambda q: attend(q, keys, values, seg_ids, j, parts), queries)
         attended.append(out[0])
         probs += out[1:]
-        mine, other = run(lambda a: pairs(core, "nn", [(a, w_out)], mine_other((-1,), (-2,))), out[0])
-        near.append(run(near_add, to_core(other, 4), mine))
+        mine, *other = run(lambda a: split_pair(core, a, w_out), out[0])
+        other = [to_core(piece) for piece in other]
+        near.append(run(near_add, other[0], other[1:], mine))
         far.append(to_chip(near[j]))
 
     grad_low = run(lambda c: live_rows(core, c, seg_ids), cotangent)
+    grad_low, where = lax.optimization_barrier((grad_low, where))
     d_hidden = run(lambda g: times_turned([g], w_down), grad_low)
     x_own = both_parts(lambda j: own_rows(tokens, j))
 
     resid, fed = [], ()
     for j in range(parts):
-        held, inner_own = run(lambda f: settle(x_own[j], near[j], f, mlp_gain), far[j])
+        held, *inner_own = run(lambda f: settle(x_own[j], near[j], f, mlp_gain), far[j])
         resid.append(held)
-        inner_other = to_core(inner_own, 4)
-        fed = run(lambda o: feed(inner_own, o, w_gate, w_up, d_hidden, j, fed), inner_other)
+        inner_other = [to_core(piece) for piece in inner_own]
+        fed = run(
+            lambda o: feed(inner_own[0], [*inner_own[1:], o, *inner_other[1:]], w_gate, w_up, d_hidden, j, fed),
+            inner_other[0],
+        )
     inner, hidden, d_gate, d_up = fed
 
     def shape(*extent):
@@ -776,8 +982,12 @@
     q_cols, k_cols = w_query.shape[1], w_key.shape[1]
     active, results = [], {}
 
-    def ring(name, part, last, last_shapes):
-        active.append((name, Ring(n, where, order, part, last, last_shapes)))
+    def ring(groups, ahead_made, turned, *last_shapes):
+        return Ring(n, where, order, groups, ahead_made, turned, last_shapes)
+
+    def begin(name, made):
+        made.begin()
+        active.append((name, made))
 
     def tick():
         for item in list(active):
@@ -786,8 +996,16 @@
                 results[item[0]] = item[1].result
                 active.remove(item)
 
-    down_part = run(lambda h: weight_grad([([grad_low], [h])]), hidden)
-    ring("down", down_part, ring_last_turned, shape(units, share))
+    def prepare():
+        for item in active:
+            item[1].prepare()
+
+    mlp_ring = ring(
+        [([grad_low], [hidden]), ([inner], [d_gate, d_up])], True, (True, False, False),
+        shape(units, share), shape(share, units), shape(share, units),
+    )
+    begin("mlp", mlp_ring)
+    prepare()
     made = ()
     for half in range(2):
         made = run(
@@ -796,19 +1014,14 @@
             ),
             d_gate,
         )
-        tick()
-    came3 = to_core(order.tie(made[1]))
-    gate_part = run(lambda d: weight_grad([([inner], [d])]), d_gate)
     tick()
-    near3 = run(near_add, came3, made[0])
+    came3 = cut_up(order.tie(made[1]), parts, CORE_SWAP)
+    near3 = run(near_add, came3[0], came3[1:], made[0])
     far3 = to_chip(near3)
-    ring("gate", gate_part, ring_last, shape(share, units))
-    up_part = run(lambda d: weight_grad([([inner], [d])]), d_up)
-    tick()
+    prepare()
     mixed_mine, mixed_other = run(
         lambda h: pairs(core, "nn", [(h, w_down)], mine_other((0, 2), (1, 3))), hidden
     )
-    tick()
     blocks = [part[i : i + BLOCK] for part in attended for i in range(0, rows, BLOCK)]
     attended_mine_first = jnp.where(
         core_no == 0,
@@ -818,16 +1031,16 @@
     grad_own = jnp.concatenate([grad_low[j * rows : j * rows + BLOCK] for j in range(parts)], 0)
     resid_own = jnp.concatenate(resid, 0)
     tick()
+    prepare()
+    tick()
     d_resid, branch_own, mlp_sums = run(
         lambda f: unsettle(near3, f, resid_own, grad_own, mlp_gain), far3
     )
-    both = to_core(jnp.concatenate([branch_own, order.tie(mixed_other)], 0))
-    branch_other, came2 = both[: branch_own.shape[0]], both[branch_own.shape[0] :]
-    tick()
-    ring("up", up_part, ring_last, shape(share, units))
-    near2 = run(near_add, came2, mixed_mine)
-    far2 = to_chip(near2)
-    d_branch = [b[j * BLOCK : (j + 1) * BLOCK] for j in range(parts) for b in (branch_own, branch_other)]
+    branch_other = cut_up(branch_own, parts, CORE_SWAP)
+    prepare()
+    d_branch = []
+    for j in range(parts):
+        d_branch += [branch_own[j * BLOCK : (j + 1) * BLOCK], branch_other[j]]
     d_attended = run(lambda d: times_turned([*d_branch[:-1], d], w_out), d_branch[-1])
     heads_count = k_cols // size
     d_lin, gain_sums = (), jnp.zeros((8, size), jnp.float32)
@@ -840,68 +1053,79 @@
             d_attended,
         )
         gain_sums = gain_sums + total
-        tick()
+        if g == 0:
+            tick()
+            came2 = cut_up(order.tie(mixed_other), parts, CORE_SWAP)
+            prepare()
+    near2 = run(near_add, came2[0], came2[1:], mixed_mine)
+    far2 = to_chip(near2)
     d_q_lin, d_k_lin, d_values = d_lin
-    lin_part = run(
-        lambda d: weight_grad([(d_branch, [attended_mine_first]), ([normed], [d, d_k_lin, d_values])]),
-        d_q_lin,
-    )
-    mine, other = run(
+    mine, other, attn_sums = run(
         lambda d: pairs(
             core, "nt", [(d, w_query), (d_k_lin, w_key), (d_values, w_value)],
-            mine_other((-1, -3), (-2, -4)),
+            mine_other((-1, -3), (-2, -4)), weights=normed,
         ),
         d_q_lin,
     )
+    gains = [0.5 * mlp_sums[0], attn_sums[0] / attn_gain, gain_sums[0], gain_sums[1]]
+    gains = jnp.concatenate([part.reshape(n, -1) for part in gains], 1)
     tick()
-    ring(
-        "lin", lin_part, ring_last_lin,
-        [shape(q_cols, share), shape(share, q_cols), shape(share, k_cols), shape(share, k_cols)],
-    )
+    came4 = cut_up(order.tie(other), parts, CORE_SWAP)
+    near4 = run(near_add, came4[0], came4[1:], mine)
+    far4 = to_chip(near4)
+    prepare()
+    gains = run(jnp.add, to_core(gains), gains)
+    out_value = ring(
+        [(d_branch, [attended_mine_first]), ([normed], [d_values])], False, (True, False),
+        shape(q_cols, share), shape(share, k_cols),
+    )
+    gains = run(jnp.add, to_chip(gains), gains)
+    extra_cols = q_cols + k_cols
+    extra = jnp.pad(low(gains), ((0, 0), (0, EXTRA * extra_cols - gains.shape[1])))
+    out_value.add(extra.reshape(n * EXTRA, extra_cols))
+    tick()
     mixed = run(lambda f, n_, r: rows_call(
         mixed_kernel, "mixed", n_.shape[0], (r, n_, f), [jax.ShapeDtypeStruct(n_.shape, jnp.bfloat16)]
     )[0], far2, near2, resid_own)
-    both = to_core(jnp.concatenate([mixed, order.tie(other)], 0))
-    mixed_far, came4 = both[: mixed.shape[0]], both[mixed.shape[0] :]
+    mixed_far = cut_up(mixed, parts, CORE_SWAP)
+    prepare()
+    query_key = ring(
+        [([normed], [d_q_lin, d_k_lin])], False, (False, False),
+        shape(share, q_cols), shape(share, k_cols),
+    )
+    mixed = run(join, mixed_far[0], mixed_far[1:], core, mixed)
     tick()
-    near4 = run(near_add, came4, mine)
-    far4 = to_chip(near4)
-    mixed = run(join, mixed_far, core, mixed)
+    begin("out value", out_value)
+    begin("query key", query_key)
     tick()
     tick()
     tick()
-    grad_tokens, attn_sums = run(
+    grad_tokens = run(
         lambda f: unsettle_last(near4, f, jnp.concatenate(x_own, 0), d_resid, attn_gain), far4
     )
-    grad_tokens_other = to_core(grad_tokens)
-    heads_sum = gain_sums[:2].reshape(-1)
-    heads_sum = heads_sum + to_chip(heads_sum)
-    gains = jnp.concatenate([mlp_sums[0], attn_sums[0], heads_sum])
+    other = cut_up(grad_tokens, parts, CORE_SWAP)
     tick()
-    grad_tokens = run(join, grad_tokens_other, core, grad_tokens)
-    gains = all_sum_dp(n, gains + to_core(gains))
+    grad_tokens = run(join, other[0], other[1:], core, grad_tokens)
     while active:
         tick()
-    my_dp = lax.axis_index("dp")
-
-    def own(begin, extent):
-        return lax.dynamic_slice(gains, (begin + my_dp * (extent // n),), (extent // n,))
-
-    grad_out, grad_query, grad_key, grad_value = results["lin"]
+    grad_down, grad_gate, grad_up = results["mlp"]
+    (grad_out, grad_value, extra), (grad_query, grad_key) = results["out value"], results["query key"]
+    gains, begins = extra.reshape(-1), np.cumsum([0, width, width, size, size]) // n
+    mlp_sum, attn_sum, q_sum, k_sum = [gains[begins[i] : begins[i + 1]] for i in range(4)]
     return (
         mixed,
         grad_tokens,
-        own(width, width),
+        attn_sum,
         grad_query,
         grad_key,
         grad_value,
         grad_out,
-        own(0, width),
-        results["gate"],
-        results["up"],
-        results["down"],
-        own(2 * width, size),
-        own(2 * width + size, size),
+        mlp_sum,
+        grad_gate,
+        grad_up,
+        grad_down,
+        q_sum,
+        k_sum,
     )
 
 

time: 485 us -> 428 us (0.88)
  waiting for transfers between devices: 102 us -> 60 us
  starting transfers between devices: 70.1 us -> 58 us
  Pallas kernels: 254 us -> 264 us
  local copies, waits for them, and re-layouts: 43.2 us -> 35.7 us
    pallas_call x8 -> x30, Pallas kernels: 70.4 us -> 144 us  [the longest x8 52.6 us: ring_mm_call(): pl.pallas_call(kernel, in_specs=[pl.BlockSpec(memory_space=pltpu.SMEM)] +...]
    pallas_call x32 -> x16, Pallas kernels: 68.4 us -> 29.2 us  [ring_call(): pl.pallas_call(kernel, in_specs=[pl.BlockSpec(memory_space=pltpu.SMEM)] +...]
    ppermute x28 -> x21, waiting for transfers between devices: 61.8 us -> 30.2 us  [send(): lax.ppermute(held[0], 'dp', self.ahead)]
    pallas_call x4 -> x2, Pallas kernels: 44.9 us -> 17.1 us  [weight_grad(): pl.pallas_call(functools.partial(weight_grad_kernel, [(len(a), len(b)) fo...]
    unnamed x135 -> x109, local copies, waits for them, and re-layouts: 35.3 us -> 22.8 us
    ppermute x24 -> x21, waiting for transfers between devices: 20.3 us -> 10.3 us  [the longest x9 8.66 us: to_core(): return lax.ppermute(value, 'tensor', CORE_SWAP)]
    ppermute x28 -> x21, starting transfers between devices: 40.2 us -> 30.9 us  [send(): lax.ppermute(held[0], 'dp', self.ahead)]
    pallas_call x10 -> x3, Pallas kernels: 17.3 us -> 12.5 us  [rows_call(): pl.pallas_call(kernel, grid=(rows // ROWS,), in_specs=[spec(a.shape) for...]
  transfers between devices with their start and end apart: 86 -> 69, of which waited for: 46 -> 29; matrix products, arithmetic and copies ran while one was open for 2% -> 3% of each run, Pallas kernels for 39% -> 51%
where the time goes in v3:
time: 428 us; the launch traced here: 424 us
  Pallas kernels  264 us (62%)
  waiting for transfers between devices  60 us (14%)
  starting transfers between devices  58 us (14%)
  local copies, waits for them, and re-layouts  35.7 us (8%)
  other arithmetic  4.75 us (1%)
    pallas_call x8, Pallas kernels, ring_mm_call(): pl.pallas_call(kernel, in_specs=[pl.BlockSpec(memory_space=pltpu.SMEM)] +...  52.6 us
    pallas_call x4, Pallas kernels, pairs(): pl.pallas_call(functools.partial(pairs_kernel, kind, outs, len(terms), in...  40.1 us
    ppermute x21, starting transfers between devices, send(): lax.ppermute(held[0], 'dp', self.ahead)  30.9 us
    ppermute x21, waiting for transfers between devices, send(): lax.ppermute(held[0], 'dp', self.ahead)  30.2 us
    pallas_call x16, Pallas kernels, ring_call(): pl.pallas_call(kernel, in_specs=[pl.BlockSpec(memory_space=pltpu.SMEM)] +...  29.2 us
    pallas_call x2, Pallas kernels, feed(): pl.pallas_call(functools.partial(feed_kernel, len(lefts)), grid=(units //...  24.6 us
    unnamed x109, local copies, waits for them, and re-layouts  22.8 us
    pallas_call x2, Pallas kernels, attend_back(): pl.pallas_call(functools.partial(attend_back_kernel, blocks), grid=(1,),...  18.1 us
  transfers between devices with their start and end apart: 69, of which 29 were waited for; matrix products, arithmetic and copies ran while one was open for 3% of the time, Pallas kernels for 51%

profile of v3, /device:TPU:0, one launch (start us, length us, event | category | flops | bytes accessed | tf_op | source)
XLA Modules:
  0.0 424.0 jit_solution(3335161772006893181)
XLA Ops:
  4.6 10.9 %front.1 = (bf16[1024,2048]{1,0:T(8,128)(2,1)}, bf16[1024,512]{1,0:T(8,128)(2,1)}, bf16[1024,256]{1,0:T(8,128)(2,1)}, bf16[1024,256]{1,0:T(8,128)(2,1)}, f32[1024,512]{1,0:T(8,128)}, /*index=5*/f32[1024,256]{1,0:T(8,128)}) custom-call(bf16[1024,2048]{1,0:T(8,128)(2,1)} %x_ref.1, f32[1,2048]{1,0:T(1,128)S(1)} %bitcast.15, bf16[2048,512]{1,0:T(8,128)(2,1)} %refs_1_.7, ...), custom_call_target="tpu_custom_call" | custom-call | tf_op jit(solution)/shard_map/front/pallas_call | solution.py:83
  31.3 6.4 %attend.3 = (bf16[512,512]{1,0:T(8,128)(2,1)S(1)}, bf16[2,512,768]{2,1,0:T(8,128)(2,1)}, bf16[2,512,1024]{2,1,0:T(8,128)(2,1)}) custom-call(bf16[1024,512]{1,0:T(8,128)(2,1)} %get-tuple-element.207.q_ref.refs_2_, bf16[1024,256]{1,0:T(8,128)(2,1)} %get-tuple-element.199.k_ref.refs_3_, bf16[1024,256]{1,0:T(8,128)(2,1)} %get-tuple-element.200.v_ref.refs_4_, ...), custom_call_target="tpu_custom_call" | custom-call | tf_op jit(solution)/shard_map/attend/pallas_call | solution.py:144
  51.5 8.1 %times_turned.2.refs_6_ = bf16[1024,1536]{1,0:T(8,128)(2,1)} custom-call(bf16[1536,2048]{1,0:T(8,128)(2,1)S(1)} %bitcast.11, bf16[1024,2048]{1,0:T(8,128)(2,1)S(1)} %live_rows.1.refs_1_.refs_0_), custom_call_target="tpu_custom_call" | custom-call | tf_op jit(solution)/shard_map/times_turned/pallas_call | solution.py:817
  64.6 12.4 %feed.2 = (bf16[1024,2048]{1,0:T(8,128)(2,1)}, bf16[1024,1536]{1,0:T(8,128)(2,1)}, bf16[1024,1536]{1,0:T(8,128)(2,1)}, bf16[1024,1536]{1,0:T(8,128)(2,1)}) custom-call(bf16[128,2048]{1,0:T(8,128)(2,1)S(1)} %get-tuple-element.219.refs_0_, bf16[128,2048]{1,0:T(8,128)(2,1)S(1)} %get-tuple-element.220.refs_1_, ...), custom_call_target="tpu_custom_call" | custom-call | tf_op jit(solution)/shard_map/feed/pallas_call | solution.py:279
  84.3 12.2 %feed.3 = (bf16[1024,2048]{1,0:T(8,128)(2,1)}, bf16[1024,1536]{1,0:T(8,128)(2,1)}, bf16[1024,1536]{1,0:T(8,128)(2,1)}, bf16[1024,1536]{1,0:T(8,128)(2,1)}) custom-call(bf16[128,2048]{1,0:T(8,128)(2,1)S(1)} %get-tuple-element.225.refs_0_, ...), custom_call_target="tpu_custom_call", output_to_operand_aliasing={{0}: (7, {}), {1}: (8, {}), {2}: (9, {}), {3}: (10, {})} | custom-call | tf_op jit(solution)/shard_map/feed/pallas_call | solution.py:279
  96.5 6.5 %ring_first.10 = (bf16[256,2304]{1,0:T(8,128)(2,1)S(1)}, bf16[256,2304]{1,0:T(8,128)(2,1)S(1)}) custom-call(s32[16]{0:T(128)S(1)} %fusion.1.where_ref, bf16[1024,2048]{1,0:T(8,128)(2,1)} %copy-done, bf16[1024,2048]{1,0:T(8,128)(2,1)} %get-tuple-element.234.refs_1_, bf16[1024,1536]{1,0:T(8,128)(2,1)} %get-tuple-element.254.refs_2_.refs_0_, ...), custom_call_target="tpu_custom_call" | custom-call | tf_op jit(solution)/shard_map/ring_first/pallas_call | solution.py:587
  105.1 6.5 %ring_first.11 = (bf16[256,2304]{1,0:T(8,128)(2,1)S(1)}, bf16[256,2304]{1,0:T(8,128)(2,1)S(1)}) custom-call(s32[16]{0:T(128)S(1)} %fusion.1.where_ref, bf16[1024,2048]{1,0:T(8,128)(2,1)} %copy-done, bf16[1024,2048]{1,0:T(8,128)(2,1)} %get-tuple-element.234.refs_1_, bf16[1024,1536]{1,0:T(8,128)(2,1)} %get-tuple-element.254.refs_2_.refs_0_, ...), custom_call_target="tpu_custom_call" | custom-call | tf_op jit(solution)/shard_map/ring_first/pallas_call | solution.py:587
  111.5 11.1 %pairs.4 = (f32[512,2048]{1,0:T(8,128)S(1)}, bf16[512,2048]{1,0:T(8,128)(2,1)S(1)}) custom-call(s32[1]{0:T(128)} %bitcast.core_ref.refs_0_, bf16[1024,1536]{1,0:T(8,128)(2,1)} %get-tuple-element.242.refs_3_.refs_0_, bf16[2048,1536]{1,0:T(8,128)(2,1)} %refs_1_.5, bf16[1024,1536]{1,0:T(8,128)(2,1)} %get-tuple-element.236.refs_4_.refs_2_, ...), custom_call_target="tpu_custom_call" | custom-call | tf_op jit(solution)/shard_map/pairs/pallas_call | solution.py:727
  122.6 10.9 %pairs.5 = (f32[512,2048]{1,0:T(8,128)S(1)}, bf16[512,2048]{1,0:T(8,128)(2,1)S(1)}) custom-call(s32[1]{0:T(128)} %bitcast.core_ref.refs_0_, bf16[1024,1536]{1,0:T(8,128)(2,1)} %get-tuple-element.242.refs_3_.refs_0_, bf16[2048,1536]{1,0:T(8,128)(2,1)} %refs_1_.5, ...), custom_call_target="tpu_custom_call", output_to_operand_aliasing={{0}: (5, {}), {1}: (6, {})} | custom-call | tf_op jit(solution)/shard_map/pairs/pallas_call | solution.py:727
  140.7 6.5 %ring_first.12 = (bf16[256,2304]{1,0:T(8,128)(2,1)S(1)}, bf16[256,2304]{1,0:T(8,128)(2,1)S(1)}) custom-call(s32[16]{0:T(128)S(1)} %fusion.1.where_ref, bf16[1024,2048]{1,0:T(8,128)(2,1)} %copy-done, bf16[1024,2048]{1,0:T(8,128)(2,1)} %get-tuple-element.234.refs_1_, bf16[1024,1536]{1,0:T(8,128)(2,1)} %get-tuple-element.254.refs_2_.refs_0_, ...), custom_call_target="tpu_custom_call" | custom-call | tf_op jit(solution)/shard_map/ring_first/pallas_call | solution.py:587
  148.2 10.0 %pairs.6 = (f32[512,2048]{1,0:T(8,128)S(1)}, bf16[512,2048]{1,0:T(8,128)(2,1)S(1)}) custom-call(s32[1]{0:T(128)} %bitcast.core_ref.refs_0_, bf16[1024,1536]{1,0:T(8,128)(2,1)} %get-tuple-element.254.refs_2_.refs_0_, bf16[1536,2048]{1,0:T(8,128)(2,1)} %refs_1_.6), custom_call_target="tpu_custom_call" | custom-call | tf_op jit(solution)/shard_map/pairs/pallas_call | solution.py:727
  172.6 7.4 %ring_first.13 = (bf16[256,2304]{1,0:T(8,128)(2,1)S(1)}, bf16[256,2304]{1,0:T(8,128)(2,1)S(1)}) custom-call(s32[16]{0:T(128)S(1)} %fusion.1.where_ref, bf16[1024,2048]{1,0:T(8,128)(2,1)} %copy-done, bf16[1024,2048]{1,0:T(8,128)(2,1)} %get-tuple-element.234.refs_1_, bf16[1024,1536]{1,0:T(8,128)(2,1)} %get-tuple-element.254.refs_2_.refs_0_, ...), custom_call_target="tpu_custom_call" | custom-call | tf_op jit(solution)/shard_map/ring_first/pallas_call | solution.py:587
  180.0 15.7 %collective-permute-done.16.came_a_ref = bf16[256,2304]{1,0:T(8,128)(2,1)S(1)} collective-permute-done((bf16[256,2304]{1,0:T(8,128)(2,1)S(1)}, bf16[256,2304]{1,0:T(8,128)(2,1)S(1)}, u32[]{:S(2)}, u32[]{:S(2)}) %collective-permute-start.16) | collective-permute-done | bytes 1179680 | tf_op jit(solution)/shard_map/ppermute | solution.py:666
  207.0 6.5 %ring_first.14 = (bf16[256,2304]{1,0:T(8,128)(2,1)S(1)}, bf16[256,2304]{1,0:T(8,128)(2,1)S(1)}) custom-call(s32[16]{0:T(128)S(1)} %fusion.1.where_ref, bf16[1024,2048]{1,0:T(8,128)(2,1)} %copy-done, bf16[1024,2048]{1,0:T(8,128)(2,1)} %get-tuple-element.234.refs_1_, bf16[1024,1536]{1,0:T(8,128)(2,1)} %get-tuple-element.254.refs_2_.refs_0_, ...), custom_call_target="tpu_custom_call" | custom-call | tf_op jit(solution)/shard_map/ring_first/pallas_call | solution.py:587
  218.1 9.0 %attend_back.2 = (bf16[1024,512]{1,0:T(8,128)(2,1)S(1)}, bf16[1024,256]{1,0:T(8,128)(2,1)S(1)}, bf16[1024,256]{1,0:T(8,128)(2,1)S(1)}, f32[8,128]{1,0:T(8,128)S(1)}) custom-call(s32[1]{0:T(128)} %bitcast.core_ref.refs_0_, bf16[1024,512]{1,0:T(8,128)(2,1)S(1)} %copy-done.7, bf16[1024,512]{1,0:T(8,128)(2,1)} %get-tuple-element.207.q_ref.refs_2_, ...), custom_call_target="tpu_custom_call" | custom-call | tf_op jit(solution)/shard_map/attend_back/pallas_call | solution.py:224
  230.8 6.5 %ring_first.15 = (bf16[256,2304]{1,0:T(8,128)(2,1)S(1)}, bf16[256,2304]{1,0:T(8,128)(2,1)S(1)}) custom-call(s32[16]{0:T(128)S(1)} %fusion.1.where_ref, bf16[1024,2048]{1,0:T(8,128)(2,1)} %copy-done, bf16[1024,2048]{1,0:T(8,128)(2,1)} %get-tuple-element.234.refs_1_, bf16[1024,1536]{1,0:T(8,128)(2,1)} %get-tuple-element.254.refs_2_.refs_0_, ...), custom_call_target="tpu_custom_call" | custom-call | tf_op jit(solution)/shard_map/ring_first/pallas_call | solution.py:587
  237.2 9.0 %attend_back.3 = (bf16[1024,512]{1,0:T(8,128)(2,1)S(1)}, bf16[1024,256]{1,0:T(8,128)(2,1)S(1)}, bf16[1024,256]{1,0:T(8,128)(2,1)S(1)}, f32[8,128]{1,0:T(8,128)S(1)}) custom-call(s32[1]{0:T(128)} %bitcast.core_ref.refs_0_, bf16[1024,512]{1,0:T(8,128)(2,1)S(1)} %copy-done.7, ...), custom_call_target="tpu_custom_call", output_to_operand_aliasing={{0}: (15, {}), {1}: (16, {}), {2}: (17, {})} | custom-call | tf_op jit(solution)/shard_map/attend_back/pallas_call | solution.py:224
  249.1 8.2 %pairs.7 = (f32[512,2048]{1,0:T(8,128)S(1)}, bf16[512,2048]{1,0:T(8,128)(2,1)S(1)}, f32[8,2048]{1,0:T(8,128)S(1)}) custom-call(s32[1]{0:T(128)} %bitcast.core_ref.refs_0_, bf16[1024,512]{1,0:T(8,128)(2,1)} %copy-done.12, bf16[2048,512]{1,0:T(8,128)(2,1)} %refs_1_.7, bf16[1024,256]{1,0:T(8,128)(2,1)} %copy-done.26, bf16[2048,256]{1,0:T(8,128)(2,1)} %refs_3_.5, ...), custom_call_target="tpu_custom_call" | custom-call | tf_op jit(solution)/shard_map/pairs/pallas_call | solution.py:727
  273.0 6.5 %ring_first.16 = (bf16[256,2304]{1,0:T(8,128)(2,1)S(1)}, bf16[256,2304]{1,0:T(8,128)(2,1)S(1)}) custom-call(s32[16]{0:T(128)S(1)} %fusion.1.where_ref, bf16[1024,2048]{1,0:T(8,128)(2,1)} %copy-done, bf16[1024,2048]{1,0:T(8,128)(2,1)} %get-tuple-element.234.refs_1_, bf16[1024,1536]{1,0:T(8,128)(2,1)} %get-tuple-element.254.refs_2_.refs_0_, ...), custom_call_target="tpu_custom_call" | custom-call | tf_op jit(solution)/shard_map/ring_first/pallas_call | solution.py:587
  282.8 9.1 %weight_grad.2.refs_0_.refs_2_ = bf16[2048,768]{1,0:T(8,128)(2,1)S(1)} custom-call(bf16[256,2048]{1,0:T(8,128)(2,1)} %copy-done.11, bf16[256,2048]{1,0:T(8,128)(2,1)} %copy-done.29, bf16[256,2048]{1,0:T(8,128)(2,1)} %copy-done.10, bf16[256,2048]{1,0:T(8,128)(2,1)} %copy-done.28, bf16[1024,512]{1,0:T(8,128)(2,1)} %maximum_select_fusion.refs_4_, ...), custom_call_target="tpu_custom_call" | custom-call | tf_op jit(solution)/shard_map/weight_grad/pallas_call | solution.py:852
  307.6 6.5 %ring_first.17 = (bf16[256,2304]{1,0:T(8,128)(2,1)S(1)}, bf16[256,2304]{1,0:T(8,128)(2,1)S(1)}) custom-call(s32[16]{0:T(128)S(1)} %fusion.1.where_ref, bf16[1024,2048]{1,0:T(8,128)(2,1)} %copy-done, bf16[1024,2048]{1,0:T(8,128)(2,1)} %get-tuple-element.234.refs_1_, bf16[1024,1536]{1,0:T(8,128)(2,1)} %get-tuple-element.254.refs_2_.refs_0_, ...), custom_call_target="tpu_custom_call" | custom-call | tf_op jit(solution)/shard_map/ring_first/pallas_call | solution.py:587
  314.0 8.0 %weight_grad.3.refs_0_.refs_2_ = bf16[2048,768]{1,0:T(8,128)(2,1)S(1)} custom-call(bf16[1024,2048]{1,0:T(8,128)(2,1)} %get-tuple-element.197.refs_6_.refs_5_.refs_0_, bf16[1024,512]{1,0:T(8,128)(2,1)} %copy-done.12, bf16[1024,256]{1,0:T(8,128)(2,1)} %copy-done.26), custom_call_target="tpu_custom_call" | custom-call | tf_op jit(solution)/shard_map/weight_grad/pallas_call | solution.py:852
  322.0 5.1 %join.2 = bf16[1024,2048]{1,0:T(8,128)(2,1)} custom-call(s32[1]{0:T(128)} %bitcast.core_ref.refs_0_, bf16[512,2048]{1,0:T(8,128)(2,1)S(1)} %mixed.1.mine_ref, bf16[256,2048]{1,0:T(8,128)(2,1)} %collective-permute-done.34.refs_0_, bf16[256,2048]{1,0:T(8,128)(2,1)} %collective-permute-done.35.refs_1_), custom_call_target="tpu_custom_call" | custom-call | tf_op jit(solution)/shard_map/join/pallas_call | solution.py:881
  371.2 5.0 %unsettle_last.1.mine_ref = bf16[512,2048]{1,0:T(8,128)(2,1)S(1)} custom-call(bf16[512,2048]{1,0:T(8,128)(2,1)} %near_add.9.near_ref, bf16[512,2048]{1,0:T(8,128)(2,1)} %collective-permute-done.36.far_ref, bf16[512,2048]{1,0:T(8,128)(2,1)S(1)} %pad_maximum_fusion.1.resid_ref, f32[512,2048]{1,0:T(8,128)S(1)} %copy-done.34, f32[1,2048]{1,0:T(1,128)S(1)} %bitcast.16), custom_call_target="tpu_custom_call" | custom-call | tf_op jit(solution)/shard_map/unsettle_last/pallas_call | solution.py:303
  (322 shorter events, 218.2 us)
Async XLA Ops:
  28.5 31.2 %collective-permute-start.2 = (bf16[256,2048]{1,0:T(8,128)(2,1)}, bf16[256,2048]{1,0:T(8,128)(2,1)}, u32[]{:S(2)}, u32[]{:S(2)}) collective-permute-start(bf16[256,2048]{1,0:T(8,128)(2,1)} %near_add.5.near_ref), channel_id=1, source_target_pairs={{0,2},{1,3},{2,0},{3,1},{4,6},{5,7},{6,4},{7,5},{8,10},{9,11},{10,... | collective-permute-start | bytes 3145736 | tf_op jit(solution)/shard_map/ppermute | solution.py:909
  43.7 33.8 %collective-permute-start.5 = (bf16[256,2048]{1,0:T(8,128)(2,1)}, bf16[256,2048]{1,0:T(8,128)(2,1)}, u32[]{:S(2)}, u32[]{:S(2)}) collective-permute-start(bf16[256,2048]{1,0:T(8,128)(2,1)} %near_add.6.near_ref), channel_id=1, source_target_pairs={{0,2},{1,3},{2,0},{3,1},{4,6},{5,7},{6,4},{7,5},{8,10},{9,11},{10,... | collective-permute-start | bytes 3145736 | tf_op jit(solution)/shard_map/ppermute | solution.py:909
  103.0 30.5 %collective-permute-start.10 = (bf16[256,2304]{1,0:T(8,128)(2,1)S(1)}, bf16[256,2304]{1,0:T(8,128)(2,1)S(1)}, u32[]{:S(2)}, u32[]{:S(2)}) collective-permute-start(bf16[256,2304]{1,0:T(8,128)(2,1)S(1)} %get-tuple-element.237), channel_id=1, source_target_pairs={{0,8},{8,16},{16,24},{24,28},{28,20},{20,12},{12,4},{4,0},{1,9},{9... | collective-permute-start | bytes 3538952 | tf_op jit(solution)/shard_map/ppermute | solution.py:666
  104.9 28.6 %collective-permute-start.11 = (bf16[256,2304]{1,0:T(8,128)(2,1)S(1)}, bf16[256,2304]{1,0:T(8,128)(2,1)S(1)}, u32[]{:S(2)}, u32[]{:S(2)}) collective-permute-start(bf16[256,2304]{1,0:T(8,128)(2,1)S(1)} %get-tuple-element.247), channel_id=1, source_target_pairs={{8,0},{16,8},{24,16},{28,24},{20,28},{12,20},{4,12},{0,4},{9,1},{1... | collective-permute-start | bytes 3538952 | tf_op jit(solution)/shard_map/ppermute | solution.py:666
  134.9 28.0 %collective-permute-start.14 = (bf16[256,2304]{1,0:T(8,128)(2,1)S(1)}, bf16[256,2304]{1,0:T(8,128)(2,1)S(1)}, u32[]{:S(2)}, u32[]{:S(2)}) collective-permute-start(bf16[256,2304]{1,0:T(8,128)(2,1)S(1)} %get-tuple-element.249), channel_id=1, source_target_pairs={{0,8},{8,16},{16,24},{24,28},{28,20},{20,12},{12,4},{4,0},{1,9},{9... | collective-permute-start | bytes 3538952 | tf_op jit(solution)/shard_map/ppermute | solution.py:666
  136.7 27.7 %collective-permute-start.15 = (bf16[256,2304]{1,0:T(8,128)(2,1)S(1)}, bf16[256,2304]{1,0:T(8,128)(2,1)S(1)}, u32[]{:S(2)}, u32[]{:S(2)}) collective-permute-start(bf16[256,2304]{1,0:T(8,128)(2,1)S(1)} %get-tuple-element.258), channel_id=1, source_target_pairs={{8,0},{16,8},{24,16},{28,24},{20,28},{12,20},{4,12},{0,4},{9,1},{1... | collective-permute-start | bytes 3538952 | tf_op jit(solution)/shard_map/ppermute | solution.py:666
  138.9 60.7 %collective-permute-start.19 = (bf16[512,2048]{1,0:T(8,128)(2,1)S(1)}, bf16[512,2048]{1,0:T(8,128)(2,1)}, u32[]{:S(2)}, u32[]{:S(2)}) collective-permute-start(bf16[512,2048]{1,0:T(8,128)(2,1)S(1)} %near_add.7.near_ref), channel_id=1, source_target_pairs={{0,2},{1,3},{2,0},{3,1},{4,6},{5,7},{6,4},{7,5},{8,10},{9,11},{10,... | collective-permute-start | bytes 6291464 | tf_op jit(solution)/shard_map/ppermute | solution.py:909
  168.5 27.2 %collective-permute-start.17 = (bf16[256,2304]{1,0:T(8,128)(2,1)S(1)}, bf16[256,2304]{1,0:T(8,128)(2,1)S(1)}, u32[]{:S(2)}, u32[]{:S(2)}) collective-permute-start(bf16[256,2304]{1,0:T(8,128)(2,1)S(1)} %get-tuple-element.264), channel_id=1, source_target_pairs={{8,0},{16,8},{24,16},{28,24},{20,28},{12,20},{4,12},{0,4},{9,1},{1... | collective-permute-start | bytes 3538952 | tf_op jit(solution)/shard_map/ppermute | solution.py:666
  168.8 26.9 %collective-permute-start.16 = (bf16[256,2304]{1,0:T(8,128)(2,1)S(1)}, bf16[256,2304]{1,0:T(8,128)(2,1)S(1)}, u32[]{:S(2)}, u32[]{:S(2)}) collective-permute-start(bf16[256,2304]{1,0:T(8,128)(2,1)S(1)} %get-tuple-element.260), channel_id=1, source_target_pairs={{0,8},{8,16},{16,24},{24,28},{28,20},{20,12},{12,4},{4,0},{1,9},{9... | collective-permute-start | bytes 3538952 | tf_op jit(solution)/shard_map/ppermute | solution.py:666
  197.2 30.0 %collective-permute-start.22 = (bf16[256,2304]{1,0:T(8,128)(2,1)S(1)}, bf16[256,2304]{1,0:T(8,128)(2,1)S(1)}, u32[]{:S(2)}, u32[]{:S(2)}) collective-permute-start(bf16[256,2304]{1,0:T(8,128)(2,1)S(1)} %get-tuple-element.282), channel_id=1, source_target_pairs={{8,0},{16,8},{24,16},{28,24},{20,28},{12,20},{4,12},{0,4},{9,1},{1... | collective-permute-start | bytes 3538952 | tf_op jit(solution)/shard_map/ppermute | solution.py:666
  198.7 28.4 %collective-permute-start.18 = (bf16[256,2304]{1,0:T(8,128)(2,1)}, bf16[256,2304]{1,0:T(8,128)(2,1)S(1)}, u32[]{:S(2)}, u32[]{:S(2)}) collective-permute-start(bf16[256,2304]{1,0:T(8,128)(2,1)} %get-tuple-element.266), channel_id=1, source_target_pairs={{0,8},{8,16},{16,24},{24,28},{28,20},{20,12},{12,4},{4,0},{1,9},{9... | collective-permute-start | bytes 3538952 | tf_op jit(solution)/shard_map/ppermute | solution.py:666
  227.7 29.6 %collective-permute-start.26 = (bf16[256,2304]{1,0:T(8,128)(2,1)S(1)}, bf16[256,2304]{1,0:T(8,128)(2,1)S(1)}, u32[]{:S(2)}, u32[]{:S(2)}) collective-permute-start(bf16[256,2304]{1,0:T(8,128)(2,1)S(1)} %get-tuple-element.284), channel_id=1, source_target_pairs={{0,8},{8,16},{16,24},{24,28},{28,20},{20,12},{12,4},{4,0},{1,9},{9... | collective-permute-start | bytes 3538952 | tf_op jit(solution)/shard_map/ppermute | solution.py:666
  229.2 28.1 %collective-permute-start.27 = (bf16[256,2304]{1,0:T(8,128)(2,1)S(1)}, bf16[256,2304]{1,0:T(8,128)(2,1)S(1)}, u32[]{:S(2)}, u32[]{:S(2)}) collective-permute-start(bf16[256,2304]{1,0:T(8,128)(2,1)S(1)} %get-tuple-element.298), channel_id=1, source_target_pairs={{8,0},{16,8},{24,16},{28,24},{20,28},{12,20},{4,12},{0,4},{9,1},{1... | collective-permute-start | bytes 3538952 | tf_op jit(solution)/shard_map/ppermute | solution.py:666
  230.2 16.1 %collective-permute-start.23 = (bf16[256,2048]{1,0:T(8,128)(2,1)S(1)}, bf16[256,2048]{1,0:T(8,128)(2,1)S(1)}, u32[]{:S(2)}, u32[]{:S(2)}) collective-permute-start(bf16[256,2048]{1,0:T(8,128)(2,1)S(1)} %get-tuple-element.392), channel_id=1, source_target_pairs={{0,1},{1,0},{2,3},{3,2},{4,5},{5,4},{6,7},{7,6},{8,9},{9,8},{10,11... | collective-permute-start | bytes 3145736 | tf_op jit(solution)/shard_map/ppermute | solution.py:900
  230.3 16.1 %collective-permute-start.24 = (bf16[256,2048]{1,0:T(8,128)(2,1)S(1)}, bf16[256,2048]{1,0:T(8,128)(2,1)S(1)}, u32[]{:S(2)}, u32[]{:S(2)}) collective-permute-start(bf16[256,2048]{1,0:T(8,128)(2,1)S(1)} %get-tuple-element.391), channel_id=1, source_target_pairs={{0,1},{1,0},{2,3},{3,2},{4,5},{5,4},{6,7},{7,6},{8,9},{9,8},{10,11... | collective-permute-start | bytes 3145736 | tf_op jit(solution)/shard_map/ppermute | solution.py:900
  247.6 54.6 %collective-permute-start.25 = (bf16[512,2048]{1,0:T(8,128)(2,1)S(1)}, bf16[512,2048]{1,0:T(8,128)(2,1)}, u32[]{:S(2)}, u32[]{:S(2)}) collective-permute-start(bf16[512,2048]{1,0:T(8,128)(2,1)S(1)} %near_add.8.near_ref), channel_id=1, source_target_pairs={{0,2},{1,3},{2,0},{3,1},{4,6},{5,7},{6,4},{7,5},{8,10},{9,11},{10,... | collective-permute-start | bytes 6291464 | tf_op jit(solution)/shard_map/ppermute | solution.py:909
  262.0 34.5 %collective-permute-start.28 = (bf16[256,2304]{1,0:T(8,128)(2,1)}, bf16[256,2304]{1,0:T(8,128)(2,1)}, u32[]{:S(2)}, u32[]{:S(2)}) collective-permute-start(bf16[256,2304]{1,0:T(8,128)(2,1)} %copy-done.49), channel_id=1, source_target_pairs={{0,8},{8,16},{16,24},{24,28},{28,20},{20,12},{12,4},{4,0},{1,9},{9... | collective-permute-start | bytes 3538952 | tf_op jit(solution)/shard_map/ppermute | solution.py:666
  263.5 33.1 %collective-permute-start.33 = (bf16[256,2304]{1,0:T(8,128)(2,1)}, bf16[256,2304]{1,0:T(8,128)(2,1)}, u32[]{:S(2)}, u32[]{:S(2)}) collective-permute-start(bf16[256,2304]{1,0:T(8,128)(2,1)} %copy-done.48), channel_id=1, source_target_pairs={{8,0},{16,8},{24,16},{28,24},{20,28},{12,20},{4,12},{0,4},{9,1},{1... | collective-permute-start | bytes 3538952 | tf_op jit(solution)/shard_map/ppermute | solution.py:666
  279.5 17.0 %collective-permute-start.32 = (f32[8,544]{1,0:T(8,128)S(1)}, f32[8,544]{1,0:T(8,128)S(1)}, u32[]{:S(2)}, u32[]{:S(2)}) collective-permute-start(f32[8,544]{1,0:T(8,128)S(1)} %fusion.13), channel_id=1, source_target_pairs={{0,2},{1,3},{2,0},{3,1},{4,6},{5,7},{6,4},{7,5},{8,10},{9,11},{10,... | collective-permute-start | bytes 52232 | tf_op jit(solution)/shard_map/ppermute | solution.py:909
  281.5 89.7 %collective-permute-start.36 = (bf16[512,2048]{1,0:T(8,128)(2,1)}, bf16[512,2048]{1,0:T(8,128)(2,1)}, u32[]{:S(2)}, u32[]{:S(2)}) collective-permute-start(bf16[512,2048]{1,0:T(8,128)(2,1)} %near_add.9.near_ref), channel_id=1, source_target_pairs={{0,2},{1,3},{2,0},{3,1},{4,6},{5,7},{6,4},{7,5},{8,10},{9,11},{10,... | collective-permute-start | bytes 6291464 | tf_op jit(solution)/shard_map/ppermute | solution.py:909
  300.1 27.9 %collective-permute-start.38 = (bf16[256,2304]{1,0:T(8,128)(2,1)}, bf16[256,2304]{1,0:T(8,128)(2,1)}, u32[]{:S(2)}, u32[]{:S(2)}) collective-permute-start(bf16[256,2304]{1,0:T(8,128)(2,1)} %get-tuple-element.323), channel_id=1, source_target_pairs={{8,0},{16,8},{24,16},{28,24},{20,28},{12,20},{4,12},{0,4},{9,1},{1... | collective-permute-start | bytes 3538952 | tf_op jit(solution)/shard_map/ppermute | solution.py:666
  301.7 26.4 %collective-permute-start.37 = (bf16[256,2304]{1,0:T(8,128)(2,1)}, bf16[256,2304]{1,0:T(8,128)(2,1)}, u32[]{:S(2)}, u32[]{:S(2)}) collective-permute-start(bf16[256,2304]{1,0:T(8,128)(2,1)} %get-tuple-element.316), channel_id=1, source_target_pairs={{0,8},{8,16},{16,24},{24,28},{28,20},{20,12},{12,4},{4,0},{1,9},{9... | collective-permute-start | bytes 3538952 | tf_op jit(solution)/shard_map/ppermute | solution.py:666
  376.4 18.1 %collective-permute-start.51 = (bf16[256,2048]{1,0:T(8,128)(2,1)S(1)}, bf16[256,2048]{1,0:T(8,128)(2,1)S(1)}, u32[]{:S(2)}, u32[]{:S(2)}) collective-permute-start(bf16[256,2048]{1,0:T(8,128)(2,1)S(1)} %get-tuple-element.386), channel_id=1, source_target_pairs={{0,1},{1,0},{2,3},{3,2},{4,5},{5,4},{6,7},{7,6},{8,9},{9,8},{10,11... | collective-permute-start | bytes 3145736 | tf_op jit(solution)/shard_map/ppermute | solution.py:900
  376.5 18.4 %collective-permute-start.56 = (bf16[256,2048]{1,0:T(8,128)(2,1)S(1)}, bf16[256,2048]{1,0:T(8,128)(2,1)S(1)}, u32[]{:S(2)}, u32[]{:S(2)}) collective-permute-start(bf16[256,2048]{1,0:T(8,128)(2,1)S(1)} %get-tuple-element.385), channel_id=1, source_target_pairs={{0,1},{1,0},{2,3},{3,2},{4,5},{5,4},{6,7},{7,6},{8,9},{9,8},{10,11... | collective-permute-start | bytes 3145736 | tf_op jit(solution)/shard_map/ppermute | solution.py:900
  (99 other events, 602.2 us)

commit v4 on v3

--- a/solution.py
+++ b/solution.py
@@ -31,6 +31,34 @@
     return lax.dot_general(
         left, right, (((0,), (0,)), ((), ())), preferred_element_type=jnp.float32
     )
+
+SENDS = {
+    "core3": CORE_SWAP,
+    "x3": CHIP_SWAP,
+    "core2": CORE_SWAP,
+    "x2": CHIP_SWAP,
+    "coreM": CORE_SWAP,
+    "coreB": CORE_SWAP,
+    "gains1": CORE_SWAP,
+    "gains2": CHIP_SWAP,
+    "core4": CORE_SWAP,
+    "x4": CHIP_SWAP,
+    "coreG": CORE_SWAP,
+}
+TIES = {
+    "coreM": ("lp", 1),
+    "x4": ("add", 6),
+    "core2": ("add", 2),
+}
+SCHEDULE = (
+    "piece0", "dih0", "dih1", "piece", "add", "near3", "piece", "piece",
+    "mixp", "add", "near2", "piece", "unsettle", "add", "piece", "datt",
+    "att0", "sel", "add", "att1", "dn", "mixed", "add", "piece",
+    "gc", "gx", "lp", "lf", "near4", "lp", "add", "la",
+    "lp", "la", "joinM", "lp", "la", "lp", "lp", "piece",
+    "la", "ul", "la", "add", "lp", "la", "joinG", "lp",
+    "la",
+)
 
 
 def hbm(value):
@@ -233,9 +261,9 @@
         + [pl.BlockSpec(memory_space=pl.ANY)] * len(before),
         out_specs=[cols(group * size), cols(size), cols(size), whole(8)],
         out_shape=[
-            jax.ShapeDtypeStruct(queries.shape, jnp.bfloat16),
-            jax.ShapeDtypeStruct(keys.shape, jnp.bfloat16),
-            jax.ShapeDtypeStruct(keys.shape, jnp.bfloat16),
+            pltpu.HBM(queries.shape, jnp.bfloat16),
+            pltpu.HBM(keys.shape, jnp.bfloat16),
+            pltpu.HBM(keys.shape, jnp.bfloat16),
             jax.ShapeDtypeStruct((8, size), jnp.float32),
         ],
         input_output_aliases={11 + blocks + i: i for i in range(len(before))},
@@ -244,8 +272,9 @@
         cost_estimate=COST,
         name="attend_back",
     )(
-        core, grad, hbm(queries), hbm(keys), hbm(values), hbm(q_lin), hbm(k_lin), cosine, sine,
-        q_gain[None, :], k_gain[None, :], *[hbm(p) for p in probs], *before,
+        core, hbm(grad), hbm(queries), hbm(keys), hbm(values), hbm(q_lin), hbm(k_lin), hbm(cosine),
+        hbm(sine), q_gain[None, :], k_gain[None, :], *[hbm(p) for p in probs],
+        *[hbm(array) for array in before],
     )
 
 
@@ -294,29 +323,12 @@
 ROWS = 128
 
 
-def rows_call(kernel, name, rows, ins, outs):
-    def spec(shape):
-        if shape[0] == rows:
-            return pl.BlockSpec((ROWS, shape[1]), lambda i: (i, 0))
-        return pl.BlockSpec(shape, lambda i: (0, 0))
-
-    return pl.pallas_call(
-        kernel,
-        grid=(rows // ROWS,),
-        in_specs=[spec(a.shape) for a in ins],
-        out_specs=[spec(o.shape) for o in outs],
-        out_shape=outs,
-        compiler_params=pltpu.CompilerParams(vmem_limit_bytes=24 * MIB),
-        cost_estimate=COST,
-        name=name,
-    )(*ins)
-
-
 def wide(ref):
     return ref[...].astype(jnp.float32)
 
 
-def settle_kernel(x_ref, near_ref, far_ref, gain_ref, resid_ref, *inner_refs):
+def settle_kernel(core_ref, x_ref, near_ref, far_ref, gain_ref, *refs):
+    resid_ref, inner_refs = refs[-1 - BLOCK // ROWS], refs[-(BLOCK // ROWS) :]
     resid = wide(x_ref) + (wide(near_ref) + wide(far_ref))
     resid_ref[...] = resid
     factor = lax.rsqrt(row_mean(resid * resid) + EPS)
@@ -328,24 +340,56 @@
             inner_ref[...] = inner
 
 
-def settle(x, near, far, gain):
-    rows, width = x.shape
+def settle(core, tokens, near, far, gain, part, parts, before):
+    rows, width = near.shape
     pieces = rows // ROWS
-    block = pl.BlockSpec((ROWS, width), lambda i: (i, 0))
+    block = pl.BlockSpec((ROWS, width), lambda i, core_ref: (i, 0))
     return pl.pallas_call(
         settle_kernel,
-        grid=(pieces,),
-        in_specs=[block, block, block, pl.BlockSpec((1, width), lambda i: (0, 0))],
-        out_specs=[block] + [pl.BlockSpec((ROWS, width), lambda i: (0, 0))] * pieces,
-        out_shape=[jax.ShapeDtypeStruct((rows, width), jnp.float32)]
+        grid_spec=pltpu.PrefetchScalarGridSpec(
+            num_scalar_prefetch=1,
+            grid=(pieces,),
+            in_specs=[
+                pl.BlockSpec(
+                    (ROWS, width), lambda i, core_ref: ((2 * part + core_ref[0]) * pieces + i, 0)
+                ),
+                block,
+                block,
+                pl.BlockSpec((1, width), lambda i, core_ref: (0, 0)),
+            ]
+            + [pl.BlockSpec(memory_space=pl.ANY)] * len(before),
+            out_specs=[pl.BlockSpec((ROWS, width), lambda i, core_ref: (part * pieces + i, 0))]
+            + [pl.BlockSpec((ROWS, width), lambda i, core_ref: (0, 0))] * pieces,
+        ),
+        out_shape=[pltpu.HBM((parts * rows, width), jnp.float32)]
         + [jax.ShapeDtypeStruct((ROWS, width), jnp.bfloat16)] * pieces,
+        input_output_aliases={5 + i: i for i in range(len(before))},
         compiler_params=pltpu.CompilerParams(vmem_limit_bytes=24 * MIB),
         cost_estimate=COST,
         name="settle",
-    )(x, near, far, gain[None, :])
-
-
-def unsettle_kernel(near_ref, far_ref, resid_ref, grad_ref, gain_ref, out_ref, low_ref, sum_ref):
+    )(core, hbm(tokens), near, far, gain[None, :], *[hbm(array) for array in before])
+
+
+def half_specs(parts, width):
+    steps = BLOCK // ROWS
+
+    def spec(j):
+        return pl.BlockSpec(
+            (ROWS, width), lambda i, *_: (jnp.clip(i - j * steps, 0, steps - 1), 0)
+        )
+
+    return [spec(j) for j in range(parts)]
+
+
+def put_halves(value, refs):
+    for j, ref in enumerate(refs):
+
+        @pl.when(lax.div(pl.program_id(0), BLOCK // ROWS) == j)
+        def _():
+            ref[...] = value
+
+
+def norm_grad(near_ref, far_ref, resid_ref, grad_ref, gain_ref):
     resid = resid_ref[...].astype(jnp.float32)
     factor = lax.rsqrt(row_mean(resid * resid) + EPS)
     hat = resid * factor
@@ -353,39 +397,73 @@
     both = d_inner * hat
     scaled = d_inner * gain_ref[...]
     back = wide(grad_ref) + factor * (scaled - hat * row_mean(both * gain_ref[...]))
-    out_ref[...] = back.astype(out_ref.dtype)
-    if low_ref is not None:
-        low_ref[...] = back.astype(jnp.bfloat16)
-
-        @pl.when(pl.program_id(0) == 0)
-        def _():
-            sum_ref[...] = jnp.zeros_like(sum_ref)
-
-        sum_ref[0:1, :] += jnp.sum(both, 0, keepdims=True)
-
-
-def last_kernel(near_ref, far_ref, resid_ref, grad_ref, gain_ref, out_ref):
-    unsettle_kernel(near_ref, far_ref, resid_ref, grad_ref, gain_ref, out_ref, None, None)
-
-
-def unsettle(near, far, resid, grad, gain):
+    return back, both
+
+
+def unsettle_kernel(near_ref, far_ref, resid_ref, grad_ref, gain_ref, out_ref, sum_ref, *low_refs):
+    back, both = norm_grad(near_ref, far_ref, resid_ref, grad_ref, gain_ref)
+    out_ref[...] = back
+    put_halves(back.astype(jnp.bfloat16), low_refs)
+
+    @pl.when(pl.program_id(0) == 0)
+    def _():
+        sum_ref[...] = jnp.zeros_like(sum_ref)
+
+    sum_ref[0:1, :] += jnp.sum(both, 0, keepdims=True)
+
+
+def unsettle(far, near, resid, grad, gain):
     rows, width = near.shape
-    return rows_call(
-        unsettle_kernel, "unsettle", rows, (near, far, resid, grad, gain[None, :]),
-        [
-            jax.ShapeDtypeStruct((rows, width), jnp.float32),
-            jax.ShapeDtypeStruct((rows, width), jnp.bfloat16),
+    pieces, parts = BLOCK // ROWS, rows // BLOCK
+    block = pl.BlockSpec((ROWS, width), lambda i: (i, 0))
+    own = pl.BlockSpec(
+        (ROWS, width), lambda i: (2 * pieces * lax.div(i, pieces) + lax.rem(i, pieces), 0)
+    )
+    return pl.pallas_call(
+        unsettle_kernel,
+        grid=(rows // ROWS,),
+        in_specs=[block, block, block, own, pl.BlockSpec((1, width), lambda i: (0, 0))],
+        out_specs=[block, pl.BlockSpec((8, width), lambda i: (0, 0)), *half_specs(parts, width)],
+        out_shape=[
+            pltpu.HBM((rows, width), jnp.float32),
             jax.ShapeDtypeStruct((8, width), jnp.float32),
-        ],
-    )
-
-
-def unsettle_last(near, far, resid, grad, gain):
+        ]
+        + [jax.ShapeDtypeStruct((BLOCK, width), jnp.bfloat16)] * parts,
+        compiler_params=pltpu.CompilerParams(vmem_limit_bytes=24 * MIB),
+        cost_estimate=COST,
+        name="unsettle",
+    )(near, far, hbm(resid), hbm(grad), gain[None, :])
+
+
+def last_kernel(core_ref, near_ref, far_ref, x_ref, grad_ref, gain_ref, *out_refs):
+    back, _ = norm_grad(near_ref, far_ref, x_ref, grad_ref, gain_ref)
+    put_halves(back.astype(jnp.bfloat16), out_refs)
+
+
+def unsettle_last(core, far, near, tokens, grad, gain):
     rows, width = near.shape
-    return rows_call(
-        last_kernel, "unsettle_last", rows, (near, far, resid, grad, gain[None, :]),
-        [jax.ShapeDtypeStruct((rows, width), jnp.bfloat16)],
-    )[0]
+    pieces, parts = BLOCK // ROWS, rows // BLOCK
+    block = pl.BlockSpec((ROWS, width), lambda i, core_ref: (i, 0))
+
+    def own(i, core_ref):
+        return ((2 * lax.div(i, pieces) + core_ref[0]) * pieces + lax.rem(i, pieces), 0)
+
+    return pl.pallas_call(
+        last_kernel,
+        grid_spec=pltpu.PrefetchScalarGridSpec(
+            num_scalar_prefetch=1,
+            grid=(rows // ROWS,),
+            in_specs=[
+                block, block, pl.BlockSpec((ROWS, width), own), block,
+                pl.BlockSpec((1, width), lambda i, core_ref: (0, 0)),
+            ],
+            out_specs=half_specs(parts, width),
+        ),
+        out_shape=[jax.ShapeDtypeStruct((BLOCK, width), jnp.bfloat16)] * parts,
+        compiler_params=pltpu.CompilerParams(vmem_limit_bytes=24 * MIB),
+        cost_estimate=COST,
+        name="unsettle_last",
+    )(core, near, far, hbm(tokens), hbm(grad), gain[None, :])
 
 
 def live_rows_kernel(core_ref, value_ref, seg_ref, out_ref):
@@ -410,7 +488,7 @@
         compiler_params=pltpu.CompilerParams(vmem_limit_bytes=24 * MIB),
         cost_estimate=COST,
         name="live_rows",
-    )(core, value, seg_ids[:, None])
+    )(core, hbm(value), seg_ids[:, None])
 
 
 def ring_of(n):
@@ -438,78 +516,71 @@
 
 
 def ring_last(turned, value_a, value_b, *out_refs):
-    whole = jnp.concatenate([value_a, value_b], 1)
-    begin, rows = 0, out_refs[0].shape[1 if turned[0] else 0]
+    rows = value_b.shape[0]
+    whole = jnp.concatenate([value_a[:rows], value_b], 1)
+    begin = 0
     for flag, ref in zip(turned, out_refs):
         width = ref.shape[0] if flag else ref.shape[1]
-        part = whole[:rows, begin : begin + width]
+        part = whole[:, begin : begin + width]
         ref[...] = part.T if flag else part
         begin += width
     if len(out_refs) > len(turned):
-        out_refs[-1][...] = whole[rows:, :]
-
-
-def ring_sum_call(finish, name, came, part, out_shape):
-    def kernel(came_a_ref, came_b_ref, a_ref, b_ref, *out_refs):
-        finish(wide(came_a_ref) + wide(a_ref), wide(came_b_ref) + wide(b_ref), *out_refs)
+        out_refs[-1][...] = value_a[rows:]
+
+
+EXTRA = 16
+
+
+def ring_sum_call(finish, name, step, came, part, extra, out_shape):
+    def kernel(*refs):
+        came_refs, refs = refs[: len(came)], refs[len(came) :]
+        values = [wide(refs[0]), wide(refs[1])]
+        if extra:
+            rows = refs[2][step * EXTRA : (step + 1) * EXTRA, :].astype(jnp.float32)
+            values[0] = jnp.concatenate([values[0], rows], 0)
+        if came:
+            values = [value + wide(ref) for value, ref in zip(values, came_refs)]
+        finish(*values, *refs[2 + len(extra) :])
 
     vmem = pl.BlockSpec(memory_space=pltpu.VMEM)
     return pl.pallas_call(
         kernel,
-        in_specs=[vmem] * 4,
+        in_specs=[vmem] * (len(came) + 2 + len(extra)),
         out_specs=jax.tree.map(lambda o: vmem, out_shape),
         out_shape=out_shape,
         compiler_params=pltpu.CompilerParams(vmem_limit_bytes=16 * MIB),
         cost_estimate=COST,
         name=name,
-    )(*came, *part)
-
-
-EXTRA = 16
-
-
-def ring_call(finish, name, n, where, step, came, source, out_shape):
-    sizes, half = [part.shape[0] // n for part in source], source[0].shape[1] // 2
-    outs = len(jax.tree.leaves(out_shape))
-
-    def kernel(where_ref, *refs):
-        came_refs, part_refs = refs[: len(came)], refs[len(came) :][: len(source)]
-        out_refs, owns, sem = refs[len(came) + len(source) :][:outs], refs[-3:-1], refs[-1]
+    )(*came, *part, *extra)
+
+
+def ring_call(n, where, step, part, out_shape):
+    size, half = part.shape[0] // n, part.shape[1] // 2
+
+    def kernel(where_ref, part_ref, *refs):
         copies = []
-        for side, own in enumerate(owns):
-            row = 0
-            for size, part_ref in zip(sizes, part_refs):
-                begin = pl.multiple_of(where_ref[2 * step + side] * size, size)
-                copies.append(
-                    pltpu.make_async_copy(
-                        part_ref.at[pl.ds(begin, size), pl.ds(side * half, half)],
-                        own.at[pl.ds(row, size), :],
-                        sem.at[len(copies)],
-                    )
+        for side, out_ref in enumerate(refs[:2]):
+            begin = pl.multiple_of(where_ref[2 * step + side] * size, size)
+            copies.append(
+                pltpu.make_async_copy(
+                    part_ref.at[pl.ds(begin, size), pl.ds(side * half, half)], out_ref, refs[2].at[side]
                 )
-                row += size
+            )
         for copy in copies:
             copy.start()
         for copy in copies:
             copy.wait()
-        values = [wide(own) for own in owns]
-        if came:
-            values = [value + wide(ref) for value, ref in zip(values, came_refs)]
-        finish(*values, *out_refs)
 
     return pl.pallas_call(
         kernel,
-        in_specs=[pl.BlockSpec(memory_space=pltpu.SMEM)]
-        + [pl.BlockSpec(memory_space=pltpu.VMEM)] * len(came)
-        + [pl.BlockSpec(memory_space=pltpu.HBM)] * len(source),
-        out_specs=jax.tree.map(lambda o: pl.BlockSpec(memory_space=pltpu.VMEM), out_shape),
+        in_specs=[pl.BlockSpec(memory_space=pltpu.SMEM), pl.BlockSpec(memory_space=pltpu.HBM)],
+        out_specs=[pl.BlockSpec(memory_space=pltpu.VMEM)] * 2,
         out_shape=out_shape,
-        scratch_shapes=[pltpu.VMEM((sum(sizes), half), jnp.bfloat16)] * 2
-        + [pltpu.SemaphoreType.DMA((2 * len(source),))],
+        scratch_shapes=[pltpu.SemaphoreType.DMA((2,))],
         compiler_params=pltpu.CompilerParams(vmem_limit_bytes=16 * MIB),
         cost_estimate=COST,
-        name=name,
-    )(where, *came, *[hbm(part) for part in source])
+        name="ring_piece",
+    )(where, hbm(part))
 
 
 def ring_sides(groups):
@@ -528,20 +599,18 @@
     return sides, half
 
 
-def ring_mm_call(finish, name, n, where, step, came, groups, out_shape):
+def ring_mm_call(n, where, step, groups, out_shape):
     lefts = [left for group, _ in groups for left in group]
     rights = [right for _, group in groups for right in group]
     count = sum(left.shape[0] for left in groups[0][0])
     size = lefts[0].shape[1] // n
     sides, half = ring_sides(groups)
-    outs = len(jax.tree.leaves(out_shape))
     used = [sorted({term[0] for term in side}) for side in sides]
 
     def kernel(where_ref, *refs):
-        came_refs, refs = refs[: len(came)], refs[len(came) :]
         left_refs, refs = refs[: len(lefts)], refs[len(lefts) :]
         right_refs, refs = refs[: len(rights)], refs[len(rights) :]
-        out_refs, refs = refs[:outs], refs[outs:]
+        out_refs, refs = refs[:2], refs[2:]
         right_bufs, left_bufs, sem = refs[:2], list(refs[2:-1]), refs[-1]
         waits, chunks = ([], []), ({}, {})
         for side in range(2):
@@ -569,7 +638,6 @@
                 copy.start()
                 waits[side].append(copy)
                 at += width
-        values = []
         for side in range(2):
             for copy in waits[side]:
                 copy.wait()
@@ -580,24 +648,25 @@
                     dot_tn(chunks[side][group][...], right_bufs[side][:, at : at + width])
                 )
                 at += width
-            value = jnp.concatenate(products, 1) if len(products) > 1 else products[0]
-            values.append(value + wide(came_refs[side]) if came else value)
-        finish(*values, *out_refs)
+            begin = 0
+            for product in products:
+                width = product.shape[1]
+                out_refs[side][:, begin : begin + width] = product.astype(jnp.bfloat16)
+                begin += width
 
     return pl.pallas_call(
         kernel,
         in_specs=[pl.BlockSpec(memory_space=pltpu.SMEM)]
-        + [pl.BlockSpec(memory_space=pltpu.VMEM)] * len(came)
         + [pl.BlockSpec(memory_space=pltpu.HBM)] * (len(lefts) + len(rights)),
-        out_specs=jax.tree.map(lambda o: pl.BlockSpec(memory_space=pltpu.VMEM), out_shape),
+        out_specs=[pl.BlockSpec(memory_space=pltpu.VMEM)] * 2,
         out_shape=out_shape,
         scratch_shapes=[pltpu.VMEM((count, half), jnp.bfloat16)] * 2
         + [pltpu.VMEM((count, size), jnp.bfloat16)] * (len(used[0]) + len(used[1]))
         + [pltpu.SemaphoreType.DMA((2,))],
         compiler_params=pltpu.CompilerParams(vmem_limit_bytes=32 * MIB),
         cost_estimate=COST,
-        name=name,
-    )(where, *came, *[hbm(i) for i in lefts + rights])
+        name="ring_piece",
+    )(where, *[hbm(i) for i in lefts + rights])
 
 
 class Order:
@@ -617,65 +686,69 @@
 
 
 class Ring:
-    def __init__(self, n, where, order, groups, ahead_made, turned, last_shapes):
+    def __init__(self, n, where, order, groups, turned, last_shapes):
         self.n, self.where, self.order = n, where, order
-        self.last, self.last_shapes = functools.partial(ring_last, turned), last_shapes
-        self.step_no = 0
+        self.last, self.last_shapes = functools.partial(ring_last, turned), [*last_shapes]
+        self.step_no, self.parts = -1, []
         _, _, self.ahead, self.back = ring_of(n)
-        size = groups[0][0][0].shape[1] // n
-        half = sum(right.shape[1] for _, rights in groups for right in rights) // 2
-        self.ahead_made = ahead_made and size % 128 == 0
-        if self.ahead_made:
+        self.size = groups[0][0][0].shape[1] // n
+        self.half = sum(right.shape[1] for _, rights in groups for right in rights) // 2
+        self.extra = ()
+        if self.size % 128 == 0:
             self.piece, self.source = ring_mm_call, groups
         else:
             (lefts, (first, *others)), *more = groups
             self.piece = ring_call
-            self.source = [order.run(lambda r: weight_grad([(lefts, [r, *others]), *more]), first)]
-        self.out = [jax.ShapeDtypeStruct((size, half), jnp.bfloat16)] * 2
+            self.source = order.run(lambda r: weight_grad([(lefts, [r, *others]), *more]), first)
+
+    def prepare(self):
+        step = self.step_no + 1 + len(self.parts)
+        if step < self.n:
+            shape = jax.ShapeDtypeStruct((self.size, self.half), jnp.bfloat16)
+            self.parts.append(
+                self.order.run(
+                    lambda w: self.piece(self.n, w, step, self.source, [shape] * 2), self.where
+                )
+            )
 
     def add(self, extra):
-        self.source.append(extra)
-        rows, half = self.out[0].shape
-        self.out = [jax.ShapeDtypeStruct((rows + EXTRA, half), jnp.bfloat16)] * 2
-        self.last_shapes = [*self.last_shapes, jax.ShapeDtypeStruct((EXTRA, 2 * half), jnp.float32)]
-
-    def begin(self):
-        self.send(self.make(0))
-
-    def make(self, step):
-        return self.order.run(
-            lambda w: self.piece(
-                ring_first, "ring_first", self.n, w, step, (), self.source, self.out
+        self.extra = (extra,)
+        self.last_shapes.append(jax.ShapeDtypeStruct((EXTRA, self.half), jnp.float32))
+
+    def step(self):
+        if self.step_no == self.n - 1:
+            return
+        if not self.parts:
+            self.prepare()
+        part = self.parts.pop(0)
+        self.step_no += 1
+        made = [
+            jax.ShapeDtypeStruct((self.size + (EXTRA if self.extra else 0), self.half), jnp.bfloat16),
+            jax.ShapeDtypeStruct((self.size, self.half), jnp.bfloat16),
+        ]
+        if self.step_no == 0 and not self.extra:
+            return self.send(part)
+        if self.step_no == 0:
+            finish, name, out, came = ring_first, "ring_first", made, ()
+        elif self.step_no < self.n - 1:
+            finish, name, out, came = ring_first, "ring_add", made, self.came
+        else:
+            finish, name, out, came = self.last, "ring_last", self.last_shapes, self.came
+        first, *others = [*came, *part]
+        result = self.order.run(
+            lambda a: ring_sum_call(
+                finish, name, self.step_no, [a, *others][: len(came)], [a, *others][len(came) :],
+                self.extra, out,
             ),
-            self.where,
+            first,
         )
-
-    def call(self, finish, name, out):
-        if self.ahead_made:
-            return self.order.run(
-                lambda a: ring_sum_call(finish, name, (a, self.came[1]), self.part, out), self.came[0]
-            )
-        return self.order.run(
-            lambda a: self.piece(
-                finish, name, self.n, self.where, self.step_no, (a, self.came[1]), self.source, out
-            ),
-            self.came[0],
-        )
+        if self.step_no < self.n - 1:
+            self.send(result)
+        else:
+            self.result = result
 
     def send(self, held):
         self.came = (lax.ppermute(held[0], "dp", self.ahead), lax.ppermute(held[1], "dp", self.back))
-
-    def prepare(self):
-        if self.ahead_made and self.step_no < self.n - 1:
-            self.part = self.make(self.step_no + 1)
-
-    def step(self):
-        if self.step_no < self.n - 1:
-            self.step_no += 1
-            if self.step_no < self.n - 1:
-                self.send(self.call(ring_first, "ring_add", self.out))
-            else:
-                self.result = self.call(self.last, "ring_last", self.last_shapes)
 
 
 DOTS = {"nn": dot_nn, "nt": dot_nt, "tn": dot_tn}
@@ -731,12 +804,12 @@
         + specs
         + [pl.BlockSpec(memory_space=pl.ANY)] * len(before),
         out_specs=[pl.BlockSpec((rows, cols), lambda j: (0, begin + j)) for rows, _ in shapes],
-        out_shape=[jax.ShapeDtypeStruct((rows, width), kind) for rows, kind in shapes],
+        out_shape=[pltpu.HBM((rows, width), kind) for rows, kind in shapes],
         input_output_aliases={1 + len(ins) + i: i for i in range(len(before))},
         compiler_params=pltpu.CompilerParams(vmem_limit_bytes=40 * MIB),
         cost_estimate=COST,
         name="pairs",
-    )(core, *[hbm(i) for i in ins], *before)
+    )(core, *[hbm(i) for i in ins], *[hbm(array) for array in before])
 
 
 def split_pair_kernel(core_ref, left_ref, right_ref, mine_ref, *other_refs):
@@ -799,8 +872,24 @@
     )(mine, *came)
 
 
-def mixed_kernel(resid_ref, near_ref, far_ref, out_ref):
-    out_ref[...] = (resid_ref[...] + (wide(near_ref) + wide(far_ref))).astype(jnp.bfloat16)
+def mixed_kernel(resid_ref, near_ref, far_ref, *out_refs):
+    total = resid_ref[...] + (wide(near_ref) + wide(far_ref))
+    put_halves(total.astype(jnp.bfloat16), out_refs)
+
+
+def mixed_rows(far, near, resid):
+    rows, width = near.shape
+    block = pl.BlockSpec((ROWS, width), lambda i: (i, 0))
+    return pl.pallas_call(
+        mixed_kernel,
+        grid=(rows // ROWS,),
+        in_specs=[block] * 3,
+        out_specs=half_specs(rows // BLOCK, width),
+        out_shape=[jax.ShapeDtypeStruct((BLOCK, width), jnp.bfloat16)] * (rows // BLOCK),
+        compiler_params=pltpu.CompilerParams(vmem_limit_bytes=24 * MIB),
+        cost_estimate=COST,
+        name="mixed",
+    )(hbm(resid), near, far)
 
 
 def nt_kernel(*refs):
@@ -824,7 +913,7 @@
         compiler_params=pltpu.CompilerParams(vmem_limit_bytes=40 * MIB),
         cost_estimate=COST,
         name="times_turned",
-    )(right, *lefts)
+    )(hbm(right), *lefts)
 
 
 def weight_grad_kernel(counts, *refs):
@@ -861,44 +950,30 @@
     )(*[hbm(i) for i in ins])
 
 
-def join_kernel(core_ref, mine_ref, *refs):
-    out_ref = refs[-1]
-
-    @pl.when(pl.program_id(0) % 2 == 0)
-    def _():
-        out_ref[...] = mine_ref[...]
-
-    for j, other_ref in enumerate(refs[:-1]):
-
-        @pl.when(pl.program_id(0) == 2 * j + 1)
+def join_kernel(core_ref, *refs):
+    for i, ref in enumerate(refs[:-1]):
+
+        @pl.when(pl.program_id(0) == i)
         def _():
-            out_ref[...] = other_ref[...]
+            refs[-1][...] = ref[...]
 
 
 def join(first, others, core, mine):
-    rows, width = mine.shape
-    came = [first, *others]
+    blocks = [block for pair in zip(mine, [first, *others]) for block in pair]
+    width = first.shape[1]
     return pl.pallas_call(
         join_kernel,
         grid_spec=pltpu.PrefetchScalarGridSpec(
             num_scalar_prefetch=1,
-            grid=(2 * rows // BLOCK,),
-            in_specs=[pl.BlockSpec((BLOCK, width), lambda i, core_ref: (i >> 1, 0))]
-            + [pl.BlockSpec((BLOCK, width), lambda i, core_ref: (0, 0))] * len(came),
+            grid=(len(blocks),),
+            in_specs=[pl.BlockSpec((BLOCK, width), lambda i, core_ref: (0, 0))] * len(blocks),
             out_specs=pl.BlockSpec((BLOCK, width), lambda i, core_ref: (i ^ core_ref[0], 0)),
         ),
-        out_shape=jax.ShapeDtypeStruct((2 * rows, width), mine.dtype),
+        out_shape=jax.ShapeDtypeStruct((BLOCK * len(blocks), width), first.dtype),
         compiler_params=pltpu.CompilerParams(vmem_limit_bytes=24 * MIB),
         cost_estimate=COST,
         name="join",
-    )(core, mine, *came)
-
-
-def cut_up(value, pieces, swap):
-    share = value.shape[0] // pieces
-    return [
-        lax.ppermute(value[i * share : (i + 1) * share], "tensor", swap) for i in range(pieces)
-    ]
+    )(core, *blocks)
 
 
 def to_core(value):
@@ -927,13 +1002,6 @@
     order = Order()
     run = order.run
 
-    def both_parts(piece):
-        return [piece(j) for j in range(parts)]
-
-    def own_rows(value, part, other=0):
-        begin = part * rows + (core_no ^ other) * BLOCK
-        return lax.dynamic_slice_in_dim(value, begin, BLOCK, 0)
-
     index = jnp.arange(count, dtype=jnp.int32)
     place = jnp.where(seg_ids >= 0, index - seg_ids, index).astype(jnp.float32)
     freq = THETA ** (-(jnp.arange(size // 2, dtype=jnp.float32) * 2.0) / size)
@@ -947,7 +1015,7 @@
     wide_low = (jnp.float32, jnp.bfloat16)
 
     def mine_other(mine, other):
-        return ((mine, wide_low[0]), (other, wide_low[1]))
+        return ((mine, wide_low[0]), *[((block,), wide_low[1]) for block in other])
 
     attended, probs, near, far = [], [], [], []
     for j in range(parts):
@@ -962,12 +1030,12 @@
     grad_low = run(lambda c: live_rows(core, c, seg_ids), cotangent)
     grad_low, where = lax.optimization_barrier((grad_low, where))
     d_hidden = run(lambda g: times_turned([g], w_down), grad_low)
-    x_own = both_parts(lambda j: own_rows(tokens, j))
-
-    resid, fed = [], ()
+    resid, fed = (), ()
     for j in range(parts):
-        held, *inner_own = run(lambda f: settle(x_own[j], near[j], f, mlp_gain), far[j])
-        resid.append(held)
+        held, *inner_own = run(
+            lambda f: settle(core, tokens, near[j], f, mlp_gain, j, parts, resid), far[j]
+        )
+        resid = (held,)
         inner_other = [to_core(piece) for piece in inner_own]
         fed = run(
             lambda o: feed(inner_own[0], [*inner_own[1:], o, *inner_other[1:]], w_gate, w_up, d_hidden, j, fed),
@@ -980,136 +1048,165 @@
 
     units, share = w_gate.shape[1], width // n
     q_cols, k_cols = w_query.shape[1], w_key.shape[1]
-    active, results = [], {}
-
-    def ring(groups, ahead_made, turned, *last_shapes):
-        return Ring(n, where, order, groups, ahead_made, turned, last_shapes)
-
-    def begin(name, made):
-        made.begin()
-        active.append((name, made))
-
-    def tick():
-        for item in list(active):
-            item[1].step()
-            if item[1].step_no == n - 1:
-                results[item[0]] = item[1].result
-                active.remove(item)
-
-    def prepare():
-        for item in active:
-            item[1].prepare()
-
-    mlp_ring = ring(
-        [([grad_low], [hidden]), ([inner], [d_gate, d_up])], True, (True, False, False),
-        shape(units, share), shape(share, units), shape(share, units),
+    (resid,) = resid
+    both = mine_other((0, 2), (1, 3))
+    turns = where[::2, None] == jnp.arange(n)[None, :]
+    made, came = {}, {}
+
+    def send(name):
+        values = made[name]
+        if name in TIES:
+            values = order.tie(values)
+        came[name] = [lax.ppermute(value, "tensor", SENDS[name]) for value in values]
+
+    def run_came(piece, name, *rest):
+        first, *others = came[name]
+        return run(piece, first, others, *rest)
+
+    mlp_ring = Ring(
+        n, where, order, [([grad_low], [hidden]), ([inner], [d_gate, d_up])], (True, False, False),
+        [shape(units, share), shape(share, units), shape(share, units)],
     )
-    begin("mlp", mlp_ring)
-    prepare()
-    made = ()
-    for half in range(2):
-        made = run(
+    rings = {"mlp": mlp_ring}
+
+    def ring_piece(name):
+        return lambda: rings[name].prepare()
+
+    def ring_step(name):
+        return lambda: rings[name].step()
+
+    def mlp_first():
+        mlp_ring.prepare()
+        mlp_ring.step()
+
+    def inner_first():
+        made["d_inner"] = run(
+            lambda d: pairs(core, "nt", [(d, w_gate), (d_up, w_up)], both, 0, 2, ()), d_gate
+        )
+
+    def inner_second():
+        made["d_inner"], *made["core3"] = run(
+            lambda d: pairs(core, "nt", [(d, w_gate), (d_up, w_up)], both, 1, 2, made["d_inner"]), d_gate
+        )
+
+    def inner_near():
+        made["x3"] = [run_came(near_add, "core3", made["d_inner"])]
+
+    def mixed_products():
+        made["mixed"], *made["core2"] = run(lambda h: pairs(core, "nn", [(h, w_down)], both), hidden)
+
+    def mixed_near():
+        made["x2"] = [run_came(near_add, "core2", made["mixed"])]
+
+    def mixed_sum():
+        made["coreM"] = run(mixed_rows, came["x2"][0], made["x2"][0], resid)
+
+    def mixed_join():
+        made["mixed"] = run_came(join, "coreM", core, made["coreM"])
+
+    def resid_grad():
+        made["d_resid"], made["mlp_sums"], *made["coreB"] = run(
+            unsettle, came["x3"][0], made["x3"][0], resid, grad_low, mlp_gain
+        )
+
+    def attended_order():
+        blocks = [part[i : i + BLOCK] for part in attended for i in range(0, rows, BLOCK)]
+
+        def swap(first):
+            turned = [blocks[i ^ 1] for i in range(len(blocks))]
+            return jnp.where(
+                core_no == 0, jnp.concatenate([first, *blocks[1:]], 0), jnp.concatenate(turned, 0)
+            )
+
+        made["attended"] = run(swap, blocks[0])
+
+    def attended_grad():
+        made["d_branch"] = [b for pair in zip(made["coreB"], came["coreB"]) for b in pair]
+        made["d_attended"] = run(
+            lambda d: times_turned([*made["d_branch"][:-1], d], w_out), made["d_branch"][-1]
+        )
+        made["d_lin"], made["head_sums"] = (), 0.0
+
+    def heads_grad(g):
+        def piece():
+            *made["d_lin"], total = run(
+                lambda a: attend_back(
+                    core, a, queries, keys, values, q_lin, k_lin, cosine, sine, query_gain, key_gain,
+                    probs, g, made["d_lin"],
+                ),
+                made["d_attended"],
+            )
+            made["head_sums"] = made["head_sums"] + total
+
+        return piece
+
+    def normed_grad():
+        d_q_lin, d_k_lin, d_values = made["d_lin"]
+        rings["lin"] = Ring(
+            n, where, order, [(made["d_branch"], [made["attended"]]), ([normed], made["d_lin"])],
+            (True, False, False, False),
+            [shape(q_cols, share), shape(share, q_cols), shape(share, k_cols), shape(share, k_cols)],
+        )
+        made["d_normed"], *made["core4"], attn_sums = run(
             lambda d: pairs(
-                core, "nt", [(d, w_gate), (d_up, w_up)], mine_other((0, 2), (1, 3)), half, 2, made
+                core, "nt", [(d, w_query), (d_k_lin, w_key), (d_values, w_value)],
+                mine_other((-1, -3), (-2, -4)), weights=normed,
             ),
-            d_gate,
+            d_q_lin,
         )
-    tick()
-    came3 = cut_up(order.tie(made[1]), parts, CORE_SWAP)
-    near3 = run(near_add, came3[0], came3[1:], made[0])
-    far3 = to_chip(near3)
-    prepare()
-    mixed_mine, mixed_other = run(
-        lambda h: pairs(core, "nn", [(h, w_down)], mine_other((0, 2), (1, 3))), hidden
-    )
-    blocks = [part[i : i + BLOCK] for part in attended for i in range(0, rows, BLOCK)]
-    attended_mine_first = jnp.where(
-        core_no == 0,
-        jnp.concatenate(blocks, 0),
-        jnp.concatenate([blocks[i ^ 1] for i in range(len(blocks))], 0),
-    )
-    grad_own = jnp.concatenate([grad_low[j * rows : j * rows + BLOCK] for j in range(parts)], 0)
-    resid_own = jnp.concatenate(resid, 0)
-    tick()
-    prepare()
-    tick()
-    d_resid, branch_own, mlp_sums = run(
-        lambda f: unsettle(near3, f, resid_own, grad_own, mlp_gain), far3
-    )
-    branch_other = cut_up(branch_own, parts, CORE_SWAP)
-    prepare()
-    d_branch = []
-    for j in range(parts):
-        d_branch += [branch_own[j * BLOCK : (j + 1) * BLOCK], branch_other[j]]
-    d_attended = run(lambda d: times_turned([*d_branch[:-1], d], w_out), d_branch[-1])
-    heads_count = k_cols // size
-    d_lin, gain_sums = (), jnp.zeros((8, size), jnp.float32)
-    for g in range(heads_count):
-        *d_lin, total = run(
-            lambda a: attend_back(
-                core, a, queries, keys, values, q_lin, k_lin, cosine, sine, query_gain, key_gain,
-                probs, g, d_lin,
-            ),
-            d_attended,
+        head_sums = made["head_sums"]
+        gains = [0.5 * made["mlp_sums"][0], attn_sums[0] / attn_gain, head_sums[0], head_sums[1]]
+        made["gains1"] = [jnp.concatenate([part.reshape(n, -1) for part in gains], 1)]
+
+    def gains_core():
+        made["gains2"] = [run_came(lambda f, o: f + made["gains1"][0], "gains1")]
+
+    def gains_chip():
+        def in_turn(came, others):
+            total = jnp.sum(jnp.where(turns[:, :, None], (came + made["gains2"][0])[None], 0.0), 1)
+            spare = EXTRA * rings["lin"].half - total.shape[1]
+            return jnp.pad(low(total), ((0, 0), (0, spare))).reshape(n * EXTRA, -1)
+
+        rings["lin"].add(run_came(in_turn, "gains2"))
+
+    def normed_near():
+        made["x4"] = [run_came(near_add, "core4", made["d_normed"])]
+
+    def tokens_grad():
+        made["coreG"] = run(
+            lambda f: unsettle_last(core, f, made["x4"][0], tokens, made["d_resid"], attn_gain),
+            came["x4"][0],
         )
-        gain_sums = gain_sums + total
-        if g == 0:
-            tick()
-            came2 = cut_up(order.tie(mixed_other), parts, CORE_SWAP)
-            prepare()
-    near2 = run(near_add, came2[0], came2[1:], mixed_mine)
-    far2 = to_chip(near2)
-    d_q_lin, d_k_lin, d_values = d_lin
-    mine, other, attn_sums = run(
-        lambda d: pairs(
-            core, "nt", [(d, w_query), (d_k_lin, w_key), (d_values, w_value)],
-            mine_other((-1, -3), (-2, -4)), weights=normed,
-        ),
-        d_q_lin,
-    )
-    gains = [0.5 * mlp_sums[0], attn_sums[0] / attn_gain, gain_sums[0], gain_sums[1]]
-    gains = jnp.concatenate([part.reshape(n, -1) for part in gains], 1)
-    tick()
-    came4 = cut_up(order.tie(other), parts, CORE_SWAP)
-    near4 = run(near_add, came4[0], came4[1:], mine)
-    far4 = to_chip(near4)
-    prepare()
-    gains = run(jnp.add, to_core(gains), gains)
-    out_value = ring(
-        [(d_branch, [attended_mine_first]), ([normed], [d_values])], False, (True, False),
-        shape(q_cols, share), shape(share, k_cols),
-    )
-    gains = run(jnp.add, to_chip(gains), gains)
-    extra_cols = q_cols + k_cols
-    extra = jnp.pad(low(gains), ((0, 0), (0, EXTRA * extra_cols - gains.shape[1])))
-    out_value.add(extra.reshape(n * EXTRA, extra_cols))
-    tick()
-    mixed = run(lambda f, n_, r: rows_call(
-        mixed_kernel, "mixed", n_.shape[0], (r, n_, f), [jax.ShapeDtypeStruct(n_.shape, jnp.bfloat16)]
-    )[0], far2, near2, resid_own)
-    mixed_far = cut_up(mixed, parts, CORE_SWAP)
-    prepare()
-    query_key = ring(
-        [([normed], [d_q_lin, d_k_lin])], False, (False, False),
-        shape(share, q_cols), shape(share, k_cols),
-    )
-    mixed = run(join, mixed_far[0], mixed_far[1:], core, mixed)
-    tick()
-    begin("out value", out_value)
-    begin("query key", query_key)
-    tick()
-    tick()
-    tick()
-    grad_tokens = run(
-        lambda f: unsettle_last(near4, f, jnp.concatenate(x_own, 0), d_resid, attn_gain), far4
-    )
-    other = cut_up(grad_tokens, parts, CORE_SWAP)
-    tick()
-    grad_tokens = run(join, other[0], other[1:], core, grad_tokens)
-    while active:
-        tick()
-    grad_down, grad_gate, grad_up = results["mlp"]
-    (grad_out, grad_value, extra), (grad_query, grad_key) = results["out value"], results["query key"]
+
+    def tokens_join():
+        made["tokens"] = run_came(join, "coreG", core, made["coreG"])
+
+    pieces = {
+        "piece0": mlp_first, "piece": ring_piece("mlp"), "add": ring_step("mlp"),
+        "dih0": inner_first, "dih1": inner_second, "near3": inner_near,
+        "sel": attended_order, "mixp": mixed_products, "near2": mixed_near, "mixed": mixed_sum, "joinM": mixed_join,
+        "unsettle": resid_grad, "datt": attended_grad, "att0": heads_grad(0), "att1": heads_grad(1),
+        "dn": normed_grad, "gc": gains_core, "gx": gains_chip, "near4": normed_near,
+        "ul": tokens_grad, "joinG": tokens_join,
+        "lp": ring_piece("lin"), "lf": ring_step("lin"), "la": ring_step("lin"),
+    }
+    producers = {
+        "core3": "dih1", "x3": "near3", "core2": "mixp", "x2": "near2", "coreM": "mixed",
+        "coreB": "unsettle", "gains1": "dn", "gains2": "gc", "core4": "dn", "x4": "near4", "coreG": "ul",
+    }
+    counts = {}
+    for step in SCHEDULE:
+        pieces[step]()
+        counts[step] = counts.get(step, 0) + 1
+        for name, producer in producers.items():
+            if TIES.get(name, (producer, 1)) == (step, counts[step]):
+                send(name)
+    for ring in rings.values():
+        while ring.step_no < n - 1:
+            ring.step()
+    mixed, grad_tokens = made["mixed"], made["tokens"]
+    grad_down, grad_gate, grad_up = mlp_ring.result
+    grad_out, grad_query, grad_key, grad_value, extra = rings["lin"].result
     gains, begins = extra.reshape(-1), np.cumsum([0, width, width, size, size]) // n
     mlp_sum, attn_sum, q_sum, k_sum = [gains[begins[i] : begins[i + 1]] for i in range(4)]
     return (

time: 428 us -> 387 us (0.904)
  local copies, waits for them, and re-layouts: 35.7 us -> 8.27 us
  starting transfers between devices: 58 us -> 42.5 us
    pallas_call x30 -> x20, Pallas kernels: 75.4 us -> 36.4 us  [the longest x15 12.8 us: ring_sum_call(): pl.pallas_call(kernel, in_specs=[vmem] * (len(came) + 2 + len(extra)), ou...]
    pallas_call x8 -> x16, Pallas kernels: 52.6 us -> 82 us  [ring_mm_call(): pl.pallas_call(kernel, in_specs=[pl.BlockSpec(memory_space=pltpu.SMEM)] +...]
    unnamed x109 -> x60, local copies, waits for them, and re-layouts: 22.8 us -> 2.82 us
    ppermute x12 -> x17, waiting for transfers between devices: 1.65 us -> 12.5 us  [send(): lax.ppermute(value, 'tensor', SENDS[name])]
    ppermute x21 -> x14, starting transfers between devices: 30.9 us -> 22.9 us  [send(): lax.ppermute(held[0], 'dp', self.ahead)]
    ppermute x21 -> x14, starting transfers between devices: 13.4 us -> 7.13 us  [send(): lax.ppermute(held[1], 'dp', self.back)]
    pallas_call x2, Pallas kernels: 11.4 us -> 16.7 us  [times_turned(): pl.pallas_call(nt_kernel, grid=(right.shape[0] // cols,), in_specs=[pl.Bl...]
    ppermute x6 -> x2, starting transfers between devices: 8.17 us -> 2.93 us  [to_chip(): return lax.ppermute(value, 'tensor', CHIP_SWAP)]
  transfers between devices with their start and end apart: 69 -> 55, of which waited for: 29 -> 31; matrix products, arithmetic and copies ran while one was open for 3% -> 2% of each run, Pallas kernels for 51% -> 57%
where the time goes in v4:
time: 387 us; the launch traced here: 384 us
  Pallas kernels  263 us (68%)
  waiting for transfers between devices  63.9 us (17%)
  starting transfers between devices  42.5 us (11%)
  local copies, waits for them, and re-layouts  8.27 us (2%)
  other arithmetic  4.63 us (1%)
    pallas_call x16, Pallas kernels, ring_mm_call(): pl.pallas_call(kernel, in_specs=[pl.BlockSpec(memory_space=pltpu.SMEM)] +...  82 us
    pallas_call x4, Pallas kernels, pairs(): pl.pallas_call(functools.partial(pairs_kernel, kind, outs, len(terms), in...  42.4 us
    ppermute x14, waiting for transfers between devices, send(): lax.ppermute(held[0], 'dp', self.ahead)  32.3 us
    pallas_call x2, Pallas kernels, feed(): pl.pallas_call(functools.partial(feed_kernel, len(lefts)), grid=(units //...  24.6 us
    ppermute x14, starting transfers between devices, send(): lax.ppermute(held[0], 'dp', self.ahead)  22.9 us
    pallas_call x2, Pallas kernels, attend_back(): pl.pallas_call(functools.partial(attend_back_kernel, blocks), grid=(1,),...  20.3 us
    pallas_call x2, Pallas kernels, times_turned(): pl.pallas_call(nt_kernel, grid=(right.shape[0] // cols,), in_specs=[pl.Bl...  16.7 us
    pallas_call x15, Pallas kernels, ring_sum_call(): pl.pallas_call(kernel, in_specs=[vmem] * (len(came) + 2 + len(extra)), ou...  12.8 us
  transfers between devices with their start and end apart: 55, of which 31 were waited for; matrix products, arithmetic and copies ran while one was open for 2% of the time, Pallas kernels for 57%

profile of v4, /device:TPU:0, one launch (start us, length us, event | category | flops | bytes accessed | tf_op | source)
XLA Modules:
  0.0 383.6 jit_solution(10114809776442108344)
XLA Ops:
  3.7 10.9 %front.1 = (bf16[1024,2048]{1,0:T(8,128)(2,1)}, bf16[1024,512]{1,0:T(8,128)(2,1)}, bf16[1024,256]{1,0:T(8,128)(2,1)}, bf16[1024,256]{1,0:T(8,128)(2,1)}, f32[1024,512]{1,0:T(8,128)}, /*index=5*/f32[1024,256]{1,0:T(8,128)}) custom-call(bf16[1024,2048]{1,0:T(8,128)(2,1)} %x_ref.7, f32[1,2048]{1,0:T(1,128)S(1)} %bitcast.13, bf16[2048,512]{1,0:T(8,128)(2,1)} %refs_1_.7, ...), custom_call_target="tpu_custom_call" | custom-call | tf_op jit(solution)/shard_map/front/pallas_call | solution.py:111
  28.7 6.4 %attend.3 = (bf16[512,512]{1,0:T(8,128)(2,1)S(1)}, bf16[2,512,768]{2,1,0:T(8,128)(2,1)}, bf16[2,512,1024]{2,1,0:T(8,128)(2,1)}) custom-call(bf16[1024,512]{1,0:T(8,128)(2,1)} %get-tuple-element.219.q_ref.refs_2_, bf16[1024,256]{1,0:T(8,128)(2,1)} %get-tuple-element.211.k_ref.refs_3_, bf16[1024,256]{1,0:T(8,128)(2,1)} %get-tuple-element.212.v_ref.refs_4_, ...), custom_call_target="tpu_custom_call" | custom-call | tf_op jit(solution)/shard_map/attend/pallas_call | solution.py:172
  44.4 11.2 %times_turned.2.refs_6_ = bf16[1024,1536]{1,0:T(8,128)(2,1)} custom-call(bf16[1536,2048]{1,0:T(8,128)(2,1)} %refs_1_.6, bf16[1024,2048]{1,0:T(8,128)(2,1)S(1)} %live_rows.1.refs_1_.refs_0_.grad_ref), custom_call_target="tpu_custom_call" | custom-call | tf_op jit(solution)/shard_map/times_turned/pallas_call | solution.py:906
  61.7 12.4 %feed.2 = (bf16[1024,2048]{1,0:T(8,128)(2,1)}, bf16[1024,1536]{1,0:T(8,128)(2,1)}, bf16[1024,1536]{1,0:T(8,128)(2,1)}, bf16[1024,1536]{1,0:T(8,128)(2,1)}) custom-call(bf16[128,2048]{1,0:T(8,128)(2,1)S(1)} %get-tuple-element.230.refs_0_, bf16[128,2048]{1,0:T(8,128)(2,1)S(1)} %get-tuple-element.231.refs_1_, ...), custom_call_target="tpu_custom_call" | custom-call | tf_op jit(solution)/shard_map/feed/pallas_call | solution.py:308
  80.9 12.2 %feed.3 = (bf16[1024,2048]{1,0:T(8,128)(2,1)}, bf16[1024,1536]{1,0:T(8,128)(2,1)}, bf16[1024,1536]{1,0:T(8,128)(2,1)}, bf16[1024,1536]{1,0:T(8,128)(2,1)}) custom-call(bf16[128,2048]{1,0:T(8,128)(2,1)S(1)} %get-tuple-element.237.refs_0_, ...), custom_call_target="tpu_custom_call", output_to_operand_aliasing={{0}: (7, {}), {1}: (8, {}), {2}: (9, {}), {3}: (10, {})} | custom-call | tf_op jit(solution)/shard_map/feed/pallas_call | solution.py:308
  93.1 6.4 %ring_piece.16 = (bf16[256,2304]{1,0:T(8,128)(2,1)S(1)}, bf16[256,2304]{1,0:T(8,128)(2,1)S(1)}) custom-call(s32[16]{0:T(128)S(1)} %dynamic-slice_bitcast_fusion.where_ref, bf16[1024,2048]{1,0:T(8,128)(2,1)} %copy-done, bf16[1024,2048]{1,0:T(8,128)(2,1)} %get-tuple-element.246.refs_1_, bf16[1024,1536]{1,0:T(8,128)(2,1)} %get-tuple-element.269.refs_2_.refs_0_, ...), custom_call_target="tpu_custom_call" | custom-call | tf_op jit(solution)/shard_map/ring_piece/pallas_call | solution.py:657
  101.5 11.5 %pairs.4 = (f32[512,2048]{1,0:T(8,128)}, bf16[256,2048]{1,0:T(8,128)(2,1)}, bf16[256,2048]{1,0:T(8,128)(2,1)}) custom-call(s32[1]{0:T(128)} %bitcast.core_ref.refs_0_, bf16[1024,1536]{1,0:T(8,128)(2,1)} %get-tuple-element.252.refs_3_.refs_0_, bf16[2048,1536]{1,0:T(8,128)(2,1)} %refs_1_.5, bf16[1024,1536]{1,0:T(8,128)(2,1)} %get-tuple-element.248.refs_4_.refs_2_, ...), custom_call_target="tpu_custom_call" | custom-call | tf_op jit(solution)/shard_map/pairs/pallas_call | solution.py:800
  113.0 11.4 %pairs.5 = (f32[512,2048]{1,0:T(8,128)}, bf16[256,2048]{1,0:T(8,128)(2,1)}, bf16[256,2048]{1,0:T(8,128)(2,1)}) custom-call(s32[1]{0:T(128)} %bitcast.core_ref.refs_0_, bf16[1024,1536]{1,0:T(8,128)(2,1)} %get-tuple-element.252.refs_3_.refs_0_, bf16[2048,1536]{1,0:T(8,128)(2,1)} %refs_1_.5, ...), custom_call_target="tpu_custom_call", output_to_operand_aliasing={{0}: (5, {}), {1}: (6, {}), {2}: (7, {})} | custom-call | tf_op jit(solution)/shard_map/pairs/pallas_call | solution.py:800
  124.9 6.4 %ring_piece.17 = (bf16[256,2304]{1,0:T(8,128)(2,1)S(1)}, bf16[256,2304]{1,0:T(8,128)(2,1)S(1)}) custom-call(s32[16]{0:T(128)S(1)} %dynamic-slice_bitcast_fusion.where_ref, bf16[1024,2048]{1,0:T(8,128)(2,1)} %copy-done, bf16[1024,2048]{1,0:T(8,128)(2,1)} %get-tuple-element.246.refs_1_, bf16[1024,1536]{1,0:T(8,128)(2,1)} %get-tuple-element.269.refs_2_.refs_0_, ...), custom_call_target="tpu_custom_call" | custom-call | tf_op jit(solution)/shard_map/ring_piece/pallas_call | solution.py:657
  136.6 6.4 %ring_piece.18 = (bf16[256,2304]{1,0:T(8,128)(2,1)S(1)}, bf16[256,2304]{1,0:T(8,128)(2,1)S(1)}) custom-call(s32[16]{0:T(128)S(1)} %dynamic-slice_bitcast_fusion.where_ref, bf16[1024,2048]{1,0:T(8,128)(2,1)} %copy-done, bf16[1024,2048]{1,0:T(8,128)(2,1)} %get-tuple-element.246.refs_1_, bf16[1024,1536]{1,0:T(8,128)(2,1)} %get-tuple-element.269.refs_2_.refs_0_, ...), custom_call_target="tpu_custom_call" | custom-call | tf_op jit(solution)/shard_map/ring_piece/pallas_call | solution.py:657
  142.9 6.4 %ring_piece.19 = (bf16[256,2304]{1,0:T(8,128)(2,1)S(1)}, bf16[256,2304]{1,0:T(8,128)(2,1)S(1)}) custom-call(s32[16]{0:T(128)S(1)} %dynamic-slice_bitcast_fusion.where_ref, bf16[1024,2048]{1,0:T(8,128)(2,1)} %copy-done, bf16[1024,2048]{1,0:T(8,128)(2,1)} %get-tuple-element.246.refs_1_, bf16[1024,1536]{1,0:T(8,128)(2,1)} %get-tuple-element.269.refs_2_.refs_0_, ...), custom_call_target="tpu_custom_call" | custom-call | tf_op jit(solution)/shard_map/ring_piece/pallas_call | solution.py:657
  149.3 10.4 %pairs.6 = (f32[512,2048]{1,0:T(8,128)}, bf16[256,2048]{1,0:T(8,128)(2,1)}, bf16[256,2048]{1,0:T(8,128)(2,1)}) custom-call(s32[1]{0:T(128)} %bitcast.core_ref.refs_0_, bf16[1024,1536]{1,0:T(8,128)(2,1)} %get-tuple-element.269.refs_2_.refs_0_, bf16[1536,2048]{1,0:T(8,128)(2,1)} %refs_1_.6), custom_call_target="tpu_custom_call" | custom-call | tf_op jit(solution)/shard_map/pairs/pallas_call | solution.py:800
  169.9 6.4 %ring_piece.20 = (bf16[256,2304]{1,0:T(8,128)(2,1)S(1)}, bf16[256,2304]{1,0:T(8,128)(2,1)S(1)}) custom-call(s32[16]{0:T(128)S(1)} %dynamic-slice_bitcast_fusion.where_ref, bf16[1024,2048]{1,0:T(8,128)(2,1)} %copy-done, bf16[1024,2048]{1,0:T(8,128)(2,1)} %get-tuple-element.246.refs_1_, bf16[1024,1536]{1,0:T(8,128)(2,1)} %get-tuple-element.269.refs_2_.refs_0_, ...), custom_call_target="tpu_custom_call" | custom-call | tf_op jit(solution)/shard_map/ring_piece/pallas_call | solution.py:657
  176.4 5.6 %collective-permute-done.19.far_ref = bf16[512,2048]{1,0:T(8,128)(2,1)S(1)} collective-permute-done((bf16[512,2048]{1,0:T(8,128)(2,1)S(1)}, bf16[512,2048]{1,0:T(8,128)(2,1)S(1)}, u32[]{:S(2)}, u32[]{:S(2)}) %collective-permute-start.19) | collective-permute-done | bytes 2097184 | tf_op jit(solution)/shard_map/ppermute | solution.py:1060
  182.0 6.9 %unsettle.1 = (f32[512,2048]{1,0:T(8,128)}, f32[8,2048]{1,0:T(8,128)S(1)}, bf16[256,2048]{1,0:T(8,128)(2,1)S(1)}, bf16[256,2048]{1,0:T(8,128)(2,1)S(1)}) custom-call(bf16[512,2048]{1,0:T(8,128)(2,1)S(1)} %near_add.7.near_ref, bf16[512,2048]{1,0:T(8,128)(2,1)S(1)} %collective-permute-done.19.far_ref, f32[512,2048]{1,0:T(8,128)} %get-tuple-element.236.resid_ref, ...), custom_call_target="tpu_custom_call" | custom-call | tf_op jit(solution)/shard_map/unsettle/pallas_call | solution.py:422
  197.9 6.4 %ring_piece.21 = (bf16[256,2304]{1,0:T(8,128)(2,1)S(1)}, bf16[256,2304]{1,0:T(8,128)(2,1)S(1)}) custom-call(s32[16]{0:T(128)S(1)} %dynamic-slice_bitcast_fusion.where_ref, bf16[1024,2048]{1,0:T(8,128)(2,1)} %copy-done, bf16[1024,2048]{1,0:T(8,128)(2,1)} %get-tuple-element.246.refs_1_, bf16[1024,1536]{1,0:T(8,128)(2,1)} %get-tuple-element.269.refs_2_.refs_0_, ...), custom_call_target="tpu_custom_call" | custom-call | tf_op jit(solution)/shard_map/ring_piece/pallas_call | solution.py:657
  204.3 5.5 %times_turned.3.refs_1_ = bf16[1024,512]{1,0:T(8,128)(2,1)} custom-call(bf16[512,2048]{1,0:T(8,128)(2,1)} %refs_0_.3, bf16[256,2048]{1,0:T(8,128)(2,1)S(1)} %get-tuple-element.283.refs_1_.refs_0_, bf16[256,2048]{1,0:T(8,128)(2,1)} %collective-permute-done.20.refs_2_.refs_1_, bf16[256,2048]{1,0:T(8,128)(2,1)S(1)} %get-tuple-element.284.refs_3_.refs_2_, ...), custom_call_target="tpu_custom_call" | custom-call | tf_op jit(solution)/shard_map/times_turned/pallas_call | solution.py:906
  209.8 10.2 %attend_back.2 = (bf16[1024,512]{1,0:T(8,128)(2,1)}, bf16[1024,256]{1,0:T(8,128)(2,1)}, bf16[1024,256]{1,0:T(8,128)(2,1)}, f32[8,128]{1,0:T(8,128)S(1)}) custom-call(s32[1]{0:T(128)} %bitcast.core_ref.refs_0_, bf16[1024,512]{1,0:T(8,128)(2,1)} %times_turned.3.refs_1_, bf16[1024,512]{1,0:T(8,128)(2,1)} %get-tuple-element.219.q_ref.refs_2_, ...), custom_call_target="tpu_custom_call" | custom-call | tf_op jit(solution)/shard_map/attend_back/pallas_call | solution.py:252
  226.6 10.1 %attend_back.3 = (bf16[1024,512]{1,0:T(8,128)(2,1)}, bf16[1024,256]{1,0:T(8,128)(2,1)}, bf16[1024,256]{1,0:T(8,128)(2,1)}, f32[8,128]{1,0:T(8,128)S(1)}) custom-call(s32[1]{0:T(128)} %bitcast.core_ref.refs_0_, bf16[1024,512]{1,0:T(8,128)(2,1)} %times_turned.3.refs_1_, ...), custom_call_target="tpu_custom_call", output_to_operand_aliasing={{0}: (15, {}), {1}: (16, {}), {2}: (17, {})} | custom-call | tf_op jit(solution)/shard_map/attend_back/pallas_call | solution.py:252
  236.8 9.1 %pairs.7 = (f32[512,2048]{1,0:T(8,128)}, bf16[256,2048]{1,0:T(8,128)(2,1)}, bf16[256,2048]{1,0:T(8,128)(2,1)}, f32[8,2048]{1,0:T(8,128)}) custom-call(s32[1]{0:T(128)} %bitcast.core_ref.refs_0_, bf16[1024,512]{1,0:T(8,128)(2,1)} %get-tuple-element.310.refs_0_.refs_6_, bf16[2048,512]{1,0:T(8,128)(2,1)} %refs_1_.7, ...), custom_call_target="tpu_custom_call" | custom-call | tf_op jit(solution)/shard_map/pairs/pallas_call | solution.py:800
  258.3 6.4 %ring_piece.22 = (bf16[256,2304]{1,0:T(8,128)(2,1)S(1)}, bf16[256,2304]{1,0:T(8,128)(2,1)S(1)}) custom-call(s32[16]{0:T(128)S(1)} %dynamic-slice_bitcast_fusion.where_ref, bf16[1024,2048]{1,0:T(8,128)(2,1)} %copy-done, bf16[1024,2048]{1,0:T(8,128)(2,1)} %get-tuple-element.246.refs_1_, bf16[1024,1536]{1,0:T(8,128)(2,1)} %get-tuple-element.269.refs_2_.refs_0_, ...), custom_call_target="tpu_custom_call" | custom-call | tf_op jit(solution)/shard_map/ring_piece/pallas_call | solution.py:657
  285.5 7.7 %collective-permute-done.31.refs_0_ = bf16[272,768]{1,0:T(8,128)(2,1)S(1)} collective-permute-done((bf16[272,768]{1,0:T(8,128)(2,1)S(1)}, bf16[272,768]{1,0:T(8,128)(2,1)S(1)}, u32[]{:S(2)}, u32[]{:S(2)}) %collective-permute-start.31) | collective-permute-done | bytes 417824 | tf_op jit(solution)/shard_map/ppermute | solution.py:751
  327.9 6.4 %ring_piece.29 = (bf16[256,2304]{1,0:T(8,128)(2,1)S(1)}, bf16[256,2304]{1,0:T(8,128)(2,1)S(1)}) custom-call(s32[16]{0:T(128)S(1)} %dynamic-slice_bitcast_fusion.where_ref, bf16[1024,2048]{1,0:T(8,128)(2,1)} %copy-done, bf16[1024,2048]{1,0:T(8,128)(2,1)} %get-tuple-element.246.refs_1_, bf16[1024,1536]{1,0:T(8,128)(2,1)} %get-tuple-element.269.refs_2_.refs_0_, ...), custom_call_target="tpu_custom_call" | custom-call | tf_op jit(solution)/shard_map/ring_piece/pallas_call | solution.py:657
  334.3 14.0 %collective-permute-done.43.refs_0_ = bf16[272,768]{1,0:T(8,128)(2,1)S(1)} collective-permute-done((bf16[272,768]{1,0:T(8,128)(2,1)S(1)}, bf16[272,768]{1,0:T(8,128)(2,1)S(1)}, u32[]{:S(2)}, u32[]{:S(2)}) %collective-permute-start.43) | collective-permute-done | bytes 417824 | tf_op jit(solution)/shard_map/ppermute | solution.py:751
  (234 shorter events, 175.4 us)
Async XLA Ops:
  25.8 29.8 %collective-permute-start.5 = (bf16[256,2048]{1,0:T(8,128)(2,1)}, bf16[256,2048]{1,0:T(8,128)(2,1)}, u32[]{:S(2)}, u32[]{:S(2)}) collective-permute-start(bf16[256,2048]{1,0:T(8,128)(2,1)} %near_add.5.near_ref), channel_id=1, source_target_pairs={{0,2},{1,3},{2,0},{3,1},{4,6},{5,7},{6,4},{7,5},{8,10},{9,11},{10,... | collective-permute-start | bytes 3145736 | tf_op jit(solution)/shard_map/ppermute | solution.py:984
  40.3 34.6 %collective-permute-start.4 = (bf16[256,2048]{1,0:T(8,128)(2,1)S(1)}, bf16[256,2048]{1,0:T(8,128)(2,1)S(1)}, u32[]{:S(2)}, u32[]{:S(2)}) collective-permute-start(bf16[256,2048]{1,0:T(8,128)(2,1)S(1)} %near_add.6.near_ref), channel_id=1, source_target_pairs={{0,2},{1,3},{2,0},{3,1},{4,6},{5,7},{6,4},{7,5},{8,10},{9,11},{10,... | collective-permute-start | bytes 3145736 | tf_op jit(solution)/shard_map/ppermute | solution.py:984
  99.4 31.9 %collective-permute-start.11 = (bf16[256,2304]{1,0:T(8,128)(2,1)S(1)}, bf16[256,2304]{1,0:T(8,128)(2,1)S(1)}, u32[]{:S(2)}, u32[]{:S(2)}) collective-permute-start(bf16[256,2304]{1,0:T(8,128)(2,1)S(1)} %get-tuple-element.249), channel_id=1, source_target_pairs={{0,8},{8,16},{16,24},{24,28},{28,20},{20,12},{12,4},{4,0},{1,9},{9... | collective-permute-start | bytes 3538952 | tf_op jit(solution)/shard_map/ppermute | solution.py:751
  101.3 30.0 %collective-permute-start.12 = (bf16[256,2304]{1,0:T(8,128)(2,1)S(1)}, bf16[256,2304]{1,0:T(8,128)(2,1)S(1)}, u32[]{:S(2)}, u32[]{:S(2)}) collective-permute-start(bf16[256,2304]{1,0:T(8,128)(2,1)S(1)} %get-tuple-element.260), channel_id=1, source_target_pairs={{8,0},{16,8},{24,16},{28,24},{20,28},{12,20},{4,12},{0,4},{9,1},{1... | collective-permute-start | bytes 3538952 | tf_op jit(solution)/shard_map/ppermute | solution.py:751
  131.9 28.0 %collective-permute-start.14 = (bf16[256,2304]{1,0:T(8,128)(2,1)S(1)}, bf16[256,2304]{1,0:T(8,128)(2,1)S(1)}, u32[]{:S(2)}, u32[]{:S(2)}) collective-permute-start(bf16[256,2304]{1,0:T(8,128)(2,1)S(1)} %get-tuple-element.262), channel_id=1, source_target_pairs={{0,8},{8,16},{16,24},{24,28},{28,20},{20,12},{12,4},{4,0},{1,9},{9... | collective-permute-start | bytes 3538952 | tf_op jit(solution)/shard_map/ppermute | solution.py:751
  133.8 27.7 %collective-permute-start.15 = (bf16[256,2304]{1,0:T(8,128)(2,1)S(1)}, bf16[256,2304]{1,0:T(8,128)(2,1)S(1)}, u32[]{:S(2)}, u32[]{:S(2)}) collective-permute-start(bf16[256,2304]{1,0:T(8,128)(2,1)S(1)} %get-tuple-element.274), channel_id=1, source_target_pairs={{8,0},{16,8},{24,16},{28,24},{20,28},{12,20},{4,12},{0,4},{9,1},{1... | collective-permute-start | bytes 3538952 | tf_op jit(solution)/shard_map/ppermute | solution.py:751
  134.8 47.2 %collective-permute-start.19 = (bf16[512,2048]{1,0:T(8,128)(2,1)S(1)}, bf16[512,2048]{1,0:T(8,128)(2,1)S(1)}, u32[]{:S(2)}, u32[]{:S(2)}) collective-permute-start(bf16[512,2048]{1,0:T(8,128)(2,1)S(1)} %near_add.7.near_ref), channel_id=1, source_target_pairs={{0,2},{1,3},{2,0},{3,1},{4,6},{5,7},{6,4},{7,5},{8,10},{9,11},{10,... | collective-permute-start | bytes 6291464 | tf_op jit(solution)/shard_map/ppermute | solution.py:1060
  162.0 27.4 %collective-permute-start.22 = (bf16[256,2304]{1,0:T(8,128)(2,1)S(1)}, bf16[256,2304]{1,0:T(8,128)(2,1)S(1)}, u32[]{:S(2)}, u32[]{:S(2)}) collective-permute-start(bf16[256,2304]{1,0:T(8,128)(2,1)S(1)} %get-tuple-element.276), channel_id=1, source_target_pairs={{0,8},{8,16},{16,24},{24,28},{28,20},{20,12},{12,4},{4,0},{1,9},{9... | collective-permute-start | bytes 3538952 | tf_op jit(solution)/shard_map/ppermute | solution.py:751
  163.7 26.5 %collective-permute-start.23 = (bf16[256,2304]{1,0:T(8,128)(2,1)S(1)}, bf16[256,2304]{1,0:T(8,128)(2,1)S(1)}, u32[]{:S(2)}, u32[]{:S(2)}) collective-permute-start(bf16[256,2304]{1,0:T(8,128)(2,1)S(1)} %get-tuple-element.287), channel_id=1, source_target_pairs={{8,0},{16,8},{24,16},{28,24},{20,28},{12,20},{4,12},{0,4},{9,1},{1... | collective-permute-start | bytes 3538952 | tf_op jit(solution)/shard_map/ppermute | solution.py:751
  192.0 29.3 %collective-permute-start.24 = (bf16[256,2304]{1,0:T(8,128)(2,1)}, bf16[256,2304]{1,0:T(8,128)(2,1)}, u32[]{:S(2)}, u32[]{:S(2)}) collective-permute-start(bf16[256,2304]{1,0:T(8,128)(2,1)} %get-tuple-element.289), channel_id=1, source_target_pairs={{0,8},{8,16},{16,24},{24,28},{28,20},{20,12},{12,4},{4,0},{1,9},{9... | collective-permute-start | bytes 3538952 | tf_op jit(solution)/shard_map/ppermute | solution.py:751
  193.6 27.7 %collective-permute-start.25 = (bf16[256,2304]{1,0:T(8,128)(2,1)}, bf16[256,2304]{1,0:T(8,128)(2,1)}, u32[]{:S(2)}, u32[]{:S(2)}) collective-permute-start(bf16[256,2304]{1,0:T(8,128)(2,1)} %get-tuple-element.303), channel_id=1, source_target_pairs={{8,0},{16,8},{24,16},{28,24},{20,28},{12,20},{4,12},{0,4},{9,1},{1... | collective-permute-start | bytes 3538952 | tf_op jit(solution)/shard_map/ppermute | solution.py:751
  194.2 51.6 %collective-permute-start.18 = (bf16[512,2048]{1,0:T(8,128)(2,1)}, bf16[512,2048]{1,0:T(8,128)(2,1)}, u32[]{:S(2)}, u32[]{:S(2)}) collective-permute-start(bf16[512,2048]{1,0:T(8,128)(2,1)} %near_add.8.near_ref), channel_id=1, source_target_pairs={{0,2},{1,3},{2,0},{3,1},{4,6},{5,7},{6,4},{7,5},{8,10},{9,11},{10,... | collective-permute-start | bytes 6291464 | tf_op jit(solution)/shard_map/ppermute | solution.py:1060
  224.2 26.6 %collective-permute-start.27 = (bf16[256,2304]{1,0:T(8,128)(2,1)S(1)}, bf16[256,2304]{1,0:T(8,128)(2,1)S(1)}, u32[]{:S(2)}, u32[]{:S(2)}) collective-permute-start(bf16[256,2304]{1,0:T(8,128)(2,1)S(1)} %get-tuple-element.305), channel_id=1, source_target_pairs={{0,8},{8,16},{16,24},{24,28},{28,20},{20,12},{12,4},{4,0},{1,9},{9... | collective-permute-start | bytes 3538952 | tf_op jit(solution)/shard_map/ppermute | solution.py:751
  225.8 26.6 %collective-permute-start.28 = (bf16[256,2304]{1,0:T(8,128)(2,1)S(1)}, bf16[256,2304]{1,0:T(8,128)(2,1)S(1)}, u32[]{:S(2)}, u32[]{:S(2)}) collective-permute-start(bf16[256,2304]{1,0:T(8,128)(2,1)S(1)} %get-tuple-element.322), channel_id=1, source_target_pairs={{8,0},{16,8},{24,16},{28,24},{20,28},{12,20},{4,12},{0,4},{9,1},{1... | collective-permute-start | bytes 3538952 | tf_op jit(solution)/shard_map/ppermute | solution.py:751
  254.4 26.7 %collective-permute-start.32 = (bf16[256,2304]{1,0:T(8,128)(2,1)}, bf16[256,2304]{1,0:T(8,128)(2,1)S(1)}, u32[]{:S(2)}, u32[]{:S(2)}) collective-permute-start(bf16[256,2304]{1,0:T(8,128)(2,1)} %get-tuple-element.324), channel_id=1, source_target_pairs={{0,8},{8,16},{16,24},{24,28},{28,20},{20,12},{12,4},{4,0},{1,9},{9... | collective-permute-start | bytes 3538952 | tf_op jit(solution)/shard_map/ppermute | solution.py:751
  255.9 25.8 %collective-permute-start.35 = (bf16[256,2304]{1,0:T(8,128)(2,1)}, bf16[256,2304]{1,0:T(8,128)(2,1)S(1)}, u32[]{:S(2)}, u32[]{:S(2)}) collective-permute-start(bf16[256,2304]{1,0:T(8,128)(2,1)} %get-tuple-element.341), channel_id=1, source_target_pairs={{8,0},{16,8},{24,16},{28,24},{20,28},{12,20},{4,12},{0,4},{9,1},{1... | collective-permute-start | bytes 3538952 | tf_op jit(solution)/shard_map/ppermute | solution.py:751
  256.5 18.5 %collective-permute-start.34 = (bf16[256,2048]{1,0:T(8,128)(2,1)}, bf16[256,2048]{1,0:T(8,128)(2,1)}, u32[]{:S(2)}, u32[]{:S(2)}) collective-permute-start(bf16[256,2048]{1,0:T(8,128)(2,1)} %get-tuple-element.337), channel_id=1, source_target_pairs={{0,1},{1,0},{2,3},{3,2},{4,5},{5,4},{6,7},{7,6},{8,9},{9,8},{10,11... | collective-permute-start | bytes 3145736 | tf_op jit(solution)/shard_map/ppermute | solution.py:1060
  282.2 68.4 %collective-permute-start.40 = (bf16[512,2048]{1,0:T(8,128)(2,1)S(1)}, bf16[512,2048]{1,0:T(8,128)(2,1)S(1)}, u32[]{:S(2)}, u32[]{:S(2)}) collective-permute-start(bf16[512,2048]{1,0:T(8,128)(2,1)S(1)} %near_add.9.near_ref), channel_id=1, source_target_pairs={{0,2},{1,3},{2,0},{3,1},{4,6},{5,7},{6,4},{7,5},{8,10},{9,11},{10,... | collective-permute-start | bytes 6291464 | tf_op jit(solution)/shard_map/ppermute | solution.py:1060
  285.0 21.7 %collective-permute-start.30 = (bf16[256,2048]{1,0:T(8,128)(2,1)S(1)}, bf16[256,2048]{1,0:T(8,128)(2,1)S(1)}, u32[]{:S(2)}, u32[]{:S(2)}) collective-permute-start(bf16[256,2048]{1,0:T(8,128)(2,1)S(1)} %copy-done.22), channel_id=1, source_target_pairs={{0,1},{1,0},{2,3},{3,2},{4,5},{5,4},{6,7},{7,6},{8,9},{9,8},{10,11... | collective-permute-start | bytes 3145736 | tf_op jit(solution)/shard_map/ppermute | solution.py:1060
  285.0 23.4 %collective-permute-start.39 = (bf16[256,2048]{1,0:T(8,128)(2,1)S(1)}, bf16[256,2048]{1,0:T(8,128)(2,1)S(1)}, u32[]{:S(2)}, u32[]{:S(2)}) collective-permute-start(bf16[256,2048]{1,0:T(8,128)(2,1)S(1)} %copy-done.24), channel_id=1, source_target_pairs={{0,1},{1,0},{2,3},{3,2},{4,5},{5,4},{6,7},{7,6},{8,9},{9,8},{10,11... | collective-permute-start | bytes 3145736 | tf_op jit(solution)/shard_map/ppermute | solution.py:1060
  306.7 52.9 %collective-permute-start.49 = (bf16[256,2304]{1,0:T(8,128)(2,1)S(1)}, bf16[256,2304]{1,0:T(8,128)(2,1)S(1)}, u32[]{:S(2)}, u32[]{:S(2)}) collective-permute-start(bf16[256,2304]{1,0:T(8,128)(2,1)S(1)} %get-tuple-element.343), channel_id=1, source_target_pairs={{0,8},{8,16},{16,24},{24,28},{28,20},{20,12},{12,4},{4,0},{1,9},{9... | collective-permute-start | bytes 3538952 | tf_op jit(solution)/shard_map/ppermute | solution.py:751
  317.5 30.8 %collective-permute-start.43 = (bf16[272,768]{1,0:T(8,128)(2,1)S(1)}, bf16[272,768]{1,0:T(8,128)(2,1)S(1)}, u32[]{:S(2)}, u32[]{:S(2)}) collective-permute-start(bf16[272,768]{1,0:T(8,128)(2,1)S(1)} %get-tuple-element.362), channel_id=1, source_target_pairs={{0,8},{8,16},{16,24},{24,28},{28,20},{20,12},{12,4},{4,0},{1,9},{9... | collective-permute-start | bytes 1253384 | tf_op jit(solution)/shard_map/ppermute | solution.py:751
  319.3 29.0 %collective-permute-start.44 = (bf16[256,768]{1,0:T(8,128)(2,1)S(1)}, bf16[256,768]{1,0:T(8,128)(2,1)S(1)}, u32[]{:S(2)}, u32[]{:S(2)}) collective-permute-start(bf16[256,768]{1,0:T(8,128)(2,1)S(1)} %get-tuple-element.370), channel_id=1, source_target_pairs={{8,0},{16,8},{24,16},{28,24},{20,28},{12,20},{4,12},{0,4},{9,1},{1... | collective-permute-start | bytes 1179656 | tf_op jit(solution)/shard_map/ppermute | solution.py:751
  319.6 40.9 %collective-permute-start.50 = (bf16[256,2304]{1,0:T(8,128)(2,1)S(1)}, bf16[256,2304]{1,0:T(8,128)(2,1)S(1)}, u32[]{:S(2)}, u32[]{:S(2)}) collective-permute-start(bf16[256,2304]{1,0:T(8,128)(2,1)S(1)} %get-tuple-element.380), channel_id=1, source_target_pairs={{8,0},{16,8},{24,16},{28,24},{20,28},{12,20},{4,12},{0,4},{9,1},{1... | collective-permute-start | bytes 3538952 | tf_op jit(solution)/shard_map/ppermute | solution.py:751
  (61 other events, 448.7 us)
